TPU v7x, 32 devices: a whole 2x2x4 slice. The times are simulated.
32 devices in a mesh: wide: 8 (over z, x), narrow: 4 (over y, core).
Axes of the slice: x: 2, y: 2, z: 4, core: 2. Of those that a mesh axis runs over, the one named last changes fastest.
Arguments:
- patches: bfloat16 [4096, 128, 384], P(('wide', 'narrow')), may hold values from -6 to 6
- visible: int32 [4096, 64], P(('wide', 'narrow')), may hold values from 0 to 127, as said below
- counts: int32 [4096], P(('wide', 'narrow')), may hold values from 13 to 64, as said below
- upstream: bfloat16 [4096, 64, 384], P(('wide', 'narrow')), may hold values from -6 to 6
- w_qkv: bfloat16 [384, 1152], replicated, may hold values from -0.3125 to 0.3125
- b_query: float32 [384], replicated, may hold values from -1.5 to 1.5
- b_value: float32 [384], replicated, may hold values from -1.5 to 1.5
- w_out: bfloat16 [384, 384], replicated, may hold values from -0.875 to 0.875
- b_out: float32 [384], replicated, may hold values from -1.5 to 1.5
- w_up: bfloat16 [384, 1536], replicated, may hold values from -0.3125 to 0.3125
- b_up: float32 [1536], replicated, may hold values from -1.5 to 1.5
- w_down: bfloat16 [1536, 384], replicated, may hold values from -0.15625 to 0.15625
- b_down: float32 [384], replicated, may hold values from -1.5 to 1.5
- gain_attn: float32 [384], replicated, may hold values from 0.25 to 1.75
- shift_attn: float32 [384], replicated, may hold values from -1.5 to 1.5
- gain_mlp: float32 [384], replicated, may hold values from 0.25 to 1.75
- shift_mlp: float32 [384], replicated, may hold values from -1.5 to 1.5
Outputs:
- encoded: bfloat16 [4096, 64, 384], P(('wide', 'narrow'))
- input_grad: bfloat16 [4096, 128, 384], P(('wide', 'narrow'))
- grad_w_qkv: float32 [384, 1152], replicated
- grad_b_query: float32 [384], replicated
- grad_b_value: float32 [384], replicated
- grad_w_out: float32 [384, 384], replicated
- grad_b_out: float32 [384], replicated
- grad_w_up: float32 [384, 1536], replicated
- grad_b_up: float32 [1536], replicated
- grad_w_down: float32 [1536, 384], replicated
- grad_b_down: float32 [384], replicated
- grad_gain_attn: float32 [384], replicated
- grad_shift_attn: float32 [384], replicated
- grad_gain_mlp: float32 [384], replicated
- grad_shift_mlp: float32 [384], replicated
Inputs may be any that keep to these rules, and one draw needn't show every extreme that they name: Devices are numbered in the order of the blocks of 128 fields. For every field number l within a block, the counts of field l over all devices sum to exactly (77) times half the number of devices. Each row lists distinct patch numbers; the first counts[f] entries of row f are the visible patches of field f.
All inputs are finite; a program needn't handle non-finite values.
Results may differ from a plain program's by a relative error of at most 0.012.
The roundings to bfloat16 on the way count: a program that leaves them out, or rounds other values in their place, can miss the bound.
Values may be sent and summed in bfloat16 or wider, within the bound.
A program may use at most 384 MiB of HBM per device.

v0:
```python
import jax
import jax.numpy as jnp
from jax import lax
from jax.sharding import PartitionSpec as P

HD = 64
OWN_ROWS = 4928


NORM_EPSILON = 1e-06
MASK_FILL = -1e30


def layer_norm(values, gain, shift):
    row_mean = jnp.mean(values, axis=-1, keepdims=True)
    centered = values - row_mean
    variance = jnp.mean(centered * centered, axis=-1, keepdims=True)
    return centered * lax.rsqrt(variance + NORM_EPSILON) * gain + shift


def gelu_exact(values):
    return jax.nn.gelu(values, approximate=False)


def round_up(value, step):
    return (value + step - 1) // step * step


def pack_layout(field_counts, row_count, total_rows):
    field_total = field_counts.shape[0]
    ends = jnp.cumsum(field_counts)
    starts = ends - field_counts
    row_iota = lax.broadcasted_iota(jnp.int32, (total_rows, 1), 0)
    owner_field = jnp.sum((row_iota >= ends[None, :]).astype(jnp.int32), axis=1)
    alive = owner_field < field_total
    field_iota = lax.broadcasted_iota(jnp.int32, (1, field_total), 1)
    start_of = jnp.sum(jnp.where(owner_field[:, None] == field_iota, starts[None, :], 0), axis=1)
    source = jnp.where(
        alive, jnp.minimum(owner_field, field_total - 1) * row_count + row_iota[:, 0] - start_of, 0
    )
    seg_ids = jnp.where(alive, owner_field, -1)
    return (seg_ids, source, alive, starts)


def pack_rows(field_rows, source, alive):
    flat_rows = field_rows.reshape(-1, field_rows.shape[-1])
    return jnp.where(alive[:, None], flat_rows[source], jnp.zeros((), field_rows.dtype))


def unpack_rows(packed_rows, field_counts, starts, row_count):
    slot_iota = lax.broadcasted_iota(jnp.int32, (1, row_count), 1)
    live_slot = slot_iota < field_counts[:, None]
    index = jnp.where(live_slot, starts[:, None] + slot_iota, 0)
    return jnp.where(live_slot[..., None], packed_rows[index], jnp.zeros((), packed_rows.dtype))


def per_device(
    patches,
    visible,
    counts,
    upstream,
    w_qkv,
    b_query,
    b_value,
    w_out,
    b_out,
    w_up,
    b_up,
    w_down,
    b_down,
    gain_attn,
    shift_attn,
    gain_mlp,
    shift_mlp,
):
    fields, patch_rows, model_width = patches.shape
    row_count = visible.shape[1]
    head_count = model_width // HD
    score_scale = HD ** (-0.5)
    f32 = jnp.float32
    bf16 = jnp.bfloat16
    gathered = jax.vmap(lambda grid_rows, picks: grid_rows[picks])(patches, visible)
    counts_bf = counts.astype(bf16)
    own_rows, own_grad, own_counts_bf = (
        lax.all_to_all(gathered, ("wide", "narrow"), split_axis=0, concat_axis=0, tiled=True),
        lax.all_to_all(upstream, ("wide", "narrow"), split_axis=0, concat_axis=0, tiled=True),
        lax.all_to_all(counts_bf, ("wide", "narrow"), split_axis=0, concat_axis=0, tiled=True),
    )
    own_counts = own_counts_bf.astype(jnp.int32)
    block = min(512, round_up(OWN_ROWS, 8))
    total_rows = round_up(OWN_ROWS, block)
    seg_ids, source, alive, starts = pack_layout(own_counts, row_count, total_rows)
    both_rows = pack_rows(jnp.concatenate([own_rows, own_grad], axis=-1), source, alive)
    x_rows = both_rows[:, :model_width]
    cot_rows = both_rows[:, model_width:]
    row_mask = (seg_ids >= 0).astype(f32)[:, None]
    inputs_f = x_rows.astype(f32)
    normed, norm_back = jax.vjp(layer_norm, inputs_f, gain_attn, shift_attn)
    normed_b = normed.astype(bf16)
    qkv_bias = jnp.concatenate([b_query, jnp.zeros_like(b_query), b_value])
    packed = jnp.dot(normed_b, w_qkv, preferred_element_type=f32) + qkv_bias
    packed_b = packed.astype(bf16)
    query_b = packed_b[:, :model_width].reshape(total_rows, head_count, HD)
    key_b = packed_b[:, model_width : 2 * model_width].reshape(total_rows, head_count, HD)
    value_b = packed_b[:, 2 * model_width :].reshape(total_rows, head_count, HD)
    key_pad = jnp.pad(key_b, ((row_count, row_count), (0, 0), (0, 0)))
    value_pad = jnp.pad(value_b, ((row_count, row_count), (0, 0), (0, 0)))
    seg_pad = jnp.pad(seg_ids, (row_count, row_count), constant_values=-1)
    window = block + 2 * row_count
    block_count = total_rows // block

    def block_scores(start):
        query_blk = lax.dynamic_slice_in_dim(query_b, start, block, 0)
        key_blk = lax.dynamic_slice_in_dim(key_pad, start, window, 0)
        seg_query = lax.dynamic_slice_in_dim(seg_ids, start, block, 0)
        seg_key = lax.dynamic_slice_in_dim(seg_pad, start, window, 0)
        raw = (
            jnp.einsum("qhe,khe->hqk", query_blk, key_blk, preferred_element_type=f32) * score_scale
        )
        allowed = (seg_query[:, None] == seg_key[None, :]) & (seg_key[None, :] >= 0)
        return jnp.where(allowed[None], raw, MASK_FILL)

    def forward_block(index):
        start = index * block
        scores = block_scores(start)
        top = jnp.max(scores, axis=-1, keepdims=True)
        expo = jnp.exp(scores - top)
        total = jnp.sum(expo, axis=-1, keepdims=True)
        probs_b = (expo / total).astype(bf16)
        value_blk = lax.dynamic_slice_in_dim(value_pad, start, window, 0)
        out = jnp.einsum("hqk,khe->qhe", probs_b, value_blk, preferred_element_type=f32)
        return (out.astype(bf16), top[..., 0], total[..., 0])

    mixed_parts, row_max, row_total = lax.map(forward_block, jnp.arange(block_count))
    mixed_b = mixed_parts.reshape(total_rows, model_width)
    residual = inputs_f + jnp.dot(mixed_b, w_out, preferred_element_type=f32) + b_out
    normed2, norm2_back = jax.vjp(layer_norm, residual, gain_mlp, shift_mlp)
    normed2_b = normed2.astype(bf16)
    up_proj = jnp.dot(normed2_b, w_up, preferred_element_type=f32) + b_up
    act_f, gelu_back = jax.vjp(gelu_exact, up_proj)
    act_b = act_f.astype(bf16)
    down_out = jnp.dot(act_b, w_down, preferred_element_type=f32) + b_down
    encoded_rows = ((residual + down_out) * row_mask).astype(bf16)
    grad_top = cot_rows.astype(f32) * row_mask
    grad_top_b = grad_top.astype(bf16)
    grad_w_down = jnp.einsum("rf,rd->fd", act_b, grad_top_b, preferred_element_type=f32)
    grad_b_down = jnp.sum(grad_top_b.astype(f32), axis=0)
    d_act = jnp.einsum("rd,fd->rf", grad_top_b, w_down, preferred_element_type=f32)
    (d_up,) = gelu_back(d_act)
    d_up_b = d_up.astype(bf16)
    grad_w_up = jnp.einsum("rd,rf->df", normed2_b, d_up_b, preferred_element_type=f32)
    grad_b_up = jnp.sum(d_up_b.astype(f32), axis=0)
    d_normed2 = jnp.einsum("rf,df->rd", d_up_b, w_up, preferred_element_type=f32)
    d_resid_norm, grad_gain_mlp, grad_shift_mlp = norm2_back(d_normed2)
    d_residual = grad_top + d_resid_norm
    d_att_b = d_residual.astype(bf16)
    grad_w_out = jnp.einsum("rd,re->de", mixed_b, d_att_b, preferred_element_type=f32)
    grad_b_out = jnp.sum(d_att_b.astype(f32), axis=0)
    d_mixed = jnp.einsum("re,de->rd", d_att_b, w_out, preferred_element_type=f32)
    d_mixed_b = d_mixed.astype(bf16).reshape(total_rows, head_count, HD)

    def backward_block(index):
        start = index * block
        scores = block_scores(start)
        probs = jnp.exp(scores - row_max[index][..., None]) / row_total[index][..., None]
        probs_b = probs.astype(bf16)
        query_blk = lax.dynamic_slice_in_dim(query_b, start, block, 0)
        key_blk = lax.dynamic_slice_in_dim(key_pad, start, window, 0)
        value_blk = lax.dynamic_slice_in_dim(value_pad, start, window, 0)
        grad_blk = lax.dynamic_slice_in_dim(d_mixed_b, start, block, 0)
        d_probs = jnp.einsum("qhe,khe->hqk", grad_blk, value_blk, preferred_element_type=f32)
        d_value_part = jnp.einsum("hqk,qhe->khe", probs_b, grad_blk, preferred_element_type=f32)
        d_scores = probs * (d_probs - jnp.sum(probs * d_probs, axis=-1, keepdims=True))
        d_scores_b = d_scores.astype(bf16)
        d_query_part = (
            jnp.einsum("hqk,khe->qhe", d_scores_b, key_blk, preferred_element_type=f32)
            * score_scale
        )
        d_key_part = (
            jnp.einsum("hqk,qhe->khe", d_scores_b, query_blk, preferred_element_type=f32)
            * score_scale
        )
        return (d_query_part, d_key_part, d_value_part)

    d_query_parts, d_key_parts, d_value_parts = lax.map(backward_block, jnp.arange(block_count))

    def fold_windows(parts):
        center = parts[:, row_count : row_count + block]
        leading = parts[:, :row_count]
        trailing = parts[:, row_count + block :]
        edge_zero = jnp.zeros((1,) + trailing.shape[1:], f32)
        from_prev = jnp.concatenate([edge_zero, trailing[:-1]], axis=0)
        from_next = jnp.concatenate([leading[1:], edge_zero], axis=0)
        pad_tail = ((0, 0), (0, block - row_count), (0, 0), (0, 0))
        pad_head = ((0, 0), (block - row_count, 0), (0, 0), (0, 0))
        center = center + jnp.pad(from_prev, pad_tail) + jnp.pad(from_next, pad_head)
        return center.reshape(total_rows, model_width)

    d_query = d_query_parts.reshape(total_rows, model_width)
    d_key = fold_windows(d_key_parts)
    d_value = fold_windows(d_value_parts)
    d_packed_b = jnp.concatenate([d_query, d_key, d_value], axis=1).astype(bf16)
    grad_w_qkv = jnp.einsum("rd,rk->dk", normed_b, d_packed_b, preferred_element_type=f32)
    packed_sums = jnp.sum(d_packed_b.astype(f32), axis=0)
    grad_b_query = packed_sums[:model_width]
    grad_b_value = packed_sums[2 * model_width :]
    d_normed = jnp.einsum("rk,dk->rd", d_packed_b, w_qkv, preferred_element_type=f32)
    d_inputs_norm, grad_gain_attn, grad_shift_attn = norm_back(d_normed)
    d_inputs = (d_residual + d_inputs_norm).astype(bf16)
    (
        sum_w_qkv,
        sum_b_query,
        sum_b_value,
        sum_w_out,
        sum_b_out,
        sum_w_up,
        sum_b_up,
        sum_w_down,
        sum_b_down,
        sum_gain_attn,
        sum_shift_attn,
        sum_gain_mlp,
        sum_shift_mlp,
    ) = lax.psum(
        (
            grad_w_qkv,
            grad_b_query,
            grad_b_value,
            grad_w_out,
            grad_b_out,
            grad_w_up,
            grad_b_up,
            grad_w_down,
            grad_b_down,
            grad_gain_attn,
            grad_shift_attn,
            grad_gain_mlp,
            grad_shift_mlp,
        ),
        ("wide", "narrow"),
    )
    out_both = unpack_rows(
        jnp.concatenate([encoded_rows, d_inputs], axis=1), own_counts, starts, row_count
    )
    out_encoded = out_both[..., :model_width]
    out_grads = out_both[..., model_width:]
    home_encoded, home_grads = (
        lax.all_to_all(out_encoded, ("wide", "narrow"), split_axis=0, concat_axis=0, tiled=True),
        lax.all_to_all(out_grads, ("wide", "narrow"), split_axis=0, concat_axis=0, tiled=True),
    )
    input_grad = jax.vmap(lambda grid_rows, picks, new_rows: grid_rows.at[picks].set(new_rows))(
        jnp.zeros_like(patches), visible, home_grads
    )
    return (
        home_encoded,
        input_grad,
        sum_w_qkv,
        sum_b_query,
        sum_b_value,
        sum_w_out,
        sum_b_out,
        sum_w_up,
        sum_b_up,
        sum_w_down,
        sum_b_down,
        sum_gain_attn,
        sum_shift_attn,
        sum_gain_mlp,
        sum_shift_mlp,
    )


def solution(mesh):
    return jax.shard_map(
        per_device,
        mesh=mesh,
        in_specs=(
            P(("wide", "narrow"), None, None),
            P(("wide", "narrow"), None),
            P(("wide", "narrow")),
            P(("wide", "narrow"), None, None),
            P(),
            P(),
            P(),
            P(),
            P(),
            P(),
            P(),
            P(),
            P(),
            P(),
            P(),
            P(),
            P(),
        ),
        out_specs=(
            P(("wide", "narrow"), None, None),
            P(("wide", "narrow"), None, None),
            P(),
            P(),
            P(),
            P(),
            P(),
            P(),
            P(),
            P(),
            P(),
            P(),
            P(),
            P(),
            P(),
        ),
        check_vma=False,
    )
```

profile of v0, /device:TPU:0, one launch (start us, length us, event | category | flops | bytes accessed | tf_op | source)
XLA Modules:
  0.0 1700.8 jit_solution(3979082835933341654)
XLA Ops:
  16.9 145.1 %gather_fusion.2 = bf16[8192,384]{1,0:T(8,128)(2,1)} fusion(bf16[128,128,384]{2,1,0:T(8,128)(2,1)} %param.21, s32[8192]{0:T(1024)S(1)} %reshape.446), kind=kCustom, calls=%fused_computation.2 | custom fusion | bytes 12648448 | tf_op jit(solution)/shard_map/vmap()/gather | solution.py:82
  162.0 144.5 %all_to_all.30 = bf16[128,64,384]{2,1,0:T(8,128)(2,1)} all-to-all(bf16[128,64,384]{2,1,0:T(8,128)(2,1)} %bitcast.129), channel_id=1, replica_groups=mesh['wide'=8,'narrow'=4] {'wide','narrow'}, dimensions={0} | all-to-all | bytes 12582912 | tf_op jit(solution)/shard_map/all_to_all | solution.py:85
  317.3 133.2 %all-to-all-done.2 = bf16[128,64,384]{2,1,0:T(8,128)(2,1)} async-done(((bf16[128,64,384]{2,1,0:T(8,128)(2,1)}), bf16[128,64,384]{2,1,0:T(8,128)(2,1)}, u32[]{:S(2)}, u32[]{:S(2)}) %all-to-all-start.2) | async-done | bytes 6291488 | tf_op jit(solution)/shard_map/all_to_all | solution.py:86
  450.5 10.6 pad_maximum_fusion
  461.1 29.9 %gather_fusion = bf16[5120,768]{1,0:T(8,128)(2,1)} fusion(bf16[8192,768]{1,0:T(8,128)(2,1)} %bitcast.117, s32[5120]{0:T(1024)S(1)} %broadcast_clamp_fusion.1), kind=kCustom, calls=%fused_computation | custom fusion | bytes 15749120 | tf_op jit(solution)/shard_map/gather | solution.py:47
  491.0 10.6 copy.64
  508.6 9.6 add_convert_fusion.1
  533.0 114.9 %while.28 = (s32[]{:T(128)}, bf16[10,512,6,64]{1,3,2,0:T(8,128)(2,1)}, f32[10,6,512]{2,1,0:T(8,128)}, f32[10,6,512]{2,1,0:T(8,128)}, s32[10]{0:T(128)S(1)}, /*in...) while((s32[]{:T(128)}, ...), condition=%wide.region_8.9_spmd, body=%wide.region_5.8_spmd.sunk | while | flops 527755904 | bytes 26808308 | solution.py:134
  663.8 83.5 %multiply_convert_fusion.1 = (bf16[5120,1536]{1,0:T(8,128)(2,1)}, f32[5120,1536]{1,0:T(8,128)}, f32[5120,1536]{1,0:T(8,128)}) fusion(f32[1536]{0:T(1024)S(1)} %copy-done.56, bf16[384,1536]{1,0:T(8,128)(2,1)S(1)} %copy-done, bf16[5120,384]{0,1:T(8,128)(2,1)S(1)} %add_convert_fusion.5.clone.4), kind=kOutput, calls=%fused_computation.59 | convolution fusion | flops 6558842880 | bytes 83761152 | tf_op jit(solution)/shard_map/dot_general | solution.py:139
  747.4 33.7 %convert_reduce_fusion = (f32[1536]{0:T(1024)}, bf16[5120,1536]{1,0:T(8,128)(2,1)}) fusion(f32[5120,1536]{1,0:T(8,128)} %get-tuple-element.217, bf16[1536,384]{1,0:T(8,128)(2,1)S(1)} %copy-done.52, f32[5120]{0:T(1024)S(1)} %copy-done.24, bf16[5120,768]{0,1:T(8,128)(2,1)} %copy-done.3, f32[5120,1536]{1,0:T(8,128)} %get-tuple-element.245, f32[1536]{0:T(1024)S(1)} %copy-done.56), kind=kOutput, calls=%fused_computation.57 | convolution fusion | flops 6179387904 | bytes 83787776 | tf_op jit(solution)/shard_map/rd,fd->rf/dot_general | solution.py:148
  781.1 14.7 fusion.85
  826.6 267.0 %while.29 = (s32[]{:T(128)}, bf16[10,512,6,64]{1,3,2,0:T(8,128)(2,1)}, f32[10,640,6,64]{1,3,2,0:T(8,128)}, f32[10,640,6,64]{1,3,2,0:T(8,128)}, s32[10]{0:T(128)S...) while((s32[]{:T(128)}, ...), condition=%wide.region_15.16_spmd, body=%wide.region_13.15_spmd.sunk | while | flops 1279047296 | bytes 97010272 | solution.py:185
  1098.9 10.6 fusion.57
  1142.9 11.6 fusion.75
  1167.6 12.7 multiply_convert_fusion.2
  1187.4 10.6 copy.71
  1198.0 41.3 %gather_fusion.1 = bf16[8192,768]{1,0:T(8,128)(2,1)} fusion(bf16[5120,768]{1,0:T(8,128)(2,1)} %copy.71, s32[8192]{0:T(1024)S(1)} %copy-done.21), kind=kCustom, calls=%fused_computation.1 | custom fusion | bytes 25198592 | tf_op jit(solution)/shard_map/gather | solution.py:54
  1250.8 144.1 %all_to_all.31 = bf16[128,64,384]{2,1,0:T(8,128)(2,1)} all-to-all(bf16[128,64,384]{2,1,0:T(8,128)(2,1)S(1)} %get-tuple-element.228), channel_id=1, replica_groups=mesh['wide'=8,'narrow'=4] {'wide','narrow'}, dimensions={0} | all-to-all | bytes 12582912 | tf_op jit(solution)/shard_map/all_to_all | solution.py:249
  1405.3 14.5 fusion.63
  1419.8 11.3 fusion.70
  1431.2 13.8 fusion.73
  1451.5 150.1 %all-reduce.11 = (f32[384]{0:T(512)}, f32[384]{0:T(512)}, f32[384]{0:T(512)}, f32[1536]{0:T(1024)}, f32[384]{0:T(512)}, /*index=5*/f32[384]{0:T(512)}, f32[384]{0:T(512)}, f32[384]{0:T(512)}, f32[384]{0:T(512)}) all-reduce(f32[384]{0:T(512)S(1)} %get-tuple-element.242, ...), channel_id=1, replica_groups=mesh['wide'=8,'narrow'=4] {'wide','narrow'}, use_global_device_ids=true, to_apply=%region_21.22 | all-reduce | flops 4608 | bytes 36864 | tf_op jit(solution)/shard_map/psum | solution.py:224
  1601.5 43.0 %scatter_custom_fusion = bf16[16384,384]{1,0:T(8,128)(2,1)} fusion(s32[8192]{0:T(1024)S(1)} %reshape.452, bf16[8192,384]{1,0:T(8,128)(2,1)} %bitcast.142, bf16[]{:T(256)} %constant.87.clone.1), kind=kCustom, calls=%fused_computation.114 | custom fusion | bytes 12583424
  1644.5 37.9 %all-reduce.15.cloned.1.call-done = (f32[384,1152]{1,0:T(8,128)}, f32[384,384]{1,0:T(8,128)}, f32[384,1536]{1,0:T(8,128)}, f32[1536,384]{1,0:T(8,128)}) async-done(((f32[384,1152]{1,0:T(8,128)}, f32[384,384]{1,0:T(8,128)}, f32[384,1536]{1,0:T(8,128)}, f32[1536,384]{1,0:T(8,128)}), (f32[384,1152]{1,0:T(8,128)}, f32[384,384]{1,0:T(8,128)}, f32[384,1536]{1,0:T(8,128)}, ...) | async-done | bytes 7077904 | tf_op jit(solution)/shard_map/psum | solution.py:224
  (451 shorter events, 535.0 us)
Async XLA Ops:
  7.2 656.6 %copy-start = (bf16[384,1536]{1,0:T(8,128)(2,1)S(1)}, bf16[384,1536]{1,0:T(8,128)(2,1)}, u32[]{:S(2)}) copy-start(bf16[384,1536]{1,0:T(8,128)(2,1)} %param.30) | copy-start | bytes 3538948
  8.7 153.3 %all-to-all-start = ((bf16[32,4,1]{1,2,0:T(2,128)(2,1)}), bf16[32,4,1]{1,2,0:T(2,128)(2,1)S(1)}, u32[]{:S(2)}, u32[]{:S(2)}) async-start(bf16[32,4,1]{1,2,0:T(2,128)(2,1)} %all_to_all.24), calls=%async_computation | async-start | bytes 32768 | tf_op jit(solution)/shard_map/all_to_all | solution.py:87
  306.6 143.9 %all-to-all-start.2 = ((bf16[128,64,384]{2,1,0:T(8,128)(2,1)}), bf16[128,64,384]{2,1,0:T(8,128)(2,1)}, u32[]{:S(2)}, u32[]{:S(2)}) async-start(bf16[128,64,384]{2,1,0:T(8,128)(2,1)} %param.24), calls=%async_computation.2 | async-start | bytes 12582912 | tf_op jit(solution)/shard_map/all_to_all | solution.py:86
  505.4 12.8 copy-start.3
  661.5 85.8 %copy-start.30 = (f32[5120]{0:T(1024)}, f32[5120]{0:T(1024)S(1)}, u32[]{:S(2)}) copy-start(f32[5120]{0:T(1024)S(1)} %multiply_reduce_fusion.3) | copy-start | bytes 61444
  661.6 85.7 %copy-start.16 = (f32[5120]{0:T(1024)}, f32[5120]{0:T(1024)S(1)}, u32[]{:S(2)}) copy-start(f32[5120]{0:T(1024)S(1)} %fusion.69) | copy-start | bytes 61444
  663.8 83.5 %copy-start.24 = (f32[5120]{0:T(1024)S(1)}, f32[5120]{0:T(1024)}, u32[]{:S(2)}) copy-start(f32[5120]{0:T(1024)} %get-tuple-element.237) | copy-start | bytes 61444
  663.8 83.5 %copy-start.52 = (bf16[1536,384]{1,0:T(8,128)(2,1)S(1)}, bf16[1536,384]{1,0:T(8,128)(2,1)}, u32[]{:S(2)}) copy-start(bf16[1536,384]{1,0:T(8,128)(2,1)} %param.32) | copy-start | bytes 3538948
  805.0 12.4 slice-start.2
  1138.5 21.7 %slice-start.8 = ((s8[7864320]{0:T(1024)(128)(4,1)}), s8[4194304]{0:T(1024)(128)(4,1)S(1)}, s32[]{:S(2)}) async-start(s8[7864320]{0:T(1024)(128)(4,1)} %bitcast.126), calls=%async_computation.14 | async-start | bytes 8388608
  1142.9 11.6 copy-start.34
  1142.9 11.6 copy-start.27
  1142.9 17.3 %slice-start.9 = ((s8[7864320]{0:T(1024)(128)(4,1)}), s8[3670016]{0:T(1024)(128)(4,1)S(1)}, s32[]{:S(2)}) async-start(s8[7864320]{0:T(1024)(128)(4,1)} %bitcast.126), calls=%async_computation.15 | async-start | bytes 7340032
  1198.0 41.3 %copy-start.37 = (pred[128,64]{1,0:T(8,128)(4,1)S(1)}, pred[128,64]{1,0:T(8,128)(4,1)}, u32[]{:S(2)}) copy-start(pred[128,64]{1,0:T(8,128)(4,1)} %iota_compare_fusion.2) | copy-start | bytes 24580
  1394.9 249.6 %all-to-all-start.3 = ((bf16[128,64,384]{2,1,0:T(8,128)(2,1)}), bf16[128,64,384]{2,1,0:T(8,128)(2,1)}, u32[]{:S(2)}, u32[]{:S(2)}) async-start(bf16[128,64,384]{2,1,0:T(8,128)(2,1)} %get-tuple-element.229), calls=%async_computation.3 | async-start | bytes 12582912 | tf_op jit(solution)/shard_map/all_to_all | solution.py:248
  1398.7 283.7 %all-reduce.15.cloned.1.call-start = ((), (), s32[]{:S(2)}) async-start(), calls=%async_computation.5 | async-start | bytes 14155776 | tf_op jit(solution)/shard_map/psum | solution.py:224
  1398.8 21.0 %slice-start.6 = ((s8[7864320]{0:T(1024)(128)(4,1)}), s8[4194304]{0:T(1024)(128)(4,1)S(1)}, s32[]{:S(2)}) async-start(s8[7864320]{0:T(1024)(128)(4,1)} %bitcast.124), calls=%async_computation.12 | async-start | bytes 8388608
  1405.3 14.5 slice-start.7
  1405.3 14.5 copy-start.60
  1419.8 11.4 copy-start.15
  1419.8 11.4 copy-start.18
  1419.8 11.4 copy-start.40
  1431.2 13.9 copy-start.36
  1431.2 14.0 copy-start.51
  (60 other events, 345.7 us)
Sparse Core Ops, SparseCore 0:
  1445.2 237.2 all-reduce.14
where the time goes:
time: 1720 us; the launch traced here: 1700 us
  matrix products  491 us (29%)
  blocking collectives  439 us (26%)
  local copies, waits for them, and re-layouts  407 us (24%)
  waiting for transfers between devices  171 us (10%)
  other arithmetic  129 us (8%)
  loops' own time  33.4 us (2%)
    psum x1, blocking collectives, per_device(): lax.psum((grad_w_qkv, grad_b_query, grad_b_value, grad_w_out, grad_b_out,...  150 us
    gather x4, local copies, waits for them, and re-layouts, per_device(): grid_rows[picks]  145 us
    all_to_all x1, blocking collectives, per_device(): lax.all_to_all(gathered, ('wide', 'narrow'), split_axis=0, concat_axis=0,...  145 us
    all_to_all x1, blocking collectives, per_device(): lax.all_to_all(out_grads, ('wide', 'narrow'), split_axis=0, concat_axis=0...  144 us
    all_to_all x1, waiting for transfers between devices, per_device(): lax.all_to_all(upstream, ('wide', 'narrow'), split_axis=0, concat_axis=0,...  133 us
    dot_general x20, matrix products, block_scores(): jnp.einsum('qhe,khe->hqk', query_blk, key_blk, preferred_element_type=f32)  88.6 us
    unnamed x154, local copies, waits for them, and re-layouts  83.6 us
    dot_general x1, matrix products, per_device(): up_proj = jnp.dot(normed2_b, w_up, preferred_element_type=f32) + b_up  83.5 us
  transfers between devices with their start and end apart: 4, of which 2 were waited for; matrix products, arithmetic and copies ran while one was open for 15% of the time, Pallas kernels for 0%

commit v1 on v0

v1 whole, which is shorter than its diff:
```python
import functools

import jax
import jax.numpy as jnp
from jax import lax
from jax.experimental import pallas as pl
from jax.experimental.pallas import tpu as pltpu
from jax.sharding import PartitionSpec as P

HEAD = 64
EPS = 1e-06
FILL = -1e30
ROWS = 512
TILE = 16
UNROLL = 4
GROUP = 8
CHUNK = 256
VMEM_BYTES = 60 * 1024 * 1024
f32 = jnp.float32
bf16 = jnp.bfloat16


def mm(left, right):
    return lax.dot_general(left, right, (((1,), (0,)), ((), ())), preferred_element_type=f32)


def mm_nt(left, right):
    return lax.dot_general(left, right, (((1,), (1,)), ((), ())), preferred_element_type=f32)


def mm_tn(left, right):
    return lax.dot_general(left, right, (((0,), (0,)), ((), ())), preferred_element_type=f32)


def row_norm(values):
    width = values.shape[-1]
    mean = jnp.sum(values, axis=-1, keepdims=True) * (1.0 / width)
    centered = values - mean
    variance = jnp.sum(centered * centered, axis=-1, keepdims=True) * (1.0 / width)
    rstd = lax.rsqrt(variance + EPS)
    return centered * rstd, rstd


def norm_back(grad, unit, rstd):
    width = grad.shape[-1]
    first = jnp.sum(grad, axis=-1, keepdims=True) * (1.0 / width)
    second = jnp.sum(grad * unit, axis=-1, keepdims=True) * (1.0 / width)
    return (grad - first - unit * second) * rstd


def fold(values):
    rows, width = values.shape
    return jnp.sum(values.reshape(rows // 8, 8, width), axis=0)


def head_mask(heads):
    size = heads * HEAD
    row = lax.broadcasted_iota(jnp.int32, (size, size), 0) // HEAD
    col = lax.broadcasted_iota(jnp.int32, (size, size), 1) // HEAD
    return row == col


def head_parts(width):
    parts, at = [], 0
    while at < width:
        size = min(4 * HEAD, width - at)
        parts.append((at, size))
        at += size
    return parts


def block_heads(values, at, size):
    part = values[:, at : at + size]
    count = size // HEAD
    tiled = jnp.concatenate([part] * count, axis=0)
    return jnp.where(head_mask(count), tiled, jnp.zeros((), tiled.dtype))


def heads_dot(left, stacked):
    parts = [
        mm_nt(left[:, at : at + size], block)
        for (at, size), block in zip(head_parts(left.shape[1]), stacked)
    ]
    return jnp.concatenate(parts, axis=1)


def heads_out(left, stacked):
    parts = [
        mm(left[:, at : at + size], block)
        for (at, size), block in zip(head_parts(left.shape[1]), stacked)
    ]
    return jnp.concatenate(parts, axis=1)


def heads_out_t(weights, values):
    window = weights.shape[1] // (values.shape[1] // HEAD)
    parts = []
    for at in range(0, values.shape[1], 2 * HEAD):
        pair = mm_tn(weights[:, at : at + 2 * HEAD], values[:, at : at + 2 * HEAD])
        lane = lax.broadcasted_iota(jnp.int32, (window, 2 * HEAD), 1)
        parts.append(jnp.where(lane < HEAD, pair[:window], pair[window:]))
    return jnp.concatenate(parts, axis=1)


def merge_store(ref, base, head, window):
    old = ref[pl.ds(base, TILE), :]
    row = lax.broadcasted_iota(jnp.int32, (TILE, window.shape[1]), 0)
    ref[pl.ds(base, TILE), :] = jnp.where(row >= head, window[:TILE], old)
    rest = window.shape[0] - TILE
    ref[pl.ds(base + TILE, rest), :] = window[TILE:]


def forward_kernel(
    fields, slots, width, hidden,
    counts, patches, visible, upstream,
    w_qkv, qkv_bias, w_out, b_out, w_up, b_up, w_down, b_down,
    gain_attn, shift_attn, gain_mlp, shift_mlp,
    starts, x_out, qkv_out, probs_out, att_out, mix_out, enc_out,
    g_up, g_down, g_out, gb_up, gb_down, gb_out, gg_mlp, gs_mlp,
    x_v, g_v, qkv_v, mix_v, probs_v, row_sems, probs_sems,
):
    def place(f, at):
        count = counts[f]
        head = lax.rem(at, TILE)
        at = jnp.where(head + count > slots, at + TILE - head, at)
        starts[f] = at
        return at + count

    total = lax.fori_loop(0, fields, place, 0)
    starts[fields] = total
    blocks = (total + ROWS - 1) // ROWS
    for ref in (g_up, g_down, g_out, gb_up, gb_down, gb_out, gg_mlp, gs_mlp):
        ref[...] = jnp.zeros_like(ref)

    def where_is(f):
        start = starts[f]
        head = lax.rem(start, TILE)
        return pl.multiple_of(start - head, TILE), head, counts[f]

    def pack(patch_blk, vis_blk, up_blk):
        step = pl.program_id(0)
        patch_row = lax.broadcasted_iota(jnp.int32, (patch_blk.shape[1], slots), 0)
        rows = lax.broadcasted_iota(jnp.int32, (slots, slots), 0)
        cols = lax.broadcasted_iota(jnp.int32, (slots, slots), 1)
        done = []
        for u in range(GROUP):
            base, head, count = where_is(step * GROUP + u)
            picks = pltpu.roll(vis_blk[pl.ds(u, 1), :], head, axis=1)[:, :slots]
            take = (patch_row == picks).astype(f32).astype(bf16)
            x_win = mm_tn(take, patch_blk[u]).astype(bf16)
            shift = ((rows - cols == head) & (cols < count)).astype(f32).astype(bf16)
            g_win = mm(shift, up_blk[u]).astype(bf16)
            done.append((base, head, x_win, g_win))
        for base, head, x_win, g_win in done:
            merge_store(x_v, base, head, x_win)
            merge_store(g_v, base, head, g_win)

    pltpu.emit_pipeline(
        pack,
        grid=(fields // GROUP,),
        in_specs=[
            pl.BlockSpec((GROUP,) + patches.shape[1:], lambda i: (i, 0, 0)),
            pl.BlockSpec((GROUP, visible.shape[1]), lambda i: (i, 0)),
            pl.BlockSpec((GROUP,) + upstream.shape[1:], lambda i: (i, 0, 0)),
        ],
    )(patches, visible, upstream)
    last, _, _ = where_is(fields - 1)
    tail = pl.multiple_of(last + slots, TILE)
    x_v[pl.ds(tail, ROWS), :] = jnp.zeros((ROWS, width), bf16)
    g_v[pl.ds(tail, ROWS), :] = jnp.zeros((ROWS, width), bf16)

    def block_copies(i):
        rows = pl.ds(pl.multiple_of(i * ROWS, ROWS), ROWS)
        return (
            pltpu.make_async_copy(x_v.at[rows], x_out.at[rows], row_sems.at[0, i]),
            pltpu.make_async_copy(qkv_v.at[rows], qkv_out.at[rows], row_sems.at[1, i]),
            pltpu.make_async_copy(g_v.at[rows], att_out.at[rows], row_sems.at[2, i]),
            pltpu.make_async_copy(mix_v.at[rows], mix_out.at[rows], row_sems.at[3, i]),
            pltpu.make_async_copy(x_v.at[rows], enc_out.at[rows], row_sems.at[4, i]),
        )

    def project(i, carry):
        rows = pl.ds(pl.multiple_of(i * ROWS, ROWS), ROWS)
        block_copies(i)[0].start()
        unit, _ = row_norm(x_v[rows, :].astype(f32))
        normed = (unit * gain_attn[...] + shift_attn[...]).astype(bf16)
        qkv_v[rows, :] = (mm(normed, w_qkv[...]) + qkv_bias[...]).astype(bf16)
        block_copies(i)[1].start()
        return carry

    lax.fori_loop(0, blocks, project, 0)
    edge = pl.multiple_of(blocks * ROWS, ROWS)
    qkv_v[pl.ds(edge, slots), :] = jnp.zeros((slots, 3 * width), bf16)

    def probs_copy(i):
        slot = lax.rem(i, 2)
        return pltpu.make_async_copy(
            probs_v.at[slot], probs_out.at[pl.ds(i * UNROLL, UNROLL)], probs_sems.at[slot]
        )

    def attend(i, carry):
        slot = lax.rem(i, 2)

        @pl.when(i >= 2)
        def _():
            probs_copy(i - 2).wait()

        done = []
        for u in range(UNROLL):
            base, head, count = where_is(i * UNROLL + u)
            window = pl.ds(base, slots)
            query = qkv_v[window, 0:width]
            key = qkv_v[window, width : 2 * width]
            value = qkv_v[window, 2 * width : 3 * width]
            stacked = [block_heads(query, at, size) for at, size in head_parts(width)]
            scores = heads_dot(key, stacked)
            row = lax.broadcasted_iota(jnp.int32, scores.shape, 0)
            scores = jnp.where((row >= head) & (row < head + count), scores, FILL)
            top = jnp.max(scores, axis=0, keepdims=True)
            expo = jnp.exp(scores - top)
            total_row = jnp.sum(expo, axis=0, keepdims=True)
            probs = (expo * (1.0 / total_row)).astype(bf16)
            probs_v[slot, u] = probs
            done.append((base, head, heads_out_t(probs, value).astype(bf16)))
        for base, head, mixed in done:
            merge_store(mix_v, base, head, mixed)
        probs_copy(i).start()
        return carry

    steps = fields // UNROLL
    lax.fori_loop(0, steps, attend, 0)
    probs_copy(steps - 2).wait()
    probs_copy(steps - 1).wait()
    mix_v[pl.ds(tail, ROWS), :] = jnp.zeros((ROWS, width), bf16)

    def feed(i, carry):
        rows = pl.ds(pl.multiple_of(i * ROWS, ROWS), ROWS)
        copies = block_copies(i)
        mixed = mix_v[rows, :]
        grad_b = g_v[rows, :]
        grad = grad_b.astype(f32)
        residual = x_v[rows, :].astype(f32) + (mm(mixed, w_out[...]) + b_out[...])
        unit, rstd = row_norm(residual)
        normed = (unit * gain_mlp[...] + shift_mlp[...]).astype(bf16)
        normed_t = normed.T
        grad_t = grad_b.T
        down = jnp.zeros((ROWS, width), f32)
        d_normed = jnp.zeros((ROWS, width), f32)
        for at in range(0, hidden, CHUNK):
            cols = slice(at, at + CHUNK)
            up = mm(normed, w_up[:, cols]) + b_up[:, cols]
            d_act = mm_nt(grad_b, w_down[cols, :])
            cdf = 0.5 + 0.5 * lax.erf(up * 0.7071067811865476)
            pdf = 0.3989422804014327 * jnp.exp(-0.5 * up * up)
            act = (up * cdf).astype(bf16)
            d_up_f = d_act * (cdf + up * pdf)
            d_up = d_up_f.astype(bf16)
            gb_up[:, cols] += fold(d_up_f)
            down += mm(act, w_down[cols, :])
            d_normed += mm_nt(d_up, w_up[:, cols])
            g_down[:, cols] += mm(grad_t, act)
            g_up[:, cols] += mm(normed_t, d_up)
        copies[0].wait()
        x_v[rows, :] = (residual + down + b_down[...]).astype(bf16)
        copies[4].start()
        gb_down[...] += fold(grad)
        gg_mlp[...] += fold(d_normed * unit)
        gs_mlp[...] += fold(d_normed)
        d_residual = grad + norm_back(d_normed * gain_mlp[...], unit, rstd)
        d_att = d_residual.astype(bf16)
        gb_out[...] += fold(d_residual)
        g_out[...] += mm_tn(mixed, d_att)
        g_v[rows, :] = d_att
        copies[2].start()
        mix_v[rows, :] = mm_nt(d_att, w_out[...]).astype(bf16)
        copies[3].start()
        return carry

    lax.fori_loop(0, blocks, feed, 0)

    def drain(i, carry):
        for copy in block_copies(i)[1:]:
            copy.wait()
        return carry

    lax.fori_loop(0, blocks, drain, 0)


def backward_kernel(
    fields, slots, width,
    counts, starts, visible, qkv, probs, att, mix, x_in, enc,
    w_qkv, gain_attn, shift_attn,
    encoded, input_grad, g_qkv, gb_qkv, gg_attn, gs_attn,
    qkv_v, mix_v, packed_v, din_v, probs_v, row_sems, probs_sems, enc_sem,
):
    total = starts[fields]
    blocks = (total + ROWS - 1) // ROWS
    for ref in (g_qkv, gb_qkv, gg_attn, gs_attn):
        ref[...] = jnp.zeros_like(ref)

    def where_is(f):
        start = starts[f]
        head = lax.rem(start, TILE)
        return pl.multiple_of(start - head, TILE), head, counts[f]

    def block_copies(i):
        rows = pl.ds(pl.multiple_of(i * ROWS, ROWS), ROWS)
        return (
            pltpu.make_async_copy(qkv.at[rows], qkv_v.at[rows], row_sems.at[0, i]),
            pltpu.make_async_copy(mix.at[rows], mix_v.at[rows], row_sems.at[1, i]),
        )

    def fetch(i, carry):
        for copy in block_copies(i):
            copy.start()
        return carry

    lax.fori_loop(0, blocks, fetch, 0)

    def probs_copy(i):
        slot = lax.rem(i, 2)
        return pltpu.make_async_copy(
            probs.at[pl.ds(i * UNROLL, UNROLL)], probs_v.at[slot], probs_sems.at[slot]
        )

    steps = fields // UNROLL
    probs_copy(0).start()
    edge = pl.multiple_of(blocks * ROWS, ROWS)
    qkv_v[pl.ds(edge, slots), :] = jnp.zeros((slots, 3 * width), bf16)
    mix_v[pl.ds(edge, slots), :] = jnp.zeros((slots, width), bf16)

    def arrive(i, carry):
        for copy in block_copies(i):
            copy.wait()
        return carry

    def attend(i, ready):
        slot = lax.rem(i, 2)
        base_last, _, _ = where_is(i * UNROLL + UNROLL - 1)
        need = jnp.minimum((base_last + slots - 1) // ROWS + 1, blocks)
        lax.fori_loop(ready, need, arrive, 0)

        @pl.when(i + 1 < steps)
        def _():
            probs_copy(i + 1).start()

        probs_copy(i).wait()
        done = []
        for u in range(UNROLL):
            base, head, count = where_is(i * UNROLL + u)
            window = pl.ds(base, slots)
            query = qkv_v[window, 0:width]
            key = qkv_v[window, width : 2 * width]
            value = qkv_v[window, 2 * width : 3 * width]
            grad = mix_v[window, :]
            row = lax.broadcasted_iota(jnp.int32, grad.shape, 0)
            grad = jnp.where((row >= head) & (row < head + count), grad, jnp.zeros((), bf16))
            weights_b = probs_v[slot, u]
            weights = weights_b.astype(f32)
            grad_blocks = [block_heads(grad, at, size) for at, size in head_parts(width)]
            query_blocks = [block_heads(query, at, size) for at, size in head_parts(width)]
            d_probs = heads_dot(value, grad_blocks)
            inner = jnp.sum(weights * d_probs, axis=0, keepdims=True)
            d_scores = (weights * (d_probs - inner)).astype(bf16)
            d_query = heads_out_t(d_scores, key) * (HEAD**-0.5)
            d_key = heads_out(d_scores, query_blocks)
            d_value = heads_out(weights_b, grad_blocks)
            done.append((base, head, d_query.astype(bf16), d_key.astype(bf16), d_value.astype(bf16)))
        for base, head, d_query, d_key, d_value in done:
            merge_store(packed_v.at[:, 0:width], base, head, d_query)
            merge_store(packed_v.at[:, width : 2 * width], base, head, d_key)
            merge_store(packed_v.at[:, 2 * width : 3 * width], base, head, d_value)
        return jnp.maximum(ready, need)

    ready = lax.fori_loop(0, steps, attend, 0)
    lax.fori_loop(ready, blocks, arrive, 0)
    last, _, _ = where_is(fields - 1)
    tail = pl.multiple_of(last + slots, TILE)
    packed_v[pl.ds(tail, ROWS), :] = jnp.zeros((ROWS, 3 * width), bf16)
    enc_v = mix_v

    def enc_copy(i):
        rows = pl.ds(pl.multiple_of(i * ROWS, ROWS), ROWS)
        return pltpu.make_async_copy(enc.at[rows], enc_v.at[rows], row_sems.at[2, i])

    def fetch_enc(i, carry):
        enc_copy(i).start()
        return carry

    lax.fori_loop(0, blocks, fetch_enc, 0)

    def project(x_blk, att_blk):
        i = pl.program_id(0)
        rows = pl.ds(pl.multiple_of(i * ROWS, ROWS), ROWS)
        packed = packed_v[rows, :]
        unit, rstd = row_norm(x_blk[...].astype(f32))
        normed = (unit * gain_attn[...] + shift_attn[...]).astype(bf16)
        g_qkv[...] += mm_tn(normed, packed)
        gb_qkv[...] += fold(packed.astype(f32))
        d_normed = mm_nt(packed, w_qkv[...])
        gg_attn[...] += fold(d_normed * unit)
        gs_attn[...] += fold(d_normed)
        d_in = att_blk[...].astype(f32) + norm_back(d_normed * gain_attn[...], unit, rstd)
        din_v[rows, :] = d_in.astype(bf16)

    pltpu.emit_pipeline(
        project,
        grid=(blocks,),
        in_specs=[
            pl.BlockSpec((ROWS, width), lambda i: (i, 0)),
            pl.BlockSpec((ROWS, width), lambda i: (i, 0)),
        ],
    )(x_in, att)

    def enc_arrive(i, carry):
        enc_copy(i).wait()
        return carry

    lax.fori_loop(0, blocks, enc_arrive, 0)
    din_v[pl.ds(edge, slots), :] = jnp.zeros((slots, width), bf16)
    enc_v[pl.ds(edge, slots), :] = jnp.zeros((slots, width), bf16)

    def unpack(vis_blk, enc_blk, grad_blk):
        step = pl.program_id(0)
        patch_row = lax.broadcasted_iota(jnp.int32, (grad_blk.shape[1], slots), 0)
        rows = lax.broadcasted_iota(jnp.int32, (slots, slots), 0)
        cols = lax.broadcasted_iota(jnp.int32, (slots, slots), 1)
        for u in range(GROUP):
            base, head, count = where_is(step * GROUP + u)
            window = pl.ds(base, slots)
            picks = pltpu.roll(vis_blk[pl.ds(u, 1), :], head, axis=1)[:, :slots]
            put = (patch_row == picks).astype(f32).astype(bf16)
            grad_blk[u] = mm(put, din_v[window, :]).astype(bf16)
            shift = ((cols - rows == head) & (rows < count)).astype(f32).astype(bf16)
            enc_blk[u] = mm(shift, enc_v[window, :]).astype(bf16)

    pltpu.emit_pipeline(
        unpack,
        grid=(fields // GROUP,),
        in_specs=[pl.BlockSpec((GROUP, visible.shape[1]), lambda i: (i, 0))],
        out_specs=[
            pl.BlockSpec((GROUP,) + encoded.shape[1:], lambda i: (i, 0, 0)),
            pl.BlockSpec((GROUP,) + input_grad.shape[1:], lambda i: (i, 0, 0)),
        ],
    )(visible, encoded, input_grad)


def local_block(
    patches, visible, counts, upstream, w_qkv, b_query, b_value, w_out, b_out,
    w_up, b_up, w_down, b_down, gain_attn, shift_attn, gain_mlp, shift_mlp,
):
    fields, patch_rows, width = patches.shape
    slots = visible.shape[1]
    hidden = w_up.shape[1]
    cap = (fields * slots + ROWS - 1) // ROWS * ROWS
    tall = cap + ROWS + slots
    blocks = tall // ROWS
    shape = jax.ShapeDtypeStruct
    hbm = pl.BlockSpec(memory_space=pl.ANY)
    vmem = pl.BlockSpec(memory_space=pltpu.VMEM)
    smem = pl.BlockSpec(memory_space=pltpu.SMEM)
    slot_iota = lax.broadcasted_iota(jnp.int32, visible.shape, 1)
    live_vis = jnp.where(slot_iota < counts[:, None], visible, -1)
    live_vis = jnp.pad(live_vis, ((0, 0), (0, 128 - slots)), constant_values=-1)
    scale = HEAD**-0.5
    w_scaled = jnp.concatenate([w_qkv[:, :width] * scale, w_qkv[:, width:]], axis=1)
    qkv_bias = jnp.concatenate([b_query * scale, jnp.zeros_like(b_query), b_value])
    row = lambda v: v[None, :]
    (
        starts, x_rows, qkv, probs, att, mix, enc,
        g_up, g_down, g_out, gb_up, gb_down, gb_out, gg_mlp, gs_mlp,
    ) = pl.pallas_call(
        functools.partial(forward_kernel, fields, slots, width, hidden),
        out_shape=[
            shape((fields + 1,), jnp.int32),
            shape((cap, width), bf16),
            shape((cap, 3 * width), bf16),
            shape((fields, slots, width), bf16),
            shape((cap, width), bf16),
            shape((cap, width), bf16),
            shape((cap, width), bf16),
            shape((width, hidden), f32),
            shape((width, hidden), f32),
            shape((width, width), f32),
            shape((8, hidden), f32),
            shape((8, width), f32),
            shape((8, width), f32),
            shape((8, width), f32),
            shape((8, width), f32),
        ],
        in_specs=[smem, hbm, hbm, hbm] + [vmem] * 12,
        out_specs=[smem] + [hbm] * 6 + [vmem] * 8,
        scratch_shapes=[
            pltpu.VMEM((tall, width), bf16),
            pltpu.VMEM((tall, width), bf16),
            pltpu.VMEM((cap + slots, 3 * width), bf16),
            pltpu.VMEM((tall, width), bf16),
            pltpu.VMEM((2, UNROLL, slots, width), bf16),
            pltpu.SemaphoreType.DMA((5, blocks)),
            pltpu.SemaphoreType.DMA((2,)),
        ],
        compiler_params=pltpu.CompilerParams(vmem_limit_bytes=VMEM_BYTES),
        name="forward_rows",
    )(
        counts, patches, live_vis, upstream,
        w_scaled, row(qkv_bias), w_out, row(b_out), w_up, row(b_up), w_down, row(b_down),
        row(gain_attn), row(shift_attn), row(gain_mlp), row(shift_mlp),
    )
    encoded, input_grad, g_qkv, gb_qkv, gg_attn, gs_attn = pl.pallas_call(
        functools.partial(backward_kernel, fields, slots, width),
        out_shape=[
            shape((fields, slots, width), bf16),
            shape((fields, patch_rows, width), bf16),
            shape((width, 3 * width), f32),
            shape((8, 3 * width), f32),
            shape((8, width), f32),
            shape((8, width), f32),
        ],
        in_specs=[smem, smem] + [hbm] * 7 + [vmem] * 3,
        out_specs=[hbm] * 2 + [vmem] * 4,
        scratch_shapes=[
            pltpu.VMEM((cap + slots, 3 * width), bf16),
            pltpu.VMEM((cap + slots, width), bf16),
            pltpu.VMEM((tall, 3 * width), bf16),
            pltpu.VMEM((cap + slots, width), bf16),
            pltpu.VMEM((2, UNROLL, slots, width), bf16),
            pltpu.SemaphoreType.DMA((3, blocks)),
            pltpu.SemaphoreType.DMA((2,)),
            pltpu.SemaphoreType.DMA,
        ],
        compiler_params=pltpu.CompilerParams(vmem_limit_bytes=VMEM_BYTES),
        name="backward_rows",
    )(
        counts, starts, live_vis, qkv, probs, att, mix, x_rows, enc,
        w_qkv, row(gain_attn), row(shift_attn),
    )
    return (
        encoded, input_grad, g_qkv, g_out, g_up, g_down,
        gb_qkv, gb_out, gb_up, gb_down, gg_attn, gs_attn, gg_mlp, gs_mlp,
    )


def per_device(*args):
    (
        encoded, input_grad, g_qkv, g_out, g_up, g_down,
        gb_qkv, gb_out, gb_up, gb_down, gg_attn, gs_attn, gg_mlp, gs_mlp,
    ) = local_block(*args)
    width = g_out.shape[0]
    small = [gb_qkv, gb_out, gb_up, gb_down, gg_attn, gs_attn, gg_mlp, gs_mlp]
    flat = jnp.concatenate([jnp.sum(v, axis=0) for v in small])
    g_qkv, g_out, g_up, g_down, flat = lax.psum(
        (g_qkv, g_out, g_up, g_down, flat), ("wide", "narrow")
    )
    out, at = [], 0
    for v in small:
        out.append(flat[at : at + v.shape[1]])
        at += v.shape[1]
    s_qkv, s_out, s_up, s_down, s_ga, s_sa, s_gm, s_sm = out
    return (
        encoded, input_grad, g_qkv, s_qkv[:width], s_qkv[2 * width :], g_out, s_out,
        g_up, s_up, g_down.T, s_down, s_ga, s_sa, s_gm, s_sm,
    )


def solution(mesh):
    rows = P(("wide", "narrow"))
    return jax.shard_map(
        per_device,
        mesh=mesh,
        in_specs=(rows,) * 4 + (P(),) * 13,
        out_specs=(rows,) * 2 + (P(),) * 13,
        check_vma=False,
    )
```

time: 1720 us -> 451 us (0.26); the launches traced: 1700 us -> 450 us
  matrix products: 491 us -> 0 us
  local copies, waits for them, and re-layouts: 407 us -> 20.1 us
  blocking collectives: 439 us -> 54.7 us
  Pallas kernels: 0 us -> 235 us
  other arithmetic: 129 us -> 4.29 us
  waiting for transfers between devices: 171 us -> 122 us
  loops' own time: 33.4 us -> 0 us
    dot_general x82 -> x0, matrix products: 491 us -> none  [the longest x20 88.6 us: block_scores(): jnp.einsum('qhe,khe->hqk', query_blk, key_blk, preferred_element_type=f32)]
    all_to_all x2 -> x0, blocking collectives: 289 us -> none  [the longest x1 145 us: per_device(): lax.all_to_all(gathered, ('wide', 'narrow'), split_axis=0, concat_axis=0,...]
    pallas_call x0 -> x2, Pallas kernels: none -> 235 us  [the longest x1 145 us: local_block(): pl.pallas_call(functools.partial(forward_kernel, fields, slots, width, hi...]
    gather x7 -> x0, local copies, waits for them, and re-layouts: 227 us -> none  [the longest x4 145 us: per_device(): grid_rows[picks]]
    all_to_all x3 -> x0, waiting for transfers between devices: 133 us -> none  [the longest x1 133 us: per_device(): lax.all_to_all(upstream, ('wide', 'narrow'), split_axis=0, concat_axis=0,...]
    psum x1, blocking collectives: 150 us -> 54.7 us  [per_device(): lax.psum((g_qkv, g_out, g_up, g_down, flat), ('wide', 'narrow'))]
    psum x1, waiting for transfers between devices: 37.9 us -> 122 us  [per_device(): lax.psum((g_qkv, g_out, g_up, g_down, flat), ('wide', 'narrow'))]
    unnamed x154 -> x34, local copies, waits for them, and re-layouts: 83.6 us -> 8.84 us
  transfers between devices with their start and end apart: 4 -> 1, of which waited for: 2 -> 1; matrix products, arithmetic and copies ran while one was open for 15% -> 0% of each run, Pallas kernels for 0% -> 0%
where the time goes in v1:
time: 451 us; the launch traced here: 450 us
  Pallas kernels  235 us (52%)
  waiting for transfers between devices  122 us (27%)
  blocking collectives  54.7 us (12%)
  local copies, waits for them, and re-layouts  20.1 us (4%)
  between operations  14.3 us (3%)
    pallas_call x1, Pallas kernels, local_block(): pl.pallas_call(functools.partial(forward_kernel, fields, slots, width, hi...  145 us
    psum x1, waiting for transfers between devices, per_device(): lax.psum((g_qkv, g_out, g_up, g_down, flat), ('wide', 'narrow'))  122 us
    pallas_call x1, Pallas kernels, local_block(): pl.pallas_call(functools.partial(backward_kernel, fields, slots, width),...  89.7 us
    psum x1, blocking collectives, per_device(): lax.psum((g_qkv, g_out, g_up, g_down, flat), ('wide', 'narrow'))  54.7 us
    broadcast_in_dim x8, local copies, waits for them, and re-layouts, local_block(): row = lambda v: v[None, :]  9.36 us
  transfers between devices with their start and end apart: 1, of which 1 were waited for; matrix products, arithmetic and copies ran while one was open for 0% of the time, Pallas kernels for 0%

profile of v1, /device:TPU:0, one launch (start us, length us, event | category | flops | bytes accessed | tf_op | source)
XLA Modules:
  0.0 450.2 jit_solution(291254640890848422)
XLA Ops:
  7.2 1.1 slice_multiply_fusion
  8.3 0.8 copy.32
  9.1 1.2 broadcast_in_dim.40.gain_attn
  10.4 1.2 broadcast_in_dim.41.shift_attn
  11.6 0.7 broadcast_multiply_fusion
  12.3 0.7 pad_maximum_fusion.1
  13.6 1.3 broadcast_in_dim.38.b_up
  14.9 1.2 broadcast_in_dim.37.b_out
  16.2 1.2 broadcast_in_dim.39.b_down
  17.4 1.2 broadcast_in_dim.42.gain_mlp
  18.6 1.2 broadcast_in_dim.43.shift_mlp
  19.9 0.7 fusion
  20.6 0.6 pad.4.visible
  21.3 1.0 pad_maximum_fusion.w_qkv
  22.2 145.2 %forward_rows.1 = (s32[129]{0:T(256)}, bf16[8192,384]{1,0:T(8,128)(2,1)}, bf16[8192,1152]{1,0:T(8,128)(2,1)}, bf16[128,64,384]{2,1,0:T(8,128)(2,1)}, bf16[8192,3...) custom-call(s32[128]{0:T(128)} %counts.3, ...), custom_call_target="tpu_custom_call" | custom-call | tf_op jit(solution)/shard_map/forward_rows/pallas_call | solution.py:472
  167.4 89.7 %backward_rows.1 = (bf16[128,64,384]{2,1,0:T(8,128)(2,1)}, bf16[128,128,384]{2,1,0:T(8,128)(2,1)}, f32[384,1152]{1,0:T(8,128)}, f32[8,1152]{1,0:T(8,128)}, f32[8,384]{1,0:T(8,128)}, /*index=5*/f32[8,384]{1,0:T(8,128)}) custom-call(s32[128]{0:T(128)} %counts.3, s32[129]{0:T(256)} %get-tuple-element.36.starts, s32[128,128]{1,0:T(8,128)} %pad.4.visible, ...), custom_call_target="tpu_custom_call" | custom-call | tf_op jit(solution)/shard_map/backward_rows/pallas_call | solution.py:509
  257.3 0.7 copy-done.4
  258.3 54.7 %psum.36 = f32[4992]{0:T(1024)S(1)} all-reduce(f32[4992]{0:T(1024)S(1)} %constant_dynamic-update-slice_fusion), channel_id=1, replica_groups=mesh['wide'=8,'narrow'=4] {'wide','narrow'}, use_global_device_ids=true, to_apply=%region_9.10 | all-reduce | flops 4992 | bytes 39936 | tf_op jit(solution)/shard_map/psum | solution.py:551
  313.5 0.6 fusion.1
  314.1 122.0 %all-reduce.4.cloned.1.call-done = (f32[384,1152]{1,0:T(8,128)}, f32[384,384]{1,0:T(8,128)}, f32[384,1536]{1,0:T(8,128)}, f32[1536,384]{0,1:T(8,128)}) async-done(((f32[384,1152]{1,0:T(8,128)}, f32[384,384]{1,0:T(8,128)}, f32[384,1536]{1,0:T(8,128)}, f32[1536,384]{0,1:T(8,128)}), (f32[384,1152]{1,0:T(8,128)}, f32[384,384]{1,0:T(8,128)}, f32[384,1536]{1,0:T(8,128)}, ...) | async-done | bytes 7077904 | tf_op jit(solution)/shard_map/psum | solution.py:551
  436.1 3.2 copy.33
  439.3 1.2 copy.46
  440.7 0.8 copy.47
  441.9 1.4 copy.48
  (45 shorter events, 2.2 us)
Async XLA Ops:
  7.2 14.1 %slice-start = ((bf16[384,1152]{1,0:T(8,128)(2,1)}), bf16[384,768]{1,0:T(8,128)(2,1)S(1)}, s32[]{:S(2)}) async-start(bf16[384,1152]{1,0:T(8,128)(2,1)} %w_qkv.1), calls=%async_computation.1 | async-start | bytes 1179648 | tf_op jit(solution)/shard_map/slice | solution.py:466
  7.2 428.9 %all-reduce.4.cloned.1.call-start = ((), (), s32[]{:S(2)}) async-start(), calls=%async_computation | async-start | bytes 14155776 | tf_op jit(solution)/shard_map/psum | solution.py:551
  257.2 0.8 copy-start.4
  257.2 0.8 copy-start.8
  257.2 0.8 copy-start.3
  257.2 0.8 copy-start.7
  257.2 0.9 copy-start.10
  257.2 0.9 copy-start.9
  257.2 0.9 copy-start.6
  257.2 0.9 copy-start.5
  436.1 3.2 copy-start.1
  439.3 1.4 copy-start.2
  439.3 2.7 copy-start
Sparse Core Ops, SparseCore 0:
  257.4 178.6 all-reduce.3

commit v2 on v1

--- a/solution.py
+++ b/solution.py
@@ -12,12 +12,15 @@
 FILL = -1e30
 ROWS = 512
 TILE = 16
-UNROLL = 4
+UNROLL = 8
 GROUP = 8
 CHUNK = 256
 VMEM_BYTES = 60 * 1024 * 1024
 f32 = jnp.float32
 bf16 = jnp.bfloat16
+
+
+LANES = 128
 
 
 def mm(left, right):
@@ -53,11 +56,10 @@
     return jnp.sum(values.reshape(rows // 8, 8, width), axis=0)
 
 
-def head_mask(heads):
-    size = heads * HEAD
-    row = lax.broadcasted_iota(jnp.int32, (size, size), 0) // HEAD
-    col = lax.broadcasted_iota(jnp.int32, (size, size), 1) // HEAD
-    return row == col
+def fill_mask(mask):
+    row = lax.broadcasted_iota(jnp.int32, mask.shape, 0) // HEAD
+    col = lax.broadcasted_iota(jnp.int32, mask.shape, 1) // HEAD
+    mask[...] = (row == col).astype(f32).astype(bf16)
 
 
 def head_parts(width):
@@ -69,11 +71,12 @@
     return parts
 
 
-def block_heads(values, at, size):
-    part = values[:, at : at + size]
-    count = size // HEAD
-    tiled = jnp.concatenate([part] * count, axis=0)
-    return jnp.where(head_mask(count), tiled, jnp.zeros((), tiled.dtype))
+def block_heads(values, mask):
+    blocks = []
+    for at, size in head_parts(values.shape[1]):
+        tiled = jnp.concatenate([values[:, at : at + size]] * (size // HEAD), axis=0)
+        blocks.append(tiled * mask[:size, :size])
+    return blocks
 
 
 def heads_dot(left, stacked):
@@ -93,13 +96,31 @@
 
 
 def heads_out_t(weights, values):
-    window = weights.shape[1] // (values.shape[1] // HEAD)
+    window = weights[0].shape[0] // 2
     parts = []
-    for at in range(0, values.shape[1], 2 * HEAD):
-        pair = mm_tn(weights[:, at : at + 2 * HEAD], values[:, at : at + 2 * HEAD])
+    for k, at in enumerate(range(0, values.shape[1], 2 * HEAD)):
+        pair = mm(weights[k], values[:, at : at + 2 * HEAD])
         lane = lax.broadcasted_iota(jnp.int32, (window, 2 * HEAD), 1)
         parts.append(jnp.where(lane < HEAD, pair[:window], pair[window:]))
     return jnp.concatenate(parts, axis=1)
+
+
+def pairs_t(values):
+    return [values[:, at : at + 2 * HEAD].T for at in range(0, values.shape[1], 2 * HEAD)]
+
+
+def add_blocks(sums, at, values):
+    rows = values.shape[0]
+    for k in range(values.shape[1] // LANES):
+        block = pl.ds(at + k * rows, rows)
+        sums[block, :] += values[:, k * LANES : (k + 1) * LANES]
+
+
+def add_vector(sums, at, partial):
+    vector = jnp.sum(partial, axis=0, keepdims=True)
+    for k in range(vector.shape[1] // LANES):
+        sums[pl.ds(at + k, 1), :] = vector[:, k * LANES : (k + 1) * LANES]
+    return at + vector.shape[1] // LANES
 
 
 def merge_store(ref, base, head, window):
@@ -110,15 +131,149 @@
     ref[pl.ds(base + TILE, rest), :] = window[TILE:]
 
 
+def mesh_bits(sizes):
+    wide = [("wide", 1 << k) for k in range(sizes["wide"].bit_length() - 1)]
+    narrow = [("narrow", 1 << k) for k in range(sizes["narrow"].bit_length() - 1)]
+    return wide, narrow
+
+
+def exchange_orders(sizes):
+    wide, narrow = mesh_bits(sizes)
+    first, last = narrow[:1], wide[-1:]
+    middle = wide[:1] + narrow[1:] + wide[1:-1]
+    return [first + middle[k:] + middle[:k] + last for k in range(min(3, len(middle)))]
+
+
+def partner(axis, distance):
+    mine = lax.axis_index(axis)
+    side = lax.rem(mine // distance, 2)
+    return side, {axis: mine + distance * (1 - 2 * side)}
+
+
+def rows_of_parts(rows, orders):
+    unit = TILE << len(orders[0])
+    units, parts, at = rows // unit, [], 0
+    for k in range(len(orders)):
+        share = (units + len(orders) - 1 - k) // len(orders) * unit
+        if share:
+            parts.append((at, share))
+        at += share
+    return parts
+
+
+class Reducer:
+    def __init__(self, orders, rows, total, sent, got, summed, send_sems, recv_sems):
+        self.orders, self.total, self.sent, self.got, self.summed = orders, total, sent, got, summed
+        self.send_sems, self.recv_sems = send_sems, recv_sems
+        self.stages = len(orders[0])
+        self.parts = rows_of_parts(rows, orders)
+        self.copies = []
+        self.step = 0
+
+    def greet(self):
+        barrier = pltpu.get_barrier_semaphore()
+        for axis, distance in self.orders[0]:
+            _, other = partner(axis, distance)
+            pl.semaphore_signal(barrier, inc=1, device_id=other, device_id_type=pl.DeviceIdType.MESH)
+        pl.semaphore_wait(barrier, self.stages)
+
+    def segment(self, part, stage):
+        base, share = self.parts[part]
+        for k in range(stage):
+            side, _ = partner(*self.orders[part][k])
+            base = base + side * (share >> (k + 1))
+        return base, share >> stage
+
+    def copy(self, part, stage, src, dst):
+        axis, distance = self.orders[part][stage if stage < self.stages else 2 * self.stages - 1 - stage]
+        _, other = partner(axis, distance)
+        return pltpu.make_async_remote_copy(
+            src_ref=src, dst_ref=dst,
+            send_sem=self.send_sems.at[part, stage], recv_sem=self.recv_sems.at[part, stage],
+            device_id=other, device_id_type=pl.DeviceIdType.MESH,
+        )
+
+    def slot(self, part, stage):
+        base, share = self.parts[part]
+        return pl.ds(base + share - (share >> stage), share >> (stage + 1))
+
+    def halve(self, part, stage):
+        base, size = self.segment(part, stage)
+        side, _ = partner(*self.orders[part][stage])
+        half = size // 2
+        away = pl.ds(pl.multiple_of(base + (1 - side) * half, TILE), half)
+        slot = self.slot(part, stage)
+        self.sent[slot, :] = self.total[away, :].astype(bf16)
+        return self.copy(part, stage, self.sent.at[slot], self.got.at[slot])
+
+    def double(self, part, stage):
+        level = 2 * self.stages - stage
+        base, size = self.segment(part, level)
+        here = pl.ds(pl.multiple_of(base, TILE), size)
+        return self.copy(part, stage, self.summed.at[here], self.summed.at[here])
+
+    def arrive(self, part, stage):
+        self.copies[stage][part].wait()
+        if stage < self.stages:
+            base, size = self.segment(part, stage + 1)
+            here = pl.ds(pl.multiple_of(base, TILE), size)
+            value = self.total[here, :] + self.got[self.slot(part, stage), :].astype(f32)
+            if stage + 1 < self.stages:
+                self.total[here, :] = value
+            else:
+                self.summed[here, :] = value.astype(bf16)
+
+    def advance(self):
+        stage = self.step
+        now = []
+        for part in range(len(self.parts)):
+            if stage:
+                self.arrive(part, stage - 1)
+            if stage < 2 * self.stages:
+                copy = self.halve(part, stage) if stage < self.stages else self.double(part, stage)
+                copy.start()
+                now.append(copy)
+        self.copies.append(now)
+        self.step += 1
+
+    @property
+    def steps(self):
+        return 2 * self.stages + 1
+
+
+def padded_rows(rows, sizes):
+    unit = TILE * sizes["wide"] * sizes["narrow"]
+    return (rows + unit - 1) // unit * unit
+
+
+def reducer_scratch(rows, sizes):
+    orders = exchange_orders(sizes)
+    flights = (len(orders), 2 * len(orders[0]))
+    return [
+        pltpu.VMEM((rows, LANES), bf16),
+        pltpu.VMEM((rows, LANES), bf16),
+        pltpu.VMEM((rows, LANES), bf16),
+        pltpu.SemaphoreType.DMA(flights),
+        pltpu.SemaphoreType.DMA(flights),
+    ]
+
+
+def sum_rows(width, hidden):
+    up, out = width * hidden // LANES, width * width // LANES
+    return 0, up, 2 * up, 2 * up + out
+
+
 def forward_kernel(
     fields, slots, width, hidden,
     counts, patches, visible, upstream,
     w_qkv, qkv_bias, w_out, b_out, w_up, b_up, w_down, b_down,
     gain_attn, shift_attn, gain_mlp, shift_mlp,
     starts, x_out, qkv_out, probs_out, att_out, mix_out, enc_out,
-    g_up, g_down, g_out, gb_up, gb_down, gb_out, gg_mlp, gs_mlp,
-    x_v, g_v, qkv_v, mix_v, probs_v, row_sems, probs_sems,
+    sums,
+    x_v, g_v, qkv_v, mix_v, probs_v, act_v, dup_v, mask_v,
+    gb_up, gb_down, gb_out, gg_mlp, gs_mlp, row_sems, probs_sems,
 ):
+    up_at, down_at, out_at, vector_at = sum_rows(width, hidden)
     def place(f, at):
         count = counts[f]
         head = lax.rem(at, TILE)
@@ -129,8 +284,9 @@
     total = lax.fori_loop(0, fields, place, 0)
     starts[fields] = total
     blocks = (total + ROWS - 1) // ROWS
-    for ref in (g_up, g_down, g_out, gb_up, gb_down, gb_out, gg_mlp, gs_mlp):
+    for ref in (sums, gb_up, gb_down, gb_out, gg_mlp, gs_mlp):
         ref[...] = jnp.zeros_like(ref)
+    fill_mask(mask_v)
 
     def where_is(f):
         start = starts[f]
@@ -142,16 +298,16 @@
         patch_row = lax.broadcasted_iota(jnp.int32, (patch_blk.shape[1], slots), 0)
         rows = lax.broadcasted_iota(jnp.int32, (slots, slots), 0)
         cols = lax.broadcasted_iota(jnp.int32, (slots, slots), 1)
-        done = []
-        for u in range(GROUP):
-            base, head, count = where_is(step * GROUP + u)
+        places = [where_is(step * GROUP + u) for u in range(GROUP)]
+        takes, shifts = [], []
+        for u, (base, head, count) in enumerate(places):
             picks = pltpu.roll(vis_blk[pl.ds(u, 1), :], head, axis=1)[:, :slots]
-            take = (patch_row == picks).astype(f32).astype(bf16)
-            x_win = mm_tn(take, patch_blk[u]).astype(bf16)
-            shift = ((rows - cols == head) & (cols < count)).astype(f32).astype(bf16)
-            g_win = mm(shift, up_blk[u]).astype(bf16)
-            done.append((base, head, x_win, g_win))
-        for base, head, x_win, g_win in done:
+            takes.append((patch_row == picks).astype(f32).astype(bf16))
+            shifts.append(((rows - cols == head) & (cols < count)).astype(f32).astype(bf16))
+        takes = [take.T for take in takes]
+        x_wins = [mm(takes[u], patch_blk[u]).astype(bf16) for u in range(GROUP)]
+        g_wins = [mm(shifts[u], up_blk[u]).astype(bf16) for u in range(GROUP)]
+        for (base, head, _), x_win, g_win in zip(places, x_wins, g_wins):
             merge_store(x_v, base, head, x_win)
             merge_store(g_v, base, head, g_win)
 
@@ -205,25 +361,28 @@
         def _():
             probs_copy(i - 2).wait()
 
-        done = []
-        for u in range(UNROLL):
-            base, head, count = where_is(i * UNROLL + u)
-            window = pl.ds(base, slots)
-            query = qkv_v[window, 0:width]
-            key = qkv_v[window, width : 2 * width]
-            value = qkv_v[window, 2 * width : 3 * width]
-            stacked = [block_heads(query, at, size) for at, size in head_parts(width)]
-            scores = heads_dot(key, stacked)
-            row = lax.broadcasted_iota(jnp.int32, scores.shape, 0)
-            scores = jnp.where((row >= head) & (row < head + count), scores, FILL)
-            top = jnp.max(scores, axis=0, keepdims=True)
-            expo = jnp.exp(scores - top)
+        places = [where_is(i * UNROLL + u) for u in range(UNROLL)]
+        windows = [pl.ds(base, slots) for base, _, _ in places]
+        scores = []
+        for window in windows:
+            stacked = block_heads(qkv_v[window, 0:width], mask_v)
+            scores.append(heads_dot(qkv_v[window, width : 2 * width], stacked))
+        weights = []
+        for (_, head, count), score in zip(places, scores):
+            row = lax.broadcasted_iota(jnp.int32, score.shape, 0)
+            score = jnp.where((row >= head) & (row < head + count), score, FILL)
+            expo = jnp.exp(score - jnp.max(score, axis=0, keepdims=True))
             total_row = jnp.sum(expo, axis=0, keepdims=True)
-            probs = (expo * (1.0 / total_row)).astype(bf16)
-            probs_v[slot, u] = probs
-            done.append((base, head, heads_out_t(probs, value).astype(bf16)))
-        for base, head, mixed in done:
-            merge_store(mix_v, base, head, mixed)
+            weights.append((expo * (1.0 / total_row)).astype(bf16))
+        for u, weight in enumerate(weights):
+            probs_v[slot, u] = weight
+        turned = [pairs_t(weight) for weight in weights]
+        mixed = [
+            heads_out_t(weight, qkv_v[window, 2 * width : 3 * width]).astype(bf16)
+            for weight, window in zip(turned, windows)
+        ]
+        for (base, head, _), out in zip(places, mixed):
+            merge_store(mix_v, base, head, out)
         probs_copy(i).start()
         return carry
 
@@ -244,22 +403,20 @@
         normed = (unit * gain_mlp[...] + shift_mlp[...]).astype(bf16)
         normed_t = normed.T
         grad_t = grad_b.T
-        down = jnp.zeros((ROWS, width), f32)
-        d_normed = jnp.zeros((ROWS, width), f32)
         for at in range(0, hidden, CHUNK):
             cols = slice(at, at + CHUNK)
             up = mm(normed, w_up[:, cols]) + b_up[:, cols]
             d_act = mm_nt(grad_b, w_down[cols, :])
             cdf = 0.5 + 0.5 * lax.erf(up * 0.7071067811865476)
             pdf = 0.3989422804014327 * jnp.exp(-0.5 * up * up)
-            act = (up * cdf).astype(bf16)
-            d_up_f = d_act * (cdf + up * pdf)
-            d_up = d_up_f.astype(bf16)
-            gb_up[:, cols] += fold(d_up_f)
-            down += mm(act, w_down[cols, :])
-            d_normed += mm_nt(d_up, w_up[:, cols])
-            g_down[:, cols] += mm(grad_t, act)
-            g_up[:, cols] += mm(normed_t, d_up)
+            act_v[:, cols] = (up * cdf).astype(bf16)
+            d_up = d_act * (cdf + up * pdf)
+            dup_v[:, cols] = d_up.astype(bf16)
+            gb_up[:, cols] += fold(d_up)
+        down = mm(act_v[...], w_down[...])
+        d_normed = mm_nt(dup_v[...], w_up[...])
+        add_blocks(sums, up_at, mm(normed_t, dup_v[...]))
+        add_blocks(sums, down_at, mm(grad_t, act_v[...]))
         copies[0].wait()
         x_v[rows, :] = (residual + down + b_down[...]).astype(bf16)
         copies[4].start()
@@ -269,7 +426,7 @@
         d_residual = grad + norm_back(d_normed * gain_mlp[...], unit, rstd)
         d_att = d_residual.astype(bf16)
         gb_out[...] += fold(d_residual)
-        g_out[...] += mm_tn(mixed, d_att)
+        add_blocks(sums, out_at, mm_tn(mixed, d_att))
         g_v[rows, :] = d_att
         copies[2].start()
         mix_v[rows, :] = mm_nt(d_att, w_out[...]).astype(bf16)
@@ -277,6 +434,9 @@
         return carry
 
     lax.fori_loop(0, blocks, feed, 0)
+    at = vector_at
+    for partial in (gb_up, gb_down, gb_out, gg_mlp, gs_mlp):
+        at = add_vector(sums, at, partial[...])
 
     def drain(i, carry):
         for copy in block_copies(i)[1:]:
@@ -290,12 +450,13 @@
     fields, slots, width,
     counts, starts, visible, qkv, probs, att, mix, x_in, enc,
     w_qkv, gain_attn, shift_attn,
-    encoded, input_grad, g_qkv, gb_qkv, gg_attn, gs_attn,
-    qkv_v, mix_v, packed_v, din_v, probs_v, row_sems, probs_sems, enc_sem,
+    encoded, input_grad, sums,
+    gb_qkv, gg_attn, gs_attn, qkv_v, mix_v, packed_v, din_v, probs_v, mask_v, row_sems, probs_sems,
 ):
+    fill_mask(mask_v)
     total = starts[fields]
     blocks = (total + ROWS - 1) // ROWS
-    for ref in (g_qkv, gb_qkv, gg_attn, gs_attn):
+    for ref in (sums, gb_qkv, gg_attn, gs_attn):
         ref[...] = jnp.zeros_like(ref)
 
     def where_is(f):
@@ -345,31 +506,39 @@
             probs_copy(i + 1).start()
 
         probs_copy(i).wait()
-        done = []
-        for u in range(UNROLL):
-            base, head, count = where_is(i * UNROLL + u)
-            window = pl.ds(base, slots)
-            query = qkv_v[window, 0:width]
-            key = qkv_v[window, width : 2 * width]
-            value = qkv_v[window, 2 * width : 3 * width]
-            grad = mix_v[window, :]
-            row = lax.broadcasted_iota(jnp.int32, grad.shape, 0)
-            grad = jnp.where((row >= head) & (row < head + count), grad, jnp.zeros((), bf16))
-            weights_b = probs_v[slot, u]
-            weights = weights_b.astype(f32)
-            grad_blocks = [block_heads(grad, at, size) for at, size in head_parts(width)]
-            query_blocks = [block_heads(query, at, size) for at, size in head_parts(width)]
-            d_probs = heads_dot(value, grad_blocks)
-            inner = jnp.sum(weights * d_probs, axis=0, keepdims=True)
-            d_scores = (weights * (d_probs - inner)).astype(bf16)
-            d_query = heads_out_t(d_scores, key) * (HEAD**-0.5)
-            d_key = heads_out(d_scores, query_blocks)
-            d_value = heads_out(weights_b, grad_blocks)
-            done.append((base, head, d_query.astype(bf16), d_key.astype(bf16), d_value.astype(bf16)))
-        for base, head, d_query, d_key, d_value in done:
-            merge_store(packed_v.at[:, 0:width], base, head, d_query)
-            merge_store(packed_v.at[:, width : 2 * width], base, head, d_key)
-            merge_store(packed_v.at[:, 2 * width : 3 * width], base, head, d_value)
+        places = [where_is(i * UNROLL + u) for u in range(UNROLL)]
+        windows = [pl.ds(base, slots) for base, _, _ in places]
+        grads = []
+        for (_, head, count), window in zip(places, windows):
+            row = lax.broadcasted_iota(jnp.int32, (slots, width), 0)
+            live = ((row >= head) & (row < head + count)).astype(f32).astype(bf16)
+            grads.append(block_heads(mix_v[window, :] * live, mask_v))
+        d_probs = [
+            heads_dot(qkv_v[window, 2 * width : 3 * width], grad)
+            for window, grad in zip(windows, grads)
+        ]
+        d_values = [
+            heads_out(probs_v[slot, u], grad).astype(bf16) for u, grad in enumerate(grads)
+        ]
+        d_scores = []
+        for u, d_prob in enumerate(d_probs):
+            weights = probs_v[slot, u].astype(f32)
+            weighted = weights * d_prob
+            inner = jnp.sum(weighted, axis=0, keepdims=True)
+            d_scores.append((weighted - weights * inner).astype(bf16))
+        d_keys = [
+            heads_out(d_score, block_heads(qkv_v[window, 0:width], mask_v)).astype(bf16)
+            for window, d_score in zip(windows, d_scores)
+        ]
+        turned = [pairs_t(d_score) for d_score in d_scores]
+        d_queries = [
+            (heads_out_t(d_score, qkv_v[window, width : 2 * width]) * (HEAD**-0.5)).astype(bf16)
+            for window, d_score in zip(windows, turned)
+        ]
+        for u, (base, head, _) in enumerate(places):
+            merge_store(packed_v.at[:, 0:width], base, head, d_queries[u])
+            merge_store(packed_v.at[:, width : 2 * width], base, head, d_keys[u])
+            merge_store(packed_v.at[:, 2 * width : 3 * width], base, head, d_values[u])
         return jnp.maximum(ready, need)
 
     ready = lax.fori_loop(0, steps, attend, 0)
@@ -395,7 +564,7 @@
         packed = packed_v[rows, :]
         unit, rstd = row_norm(x_blk[...].astype(f32))
         normed = (unit * gain_attn[...] + shift_attn[...]).astype(bf16)
-        g_qkv[...] += mm_tn(normed, packed)
+        add_blocks(sums, 0, mm_tn(normed, packed))
         gb_qkv[...] += fold(packed.astype(f32))
         d_normed = mm_nt(packed, w_qkv[...])
         gg_attn[...] += fold(d_normed * unit)
@@ -412,6 +581,10 @@
         ],
     )(x_in, att)
 
+    at = 3 * width * width // LANES
+    for partial in (gb_qkv, gg_attn, gs_attn):
+        at = add_vector(sums, at, partial[...])
+
     def enc_arrive(i, carry):
         enc_copy(i).wait()
         return carry
@@ -425,14 +598,15 @@
         patch_row = lax.broadcasted_iota(jnp.int32, (grad_blk.shape[1], slots), 0)
         rows = lax.broadcasted_iota(jnp.int32, (slots, slots), 0)
         cols = lax.broadcasted_iota(jnp.int32, (slots, slots), 1)
-        for u in range(GROUP):
-            base, head, count = where_is(step * GROUP + u)
-            window = pl.ds(base, slots)
+        places = [where_is(step * GROUP + u) for u in range(GROUP)]
+        puts, shifts = [], []
+        for u, (base, head, count) in enumerate(places):
             picks = pltpu.roll(vis_blk[pl.ds(u, 1), :], head, axis=1)[:, :slots]
-            put = (patch_row == picks).astype(f32).astype(bf16)
-            grad_blk[u] = mm(put, din_v[window, :]).astype(bf16)
-            shift = ((cols - rows == head) & (rows < count)).astype(f32).astype(bf16)
-            enc_blk[u] = mm(shift, enc_v[window, :]).astype(bf16)
+            puts.append((patch_row == picks).astype(f32).astype(bf16))
+            shifts.append(((cols - rows == head) & (rows < count)).astype(f32).astype(bf16))
+        for u, (base, _, _) in enumerate(places):
+            grad_blk[u] = mm(puts[u], din_v[pl.ds(base, slots), :]).astype(bf16)
+            enc_blk[u] = mm(shifts[u], enc_v[pl.ds(base, slots), :]).astype(bf16)
 
     pltpu.emit_pipeline(
         unpack,
@@ -446,6 +620,7 @@
 
 
 def local_block(
+    sizes,
     patches, visible, counts, upstream, w_qkv, b_query, b_value, w_out, b_out,
     w_up, b_up, w_down, b_down, gain_attn, shift_attn, gain_mlp, shift_mlp,
 ):
@@ -467,8 +642,7 @@
     qkv_bias = jnp.concatenate([b_query * scale, jnp.zeros_like(b_query), b_value])
     row = lambda v: v[None, :]
     (
-        starts, x_rows, qkv, probs, att, mix, enc,
-        g_up, g_down, g_out, gb_up, gb_down, gb_out, gg_mlp, gs_mlp,
+        starts, x_rows, qkv, probs, att, mix, enc, sums,
     ) = pl.pallas_call(
         functools.partial(forward_kernel, fields, slots, width, hidden),
         out_shape=[
@@ -479,23 +653,24 @@
             shape((cap, width), bf16),
             shape((cap, width), bf16),
             shape((cap, width), bf16),
-            shape((width, hidden), f32),
-            shape((width, hidden), f32),
-            shape((width, width), f32),
-            shape((8, hidden), f32),
-            shape((8, width), f32),
-            shape((8, width), f32),
-            shape((8, width), f32),
-            shape((8, width), f32),
+            shape((padded_rows(sum_rows(width, hidden)[3] + (hidden + 4 * width) // LANES, sizes), LANES), f32),
         ],
         in_specs=[smem, hbm, hbm, hbm] + [vmem] * 12,
-        out_specs=[smem] + [hbm] * 6 + [vmem] * 8,
+        out_specs=[smem] + [hbm] * 6 + [vmem],
         scratch_shapes=[
             pltpu.VMEM((tall, width), bf16),
             pltpu.VMEM((tall, width), bf16),
             pltpu.VMEM((cap + slots, 3 * width), bf16),
             pltpu.VMEM((tall, width), bf16),
             pltpu.VMEM((2, UNROLL, slots, width), bf16),
+            pltpu.VMEM((ROWS, hidden), bf16),
+            pltpu.VMEM((ROWS, hidden), bf16),
+            pltpu.VMEM((4 * HEAD, 4 * HEAD), bf16),
+            pltpu.VMEM((8, hidden), f32),
+            pltpu.VMEM((8, width), f32),
+            pltpu.VMEM((8, width), f32),
+            pltpu.VMEM((8, width), f32),
+            pltpu.VMEM((8, width), f32),
             pltpu.SemaphoreType.DMA((5, blocks)),
             pltpu.SemaphoreType.DMA((2,)),
         ],
@@ -506,27 +681,27 @@
         w_scaled, row(qkv_bias), w_out, row(b_out), w_up, row(b_up), w_down, row(b_down),
         row(gain_attn), row(shift_attn), row(gain_mlp), row(shift_mlp),
     )
-    encoded, input_grad, g_qkv, gb_qkv, gg_attn, gs_attn = pl.pallas_call(
+    encoded, input_grad, sums_b = pl.pallas_call(
         functools.partial(backward_kernel, fields, slots, width),
         out_shape=[
             shape((fields, slots, width), bf16),
             shape((fields, patch_rows, width), bf16),
-            shape((width, 3 * width), f32),
-            shape((8, 3 * width), f32),
-            shape((8, width), f32),
-            shape((8, width), f32),
+            shape((padded_rows((3 * width * width + 5 * width) // LANES, sizes), LANES), f32),
         ],
         in_specs=[smem, smem] + [hbm] * 7 + [vmem] * 3,
-        out_specs=[hbm] * 2 + [vmem] * 4,
+        out_specs=[hbm] * 2 + [vmem],
         scratch_shapes=[
+            pltpu.VMEM((8, 3 * width), f32),
+            pltpu.VMEM((8, width), f32),
+            pltpu.VMEM((8, width), f32),
             pltpu.VMEM((cap + slots, 3 * width), bf16),
             pltpu.VMEM((cap + slots, width), bf16),
             pltpu.VMEM((tall, 3 * width), bf16),
             pltpu.VMEM((cap + slots, width), bf16),
             pltpu.VMEM((2, UNROLL, slots, width), bf16),
+            pltpu.VMEM((4 * HEAD, 4 * HEAD), bf16),
             pltpu.SemaphoreType.DMA((3, blocks)),
             pltpu.SemaphoreType.DMA((2,)),
-            pltpu.SemaphoreType.DMA,
         ],
         compiler_params=pltpu.CompilerParams(vmem_limit_bytes=VMEM_BYTES),
         name="backward_rows",
@@ -534,38 +709,71 @@
         counts, starts, live_vis, qkv, probs, att, mix, x_rows, enc,
         w_qkv, row(gain_attn), row(shift_attn),
     )
+    return encoded, input_grad, sums, sums_b
+
+
+def sum_kernel(
+    orders, rows_a, rows_b, sums_a, sums_b, out_a, out_b, total_a, total_b,
+    sent_a, got_a, summed_a, send_a, recv_a, sent_b, got_b, summed_b, send_b, recv_b,
+):
+    first = Reducer(orders, rows_a, total_a, sent_a, got_a, summed_a, send_a, recv_a)
+    second = Reducer(orders, rows_b, total_b, sent_b, got_b, summed_b, send_b, recv_b)
+    first.greet()
+    total_a[...] = sums_a[...]
+    total_b[...] = sums_b[...]
+    for _ in range(first.steps):
+        first.advance()
+        second.advance()
+    out_a[...] = summed_a[...]
+    out_b[...] = summed_b[...]
+
+
+def add_up(sizes, sums_a, sums_b):
+    rows_a, rows_b = sums_a.shape[0], sums_b.shape[0]
+    return pl.pallas_call(
+        functools.partial(sum_kernel, exchange_orders(sizes), rows_a, rows_b),
+        out_shape=[jax.ShapeDtypeStruct(v.shape, bf16) for v in (sums_a, sums_b)],
+        scratch_shapes=[pltpu.VMEM(sums_a.shape, f32), pltpu.VMEM(sums_b.shape, f32)]
+        + reducer_scratch(rows_a, sizes)
+        + reducer_scratch(rows_b, sizes),
+        compiler_params=pltpu.CompilerParams(
+            collective_id=0, has_side_effects=True, vmem_limit_bytes=VMEM_BYTES
+        ),
+        name="sum_rows",
+    )(sums_a, sums_b)
+
+
+def unblock(blocked, at, rows, columns):
+    part = blocked[at : at + rows * columns // LANES].astype(f32)
+    return part.reshape(columns // LANES, rows, LANES).transpose(1, 0, 2).reshape(rows, columns)
+
+
+def per_device(sizes, *args):
+    encoded, input_grad, sums_a, sums_b = local_block(sizes, *args)
+    total_a, total_b = add_up(sizes, sums_a, sums_b)
+    width, hidden = args[9].shape
+    up_at, down_at, out_at, vector_at = sum_rows(width, hidden)
+    first = total_a[vector_at:].astype(f32).reshape(-1)
+    second = total_b[3 * width * width // LANES :].astype(f32).reshape(-1)
+
+    def take(flat, at, count):
+        return flat[at : at + count]
+
     return (
-        encoded, input_grad, g_qkv, g_out, g_up, g_down,
-        gb_qkv, gb_out, gb_up, gb_down, gg_attn, gs_attn, gg_mlp, gs_mlp,
-    )
-
-
-def per_device(*args):
-    (
-        encoded, input_grad, g_qkv, g_out, g_up, g_down,
-        gb_qkv, gb_out, gb_up, gb_down, gg_attn, gs_attn, gg_mlp, gs_mlp,
-    ) = local_block(*args)
-    width = g_out.shape[0]
-    small = [gb_qkv, gb_out, gb_up, gb_down, gg_attn, gs_attn, gg_mlp, gs_mlp]
-    flat = jnp.concatenate([jnp.sum(v, axis=0) for v in small])
-    g_qkv, g_out, g_up, g_down, flat = lax.psum(
-        (g_qkv, g_out, g_up, g_down, flat), ("wide", "narrow")
-    )
-    out, at = [], 0
-    for v in small:
-        out.append(flat[at : at + v.shape[1]])
-        at += v.shape[1]
-    s_qkv, s_out, s_up, s_down, s_ga, s_sa, s_gm, s_sm = out
-    return (
-        encoded, input_grad, g_qkv, s_qkv[:width], s_qkv[2 * width :], g_out, s_out,
-        g_up, s_up, g_down.T, s_down, s_ga, s_sa, s_gm, s_sm,
+        encoded, input_grad,
+        unblock(total_b, 0, width, 3 * width), take(second, 0, width), take(second, 2 * width, width),
+        unblock(total_a, out_at, width, width), take(first, hidden + width, width),
+        unblock(total_a, up_at, width, hidden), take(first, 0, hidden),
+        unblock(total_a, down_at, width, hidden).T, take(first, hidden, width),
+        take(second, 3 * width, width), take(second, 4 * width, width),
+        take(first, hidden + 2 * width, width), take(first, hidden + 3 * width, width),
     )
 
 
 def solution(mesh):
     rows = P(("wide", "narrow"))
     return jax.shard_map(
-        per_device,
+        functools.partial(per_device, dict(mesh.shape)),
         mesh=mesh,
         in_specs=(rows,) * 4 + (P(),) * 13,
         out_specs=(rows,) * 2 + (P(),) * 13,

time: 451 us -> 278 us (0.62)
  waiting for transfers between devices: 122 us -> 0 us
  blocking collectives: 54.7 us -> 0 us
  between operations: 14.3 us -> 0.76 us
  Pallas kernels: 235 us -> 242 us
  local copies, waits for them, and re-layouts: 20.1 us -> 26.8 us
    psum x1 -> x0, waiting for transfers between devices: 122 us -> none  [per_device(): lax.psum((g_qkv, g_out, g_up, g_down, flat), ('wide', 'narrow'))]
    pallas_call x0 -> x1, Pallas kernels: none -> 63.9 us  [add_up(): pl.pallas_call(functools.partial(sum_kernel, exchange_orders(sizes), rows...]
    psum x1 -> x0, blocking collectives: 54.7 us -> none  [per_device(): lax.psum((g_qkv, g_out, g_up, g_down, flat), ('wide', 'narrow'))]
    pallas_call x1, Pallas kernels: 145 us -> 113 us  [local_block(): pl.pallas_call(functools.partial(forward_kernel, fields, slots, width, hi...]
    pallas_call x1, Pallas kernels: 89.7 us -> 65.6 us  [local_block(): pl.pallas_call(functools.partial(backward_kernel, fields, slots, width),...]
  transfers between devices with their start and end apart: 1 -> 0, of which waited for: 1 -> 0; matrix products, arithmetic and copies ran while one was open for 0% -> 0% of each run, Pallas kernels for 0% -> 0%
where the time goes in v2:
time: 278 us; the launch traced here: 276 us
  Pallas kernels  242 us (87%)
  local copies, waits for them, and re-layouts  26.8 us (10%)
  other arithmetic  6.12 us (2%)
    pallas_call x1, Pallas kernels, local_block(): pl.pallas_call(functools.partial(forward_kernel, fields, slots, width, hi...  113 us
    pallas_call x1, Pallas kernels, local_block(): pl.pallas_call(functools.partial(backward_kernel, fields, slots, width),...  65.6 us
    pallas_call x1, Pallas kernels, add_up(): pl.pallas_call(functools.partial(sum_kernel, exchange_orders(sizes), rows...  63.9 us
    broadcast_in_dim x8, local copies, waits for them, and re-layouts, local_block(): row = lambda v: v[None, :]  9.42 us
    unnamed x6, local copies, waits for them, and re-layouts  5.75 us

profile of v2, /device:TPU:0, one launch (start us, length us, event | category | flops | bytes accessed | tf_op | source)
XLA Modules:
  0.0 275.8 jit_solution(4573311014861505890)
XLA Ops:
  0.7 1.3 broadcast_in_dim.40.gain_attn
  2.0 1.2 broadcast_in_dim.41.shift_attn
  3.2 1.2 broadcast_in_dim.37.b_out
  4.5 1.2 broadcast_in_dim.39.b_down
  5.7 1.2 broadcast_in_dim.42.gain_mlp
  6.9 1.2 broadcast_in_dim.43.shift_mlp
  10.2 1.3 broadcast_in_dim.38.b_up
  11.5 0.8 copy.37
  13.7 1.0 slice_multiply_fusion
  14.7 1.0 pad_maximum_fusion.w_qkv
  15.7 112.7 %forward_rows.1 = (s32[129]{0:T(256)}, bf16[8192,384]{1,0:T(8,128)(2,1)}, bf16[8192,1152]{1,0:T(8,128)(2,1)}, bf16[128,64,384]{2,1,0:T(8,128)(2,1)}, bf16[8192,3...) custom-call(s32[128]{0:T(128)} %counts.3, ...), custom_call_target="tpu_custom_call" | custom-call | tf_op jit(solution)/shard_map/forward_rows/pallas_call | solution.py:646
  128.4 65.6 %backward_rows.1 = (bf16[128,64,384]{2,1,0:T(8,128)(2,1)}, bf16[128,128,384]{2,1,0:T(8,128)(2,1)}, f32[3584,128]{1,0:T(8,128)}) custom-call(s32[128]{0:T(128)} %counts.3, s32[129]{0:T(256)} %get-tuple-element.28.starts, s32[128,128]{1,0:T(8,128)} %pad.4.visible, bf16[8192,1152]{1,0:T(8,128)(2,1)} %get-tuple-element.29.qkv, ...), custom_call_target="tpu_custom_call" | custom-call | tf_op jit(solution)/shard_map/backward_rows/pallas_call | solution.py:684
  194.0 63.9 %sum_rows.1 = (bf16[10752,128]{1,0:T(8,128)(2,1)}, bf16[3584,128]{1,0:T(8,128)(2,1)}) custom-call(f32[10752,128]{1,0:T(8,128)} %get-tuple-element.37.sums_a, f32[3584,128]{1,0:T(8,128)} %get-tuple-element.38.sums_b), custom_call_target="tpu_custom_call" | custom-call | tf_op jit(solution)/shard_map/sum_rows/pallas_call | solution.py:733
  257.9 0.9 slice_convert_fusion.1
  258.8 2.1 slice.80
  260.9 0.9 slice_convert_fusion
  263.1 1.0 slice.86
  264.0 1.2 fusion.1
  265.4 1.1 copy.43
  266.4 1.8 copy.38
  268.2 1.9 copy.42
  270.1 1.6 copy.40
  271.7 2.0 copy.44
  273.8 2.0 copy.41
  (14 shorter events, 5.0 us)
Async XLA Ops:
  0.6 14.1 %slice-start = ((bf16[384,1152]{1,0:T(8,128)(2,1)}), bf16[384,768]{1,0:T(8,128)(2,1)S(1)}, s32[]{:S(2)}) async-start(bf16[384,1152]{1,0:T(8,128)(2,1)} %w_qkv.1), calls=%async_computation | async-start | bytes 1179648 | tf_op jit(solution)/shard_map/slice | solution.py:641
  257.9 6.2 %copy-start = (bf16[10752,128]{1,0:T(8,128)(2,1)S(1)}, bf16[10752,128]{1,0:T(8,128)(2,1)}, u32[]{:S(2)}) copy-start(bf16[10752,128]{1,0:T(8,128)(2,1)} %get-tuple-element.40) | copy-start | bytes 8257540

commit v3 on v2

v3 whole, which is shorter than its diff:
```python
import functools

import jax
import jax.numpy as jnp
from jax import lax
from jax.experimental import pallas as pl
from jax.experimental.pallas import tpu as pltpu
from jax.sharding import PartitionSpec as P

HEAD = 64
EPS = 1e-06
FILL = -1e30
ROWS = 512
TILE = 16
UNROLL = 8
GROUP = 8
CHUNK = 256
VMEM_BYTES = 60 * 1024 * 1024
f32 = jnp.float32
bf16 = jnp.bfloat16


LANES = 128


def mm(left, right):
    return lax.dot_general(left, right, (((1,), (0,)), ((), ())), preferred_element_type=f32)


def mm_nt(left, right):
    return lax.dot_general(left, right, (((1,), (1,)), ((), ())), preferred_element_type=f32)


def mm_tn(left, right):
    return lax.dot_general(left, right, (((0,), (0,)), ((), ())), preferred_element_type=f32)


def row_norm(values):
    width = values.shape[-1]
    mean = jnp.sum(values, axis=-1, keepdims=True) * (1.0 / width)
    centered = values - mean
    variance = jnp.sum(centered * centered, axis=-1, keepdims=True) * (1.0 / width)
    rstd = lax.rsqrt(variance + EPS)
    return centered * rstd, rstd


def norm_back(grad, unit, rstd):
    width = grad.shape[-1]
    first = jnp.sum(grad, axis=-1, keepdims=True) * (1.0 / width)
    second = jnp.sum(grad * unit, axis=-1, keepdims=True) * (1.0 / width)
    return (grad - first - unit * second) * rstd


def fold(values):
    rows, width = values.shape
    return jnp.sum(values.reshape(rows // 8, 8, width), axis=0)


def fill_mask(mask):
    row = lax.broadcasted_iota(jnp.int32, mask.shape, 0) // HEAD
    col = lax.broadcasted_iota(jnp.int32, mask.shape, 1) // HEAD
    mask[...] = (row == col).astype(f32).astype(bf16)


def head_parts(width):
    parts, at = [], 0
    while at < width:
        size = min(4 * HEAD, width - at)
        parts.append((at, size))
        at += size
    return parts


def block_heads(values, mask):
    blocks = []
    for at, size in head_parts(values.shape[1]):
        tiled = jnp.concatenate([values[:, at : at + size]] * (size // HEAD), axis=0)
        blocks.append(tiled * mask[:size, :size])
    return blocks


def heads_dot(left, stacked):
    parts = [
        mm_nt(left[:, at : at + size], block)
        for (at, size), block in zip(head_parts(left.shape[1]), stacked)
    ]
    return jnp.concatenate(parts, axis=1)


def heads_out(left, stacked):
    parts = [
        mm(left[:, at : at + size], block)
        for (at, size), block in zip(head_parts(left.shape[1]), stacked)
    ]
    return jnp.concatenate(parts, axis=1)


def heads_out_t(weights, values):
    window = weights[0].shape[0] // 2
    parts = []
    for k, at in enumerate(range(0, values.shape[1], 2 * HEAD)):
        pair = mm(weights[k], values[:, at : at + 2 * HEAD])
        lane = lax.broadcasted_iota(jnp.int32, (window, 2 * HEAD), 1)
        parts.append(jnp.where(lane < HEAD, pair[:window], pair[window:]))
    return jnp.concatenate(parts, axis=1)


def pairs_t(values):
    return [values[:, at : at + 2 * HEAD].T for at in range(0, values.shape[1], 2 * HEAD)]


def add_blocks(sums, at, values):
    rows = values.shape[0]
    for k in range(values.shape[1] // LANES):
        block = pl.ds(at + k * rows, rows)
        sums[block, :] += values[:, k * LANES : (k + 1) * LANES]


def add_vector(sums, at, partial):
    vector = jnp.sum(partial, axis=0, keepdims=True)
    for k in range(vector.shape[1] // LANES):
        sums[pl.ds(at + k, 1), :] = vector[:, k * LANES : (k + 1) * LANES]
    return at + vector.shape[1] // LANES


def row(ref, cols=slice(None)):
    return ref[cols].reshape(1, -1)


def shifted_picks(vis, head, count):
    slots = vis.shape[1]
    lane = lax.broadcasted_iota(jnp.int32, vis.shape, 1)
    live = jnp.where(lane < count, vis, -1)
    wide = jnp.concatenate([live, jnp.full((1, LANES - slots), -1, jnp.int32)], axis=1)
    return pltpu.roll(wide, head, axis=1)[:, :slots]


def merge_store(ref, base, head, window):
    old = ref[pl.ds(base, TILE), :]
    row = lax.broadcasted_iota(jnp.int32, (TILE, window.shape[1]), 0)
    ref[pl.ds(base, TILE), :] = jnp.where(row >= head, window[:TILE], old)
    rest = window.shape[0] - TILE
    ref[pl.ds(base + TILE, rest), :] = window[TILE:]


def mesh_bits(sizes):
    wide = [("wide", 1 << k) for k in range(sizes["wide"].bit_length() - 1)]
    narrow = [("narrow", 1 << k) for k in range(sizes["narrow"].bit_length() - 1)]
    return wide, narrow


def exchange_orders(sizes):
    wide, narrow = mesh_bits(sizes)
    first, last = narrow[:1], wide[-1:]
    middle = wide[:1] + narrow[1:] + wide[1:-1]
    return [first + middle[k:] + middle[:k] + last for k in range(min(3, len(middle)))]


def partner(axis, distance):
    mine = lax.axis_index(axis)
    side = lax.rem(mine // distance, 2)
    return side, {axis: mine + distance * (1 - 2 * side)}


def rows_of_parts(rows, orders):
    unit = TILE << len(orders[0])
    units, parts, at = rows // unit, [], 0
    for k in range(len(orders)):
        share = (units + len(orders) - 1 - k) // len(orders) * unit
        if share:
            parts.append((at, share))
        at += share
    return parts


class Reducer:
    def __init__(self, orders, rows, total, sent, got, summed, send_sems, recv_sems):
        self.orders, self.total, self.sent, self.got, self.summed = orders, total, sent, got, summed
        self.send_sems, self.recv_sems = send_sems, recv_sems
        self.stages = len(orders[0])
        self.parts = rows_of_parts(rows, orders)

    def greet(self):
        barrier = pltpu.get_barrier_semaphore()
        for axis, distance in self.orders[0]:
            _, other = partner(axis, distance)
            pl.semaphore_signal(barrier, inc=1, device_id=other, device_id_type=pl.DeviceIdType.MESH)
        pl.semaphore_wait(barrier, self.stages)

    def segment(self, part, stage):
        base, share = self.parts[part]
        for k in range(stage):
            side, _ = partner(*self.orders[part][k])
            base = base + side * (share >> (k + 1))
        return base, share >> stage

    def copy(self, part, stage, src, dst):
        axis, distance = self.orders[part][stage if stage < self.stages else 2 * self.stages - 1 - stage]
        _, other = partner(axis, distance)
        return pltpu.make_async_remote_copy(
            src_ref=src, dst_ref=dst,
            send_sem=self.send_sems.at[part, stage], recv_sem=self.recv_sems.at[part, stage],
            device_id=other, device_id_type=pl.DeviceIdType.MESH,
        )

    def slot(self, part, stage):
        base, share = self.parts[part]
        return pl.ds(base + share - (share >> stage), share >> (stage + 1))

    def flight(self, part, stage):
        if stage < self.stages:
            slot = self.slot(part, stage)
            return self.copy(part, stage, self.sent.at[slot], self.got.at[slot])
        level = 2 * self.stages - stage
        base, size = self.segment(part, level)
        here = pl.ds(pl.multiple_of(base, TILE), size)
        return self.copy(part, stage, self.summed.at[here], self.summed.at[here])

    def leave(self, part, stage):
        if stage < self.stages:
            base, size = self.segment(part, stage)
            side, _ = partner(*self.orders[part][stage])
            half = size // 2
            away = pl.ds(pl.multiple_of(base + (1 - side) * half, TILE), half)
            self.sent[self.slot(part, stage), :] = self.total[away, :].astype(bf16)
        self.flight(part, stage).start()

    def arrive(self, part, stage):
        self.flight(part, stage).wait()
        if stage < self.stages:
            base, size = self.segment(part, stage + 1)
            here = pl.ds(pl.multiple_of(base, TILE), size)
            value = self.total[here, :] + self.got[self.slot(part, stage), :].astype(f32)
            if stage + 1 < self.stages:
                self.total[here, :] = value
            else:
                self.summed[here, :] = value.astype(bf16)

    def advance(self, stage):
        for part in range(len(self.parts)):
            if stage:
                self.arrive(part, stage - 1)
            if stage < 2 * self.stages:
                self.leave(part, stage)

    @property
    def steps(self):
        return 2 * self.stages + 1


def padded_rows(rows, sizes):
    unit = TILE * sizes["wide"] * sizes["narrow"]
    return (rows + unit - 1) // unit * unit


def reducer_scratch(rows, sizes):
    orders = exchange_orders(sizes)
    flights = (len(orders), 2 * len(orders[0]))
    return [
        pltpu.VMEM((rows, LANES), bf16),
        pltpu.VMEM((rows, LANES), bf16),
        pltpu.VMEM((rows, LANES), bf16),
        pltpu.SemaphoreType.DMA(flights),
        pltpu.SemaphoreType.DMA(flights),
    ]


def sum_rows(width, hidden):
    up, out = width * hidden // LANES, width * width // LANES
    return 0, up, 2 * up, 2 * up + out


def forward_kernel(
    fields, slots, width, hidden,
    counts, patches, visible, upstream,
    w_qkv, b_query, b_value, w_out, b_out, w_up, b_up, w_down, b_down,
    gain_attn, shift_attn, gain_mlp, shift_mlp,
    starts, x_out, qkv_out, probs_out, att_out, mix_out, enc_out, sums,
    x_v, g_v, qkv_v, mix_v, probs_v, act_v, dup_v, mask_v,
    gb_up, gb_down, gb_out, gg_mlp, gs_mlp, window_sems, probs_sems,
):
    up_at, down_at, out_at, vector_at = sum_rows(width, hidden)
    def place(f, at):
        count = counts[f]
        head = lax.rem(at, TILE)
        at = jnp.where(head + count > slots, at + TILE - head, at)
        starts[f] = at
        return at + count

    lax.fori_loop(0, fields, place, 0)
    last = starts[fields - 1]
    tail = pl.multiple_of(last - lax.rem(last, TILE) + slots, TILE)
    blocks = (tail + ROWS - 1) // ROWS
    for ref in (sums, gb_up, gb_down, gb_out, gg_mlp, gs_mlp):
        ref[...] = jnp.zeros_like(ref)
    fill_mask(mask_v)

    def where_is(f):
        start = starts[f]
        head = lax.rem(start, TILE)
        return pl.multiple_of(start - head, TILE), head, counts[f]

    def pack(patch_blk, vis_blk, up_blk, x_blk):
        step = pl.program_id(0)
        patch_row = lax.broadcasted_iota(jnp.int32, (patch_blk.shape[1], slots), 0)
        rows = lax.broadcasted_iota(jnp.int32, (slots, slots), 0)
        cols = lax.broadcasted_iota(jnp.int32, (slots, slots), 1)
        places = [where_is(step * GROUP + u) for u in range(GROUP)]
        takes, shifts = [], []
        for u, (base, head, count) in enumerate(places):
            picks = shifted_picks(vis_blk[pl.ds(u, 1), :], head, count)
            takes.append((patch_row == picks).astype(f32).astype(bf16))
            shifts.append(((rows - cols == head) & (cols < count)).astype(f32).astype(bf16))
        takes = [take.T for take in takes]
        x_wins = [mm(takes[u], patch_blk[u]).astype(bf16) for u in range(GROUP)]
        g_wins = [mm(shifts[u], up_blk[u]).astype(bf16) for u in range(GROUP)]
        for u, x_win in enumerate(x_wins):
            x_blk[u] = x_win
        for (base, head, _), x_win, g_win in zip(places, x_wins, g_wins):
            merge_store(x_v, base, head, x_win)
            merge_store(g_v, base, head, g_win)

    pltpu.emit_pipeline(
        pack,
        grid=(fields // GROUP,),
        in_specs=[
            pl.BlockSpec((GROUP,) + patches.shape[1:], lambda i: (i, 0, 0)),
            pl.BlockSpec((GROUP, visible.shape[1]), lambda i: (i, 0)),
            pl.BlockSpec((GROUP,) + upstream.shape[1:], lambda i: (i, 0, 0)),
        ],
        out_specs=[pl.BlockSpec((GROUP, slots, width), lambda i: (i, 0, 0))],
    )(patches, visible, upstream, x_out)
    x_v[pl.ds(tail, ROWS), :] = jnp.zeros((ROWS, width), bf16)
    g_v[pl.ds(tail, ROWS), :] = jnp.zeros((ROWS, width), bf16)

    def window_copy(f, src, dst, kind):
        base, _, _ = where_is(f)
        return pltpu.make_async_copy(src.at[pl.ds(base, slots)], dst.at[f], window_sems.at[kind])

    def project(i, carry):
        rows = pl.ds(pl.multiple_of(i * ROWS, ROWS), ROWS)
        unit, _ = row_norm(x_v[rows, :].astype(f32))
        normed = (unit * row(gain_attn) + row(shift_attn)).astype(bf16)
        third = [slice(k * width, (k + 1) * width) for k in range(3)]
        query = mm(normed, w_qkv[:, third[0]]) + row(b_query)
        qkv_v[rows, third[0]] = (query * HEAD**-0.5).astype(bf16)
        qkv_v[rows, third[1]] = mm(normed, w_qkv[:, third[1]]).astype(bf16)
        qkv_v[rows, third[2]] = (mm(normed, w_qkv[:, third[2]]) + row(b_value)).astype(bf16)
        return carry

    lax.fori_loop(0, blocks, project, 0)

    def probs_copy(i):
        slot = lax.rem(i, 2)
        return pltpu.make_async_copy(
            probs_v.at[slot], probs_out.at[pl.ds(i * UNROLL, UNROLL)], probs_sems.at[slot]
        )

    def attend(i, carry):
        slot = lax.rem(i, 2)

        @pl.when(i >= 2)
        def _():
            probs_copy(i - 2).wait()

        for u in range(UNROLL):
            window_copy(i * UNROLL + u, qkv_v, qkv_out, 0).start()
        places = [where_is(i * UNROLL + u) for u in range(UNROLL)]
        windows = [pl.ds(base, slots) for base, _, _ in places]
        scores = []
        for window in windows:
            stacked = block_heads(qkv_v[window, 0:width], mask_v)
            scores.append(heads_dot(qkv_v[window, width : 2 * width], stacked))
        weights = []
        for (_, head, count), score in zip(places, scores):
            slot_row = lax.broadcasted_iota(jnp.int32, score.shape, 0)
            live = (slot_row >= head) & (slot_row < head + count)
            score = jnp.where(live, score, FILL)
            expo = jnp.exp(score - jnp.max(score, axis=0, keepdims=True))
            total_row = jnp.sum(expo, axis=0, keepdims=True)
            weights.append((expo * (1.0 / total_row)).astype(bf16))
        for u, weight in enumerate(weights):
            probs_v[slot, u] = weight
        turned = [pairs_t(weight) for weight in weights]
        mixed = [
            heads_out_t(weight, qkv_v[window, 2 * width : 3 * width]).astype(bf16)
            for weight, window in zip(turned, windows)
        ]
        for (base, head, _), out in zip(places, mixed):
            merge_store(mix_v, base, head, out)
        probs_copy(i).start()
        return carry

    steps = fields // UNROLL
    lax.fori_loop(0, steps, attend, 0)
    probs_copy(steps - 2).wait()
    probs_copy(steps - 1).wait()
    mix_v[pl.ds(tail, ROWS), :] = jnp.zeros((ROWS, width), bf16)

    def feed(i, sent):
        rows = pl.ds(pl.multiple_of(i * ROWS, ROWS), ROWS)
        mixed = mix_v[rows, :]
        grad_b = g_v[rows, :]
        grad = grad_b.astype(f32)
        residual = x_v[rows, :].astype(f32) + (mm(mixed, w_out[...]) + row(b_out))
        unit, rstd = row_norm(residual)
        normed = (unit * row(gain_mlp) + row(shift_mlp)).astype(bf16)
        normed_t = normed.T
        grad_t = grad_b.T
        for at in range(0, hidden, CHUNK):
            cols = slice(at, at + CHUNK)
            up = mm(normed, w_up[:, cols]) + row(b_up, cols)
            d_act = mm_nt(grad_b, w_down[cols, :])
            cdf = 0.5 + 0.5 * lax.erf(up * 0.7071067811865476)
            pdf = 0.3989422804014327 * jnp.exp(-0.5 * up * up)
            act_v[:, cols] = (up * cdf).astype(bf16)
            d_up = d_act * (cdf + up * pdf)
            dup_v[:, cols] = d_up.astype(bf16)
            gb_up[:, cols] += fold(d_up)
        down = mm(act_v[...], w_down[...])
        d_normed = mm_nt(dup_v[...], w_up[...])
        add_blocks(sums, up_at, mm(normed_t, dup_v[...]))
        add_blocks(sums, down_at, mm(grad_t, act_v[...]))
        x_v[rows, :] = (residual + down + row(b_down)).astype(bf16)
        gb_down[...] += fold(grad)
        gg_mlp[...] += fold(d_normed * unit)
        gs_mlp[...] += fold(d_normed)
        d_residual = grad + norm_back(d_normed * row(gain_mlp), unit, rstd)
        d_att = d_residual.astype(bf16)
        gb_out[...] += fold(d_residual)
        add_blocks(sums, out_at, mm_tn(mixed, d_att))
        g_v[rows, :] = d_att
        mix_v[rows, :] = mm_nt(d_att, w_out[...]).astype(bf16)

        def finished(f):
            base, _, _ = where_is(jnp.minimum(f, fields - 1))
            return (f < fields) & (base + slots <= (i + 1) * ROWS)

        def send(f):
            window_copy(f, g_v, att_out, 1).start()
            window_copy(f, mix_v, mix_out, 2).start()
            window_copy(f, x_v, enc_out, 3).start()
            return f + 1

        return lax.while_loop(finished, send, sent)

    lax.fori_loop(0, blocks, feed, 0)
    at = vector_at
    for partial in (gb_up, gb_down, gb_out, gg_mlp, gs_mlp):
        at = add_vector(sums, at, partial[...])

    for kind, ref in enumerate((qkv_out, att_out, mix_out, enc_out)):
        pltpu.make_async_copy(ref, ref, window_sems.at[kind]).wait()


FIRST_IN_ATTEND = (1, 3, 6, 9, 11, 13, 15)
FIRST_IN_PROJECT = (1, 4, 8, 12)
SECOND_IN_PROJECT = (0, 2, 5, 9, 13)


def backward_kernel(
    orders, fields, slots, width,
    counts, starts, qkv, probs, mix, att, x_in, sums_a, w_qkv, gain_attn, shift_attn,
    d_in, packed, out_a, out_b,
    mask_v, gb_qkv, total_a, total_b, load_sem, store_sems,
    sent_a, got_a, summed_a, send_a, recv_a, sent_b, got_b, summed_b, send_b, recv_b,
):
    first = Reducer(orders, total_a.shape[0], total_a, sent_a, got_a, summed_a, send_a, recv_a)
    second = Reducer(orders, total_b.shape[0], total_b, sent_b, got_b, summed_b, send_b, recv_b)
    load = pltpu.make_async_copy(sums_a, total_a, load_sem)
    load.start()
    first.greet()
    fill_mask(mask_v)
    total_b[...] = jnp.zeros_like(total_b)
    gb_qkv[...] = jnp.zeros_like(gb_qkv)
    load.wait()
    steps = fields // UNROLL
    rows = UNROLL * slots

    def at_step(step, reducer, ahead, begin):
        for k, when in enumerate(ahead):

            @pl.when(step == when)
            def _(k=k):
                reducer.advance(begin + k)

    def attend(qkv_b, probs_b, mix_b, x_b, packed_b):
        step = pl.program_id(0)
        at_step(step, first, FIRST_IN_ATTEND, 0)
        grads = []
        for u in range(UNROLL):
            f = step * UNROLL + u
            head = lax.rem(starts[f], TILE)
            slot_row = lax.broadcasted_iota(jnp.int32, (slots, width), 0)
            live = (slot_row >= head) & (slot_row < head + counts[f])
            grads.append(block_heads(mix_b[u] * live.astype(f32).astype(bf16), mask_v))
        d_probs = [heads_dot(qkv_b[u, :, 2 * width :], grads[u]) for u in range(UNROLL)]
        for u in range(UNROLL):
            packed_b[u, :, 2 * width :] = heads_out(probs_b[u], grads[u]).astype(bf16)
        d_scores = []
        for u in range(UNROLL):
            weights = probs_b[u].astype(f32)
            weighted = weights * d_probs[u]
            inner = jnp.sum(weighted, axis=0, keepdims=True)
            d_scores.append((weighted - weights * inner).astype(bf16))
        for u in range(UNROLL):
            query = block_heads(qkv_b[u, :, :width], mask_v)
            packed_b[u, :, width : 2 * width] = heads_out(d_scores[u], query).astype(bf16)
        turned = [pairs_t(d_score) for d_score in d_scores]
        for u in range(UNROLL):
            d_query = heads_out_t(turned[u], qkv_b[u, :, width : 2 * width])
            packed_b[u, :, :width] = (d_query * HEAD**-0.5).astype(bf16)
        unit, _ = row_norm(x_b[...].reshape(rows, width).astype(f32))
        grad = packed_b[...].reshape(rows, 3 * width)
        add_blocks(total_b, 0, mm_tn(unit.astype(bf16), grad))
        gb_qkv[...] += fold(grad.astype(f32))

    def block(*shape):
        return pl.BlockSpec((UNROLL,) + shape, lambda i: (i, 0, 0))

    pltpu.emit_pipeline(
        attend,
        grid=(steps,),
        in_specs=[block(slots, 3 * width), block(slots, width), block(slots, width), block(slots, width)],
        out_specs=[block(slots, 3 * width)],
    )(qkv, probs, mix, x_in, packed)

    at = 3 * width * width // LANES
    add_vector(total_b, at, gb_qkv[...])
    grad_sum = jnp.sum(gb_qkv[...], axis=0, keepdims=True)
    gain = jnp.broadcast_to(row(gain_attn), (LANES, width)).T
    shift = jnp.broadcast_to(row(shift_attn), (LANES, width)).T
    gain_sum = jnp.zeros((width, LANES), f32)
    shift_sum = jnp.zeros((width, LANES), f32)
    for k in range(3 * width // LANES):
        here = pl.ds(k * width, width)
        cols = slice(k * LANES, (k + 1) * LANES)
        weight = w_qkv[:, cols].astype(f32)
        part = total_b[here, :]
        column = jnp.broadcast_to(grad_sum[:, cols], (width, LANES))
        gain_sum += weight * part
        shift_sum += weight * column
        total_b[here, :] = gain * part + shift * column
    at += 3 * width // LANES
    at = add_vector(total_b, at, gain_sum.T)
    add_vector(total_b, at, shift_sum.T)

    def project(packed_b, x_b, att_b, d_in_b):
        step = pl.program_id(0)
        at_step(step, second, SECOND_IN_PROJECT, 0)
        at_step(step, first, FIRST_IN_PROJECT, len(FIRST_IN_ATTEND))
        unit, rstd = row_norm(x_b[...].reshape(rows, width).astype(f32))
        d_normed = mm_nt(packed_b[...].reshape(rows, 3 * width), w_qkv[...])
        d_x = norm_back(d_normed * row(gain_attn), unit, rstd)
        d_x = att_b[...].reshape(rows, width).astype(f32) + d_x
        d_in_b[...] = d_x.astype(bf16).reshape(UNROLL, slots, width)

    pltpu.emit_pipeline(
        project,
        grid=(steps,),
        in_specs=[block(slots, 3 * width), block(slots, width), block(slots, width)],
        out_specs=[block(slots, width)],
    )(packed, x_in, att, d_in)

    for k in range(len(FIRST_IN_ATTEND) + len(FIRST_IN_PROJECT), first.steps):
        first.advance(k)
    store_a = pltpu.make_async_copy(summed_a, out_a, store_sems.at[0])
    store_a.start()
    for k in range(len(SECOND_IN_PROJECT), second.steps):
        second.advance(k)
    store_b = pltpu.make_async_copy(summed_b, out_b, store_sems.at[1])
    store_b.start()
    store_a.wait()
    store_b.wait()


def unblock(src, at, dst):
    rows, columns = dst.shape
    for k in range(columns // LANES):
        dst[:, k * LANES : (k + 1) * LANES] = src[pl.ds(at + k * rows, rows), :].astype(f32)


def unblock_t(src, at, dst):
    rows, columns = dst.shape
    for k in range(rows // LANES):
        part = src[pl.ds(at + k * columns, columns), :].astype(f32)
        dst[k * LANES : (k + 1) * LANES, :] = part.T


def unblock_vector(src, at, dst):
    (columns,) = dst.shape
    for k in range(columns // LANES):
        dst[k * LANES : (k + 1) * LANES] = src[pl.ds(at + k, 1), :].astype(f32).reshape(LANES)


def unpack_kernel(
    fields, slots, width, hidden,
    counts, starts, visible, d_in, enc, sums_a, sums_b,
    encoded, input_grad, w_qkv, b_query, b_value, w_out, b_out, w_up, b_up, w_down, b_down,
    gain_attn, shift_attn, gain_mlp, shift_mlp,
    qkv_v, up_v, down_v, sems,
):
    up_at, down_at, out_at, at = sum_rows(width, hidden)
    unblock(sums_a, up_at, up_v)
    copies = [pltpu.make_async_copy(up_v, w_up, sems.at[0])]
    copies[0].start()
    unblock_t(sums_a, down_at, down_v)
    copies.append(pltpu.make_async_copy(down_v, w_down, sems.at[1]))
    copies[1].start()
    unblock(sums_b, 0, qkv_v)
    copies.append(pltpu.make_async_copy(qkv_v, w_qkv, sems.at[2]))
    copies[2].start()
    unblock(sums_a, out_at, w_out)
    for ref in (b_up, b_down, b_out, gain_mlp, shift_mlp):
        unblock_vector(sums_a, at, ref)
        at += ref.shape[0] // LANES
    at = 3 * width * width // LANES
    for ref, rows in ((b_query, 2), (b_value, 1), (gain_attn, 1), (shift_attn, 1)):
        unblock_vector(sums_b, at, ref)
        at += rows * width // LANES

    def unpack(vis_blk, d_in_b, enc_b, enc_blk, grad_blk):
        step = pl.program_id(0)
        patch_row = lax.broadcasted_iota(jnp.int32, (grad_blk.shape[1], slots), 0)
        rows = lax.broadcasted_iota(jnp.int32, (slots, slots), 0)
        cols = lax.broadcasted_iota(jnp.int32, (slots, slots), 1)
        puts, shifts = [], []
        for u in range(GROUP):
            f = step * GROUP + u
            head, count = lax.rem(starts[f], TILE), counts[f]
            picks = shifted_picks(vis_blk[pl.ds(u, 1), :], head, count)
            puts.append((patch_row == picks).astype(f32).astype(bf16))
            shifts.append(((cols - rows == head) & (rows < count)).astype(f32).astype(bf16))
        for u in range(GROUP):
            grad_blk[u] = mm(puts[u], d_in_b[u]).astype(bf16)
            enc_blk[u] = mm(shifts[u], enc_b[u]).astype(bf16)

    def block(*shape):
        return pl.BlockSpec((GROUP,) + shape, lambda i: (i, 0, 0))

    pltpu.emit_pipeline(
        unpack,
        grid=(fields // GROUP,),
        in_specs=[
            pl.BlockSpec((GROUP, visible.shape[1]), lambda i: (i, 0)),
            block(slots, width),
            block(slots, width),
        ],
        out_specs=[block(*encoded.shape[1:]), block(*input_grad.shape[1:])],
    )(visible, d_in, enc, encoded, input_grad)
    for copy in copies:
        copy.wait()


def forward(sizes, args):
    (
        patches, visible, counts, upstream, w_qkv, b_query, b_value, w_out, b_out,
        w_up, b_up, w_down, b_down, gain_attn, shift_attn, gain_mlp, shift_mlp,
    ) = args
    fields, _, width = patches.shape
    slots, hidden = visible.shape[1], w_up.shape[1]
    cap = (fields * slots + ROWS - 1) // ROWS * ROWS
    tall = cap + ROWS
    vectors = (hidden + 4 * width) // LANES
    rows_a = padded_rows(sum_rows(width, hidden)[3] + vectors, sizes)
    shape = jax.ShapeDtypeStruct
    hbm = pl.BlockSpec(memory_space=pl.ANY)
    vmem = pl.BlockSpec(memory_space=pltpu.VMEM)
    smem = pl.BlockSpec(memory_space=pltpu.SMEM)
    windows = shape((fields, slots, width), bf16)
    return pl.pallas_call(
        functools.partial(forward_kernel, fields, slots, width, hidden),
        out_shape=[
            shape((fields,), jnp.int32),
            windows,
            shape((fields, slots, 3 * width), bf16),
            windows,
            windows,
            windows,
            windows,
            shape((rows_a, LANES), f32),
        ],
        in_specs=[smem, hbm, hbm, hbm] + [vmem] * 13,
        out_specs=[smem] + [hbm] * 6 + [vmem],
        scratch_shapes=[
            pltpu.VMEM((tall, width), bf16),
            pltpu.VMEM((tall, width), bf16),
            pltpu.VMEM((cap, 3 * width), bf16),
            pltpu.VMEM((tall, width), bf16),
            pltpu.VMEM((2, UNROLL, slots, width), bf16),
            pltpu.VMEM((ROWS, hidden), bf16),
            pltpu.VMEM((ROWS, hidden), bf16),
            pltpu.VMEM((4 * HEAD, 4 * HEAD), bf16),
            pltpu.VMEM((8, hidden), f32),
            pltpu.VMEM((8, width), f32),
            pltpu.VMEM((8, width), f32),
            pltpu.VMEM((8, width), f32),
            pltpu.VMEM((8, width), f32),
            pltpu.SemaphoreType.DMA((4,)),
            pltpu.SemaphoreType.DMA((2,)),
        ],
        compiler_params=pltpu.CompilerParams(vmem_limit_bytes=VMEM_BYTES),
        name="forward_rows",
    )(
        counts, patches, visible, upstream, w_qkv, b_query, b_value, w_out, b_out,
        w_up, b_up, w_down, b_down, gain_attn, shift_attn, gain_mlp, shift_mlp,
    )


def backward(sizes, counts, starts, qkv, probs, mix, att, x_rows, sums_a, w_qkv, gain, shift):
    fields, slots, width = mix.shape
    rows_b = padded_rows((3 * width * width + 5 * width) // LANES, sizes)
    shape = jax.ShapeDtypeStruct
    hbm = pl.BlockSpec(memory_space=pl.ANY)
    vmem = pl.BlockSpec(memory_space=pltpu.VMEM)
    smem = pl.BlockSpec(memory_space=pltpu.SMEM)
    return pl.pallas_call(
        functools.partial(backward_kernel, exchange_orders(sizes), fields, slots, width),
        out_shape=[
            shape(mix.shape, bf16),
            shape(qkv.shape, bf16),
            shape(sums_a.shape, bf16),
            shape((rows_b, LANES), bf16),
        ],
        in_specs=[smem, smem] + [hbm] * 6 + [vmem] * 3,
        out_specs=[hbm] * 4,
        scratch_shapes=[
            pltpu.VMEM((4 * HEAD, 4 * HEAD), bf16),
            pltpu.VMEM((8, 3 * width), f32),
            pltpu.VMEM(sums_a.shape, f32),
            pltpu.VMEM((rows_b, LANES), f32),
            pltpu.SemaphoreType.DMA,
            pltpu.SemaphoreType.DMA((2,)),
        ]
        + reducer_scratch(sums_a.shape[0], sizes)
        + reducer_scratch(rows_b, sizes),
        compiler_params=pltpu.CompilerParams(
            collective_id=0, has_side_effects=True, vmem_limit_bytes=VMEM_BYTES
        ),
        name="backward_rows",
    )(counts, starts, qkv, probs, mix, att, x_rows, sums_a, w_qkv, gain, shift)


def unpack_all(counts, starts, visible, d_in, enc, sums_a, sums_b, patch_rows, hidden):
    fields, slots, width = d_in.shape
    shape = jax.ShapeDtypeStruct
    hbm = pl.BlockSpec(memory_space=pl.ANY)
    vmem = pl.BlockSpec(memory_space=pltpu.VMEM)
    smem = pl.BlockSpec(memory_space=pltpu.SMEM)
    vector = shape((width,), f32)
    return pl.pallas_call(
        functools.partial(unpack_kernel, fields, slots, width, hidden),
        out_shape=[
            shape((fields, slots, width), bf16),
            shape((fields, patch_rows, width), bf16),
            shape((width, 3 * width), f32), vector, vector,
            shape((width, width), f32), vector,
            shape((width, hidden), f32), shape((hidden,), f32),
            shape((hidden, width), f32), vector,
            vector, vector, vector, vector,
        ],
        in_specs=[smem, smem] + [hbm] * 3 + [vmem] * 2,
        out_specs=[hbm] * 3 + [vmem] * 4 + [hbm, vmem, hbm] + [vmem] * 5,
        scratch_shapes=[
            pltpu.VMEM((width, 3 * width), f32),
            pltpu.VMEM((width, hidden), f32),
            pltpu.VMEM((hidden, width), f32),
            pltpu.SemaphoreType.DMA((3,)),
        ],
        compiler_params=pltpu.CompilerParams(vmem_limit_bytes=VMEM_BYTES),
        name="unpack_rows",
    )(counts, starts, visible, d_in, enc, sums_a, sums_b)


def per_device(sizes, *args):
    patches, visible, counts = args[:3]
    w_qkv, w_up, gain_attn, shift_attn = args[4], args[9], args[13], args[14]
    starts, x_rows, qkv, probs, att, mix, enc, sums_a = forward(sizes, args)
    d_in, _, total_a, total_b = backward(
        sizes, counts, starts, qkv, probs, mix, att, x_rows, sums_a, w_qkv, gain_attn, shift_attn
    )
    return tuple(
        unpack_all(
            counts, starts, visible, d_in, enc, total_a, total_b, patches.shape[1], w_up.shape[1]
        )
    )


def solution(mesh):
    rows = P(("wide", "narrow"))
    return jax.shard_map(
        functools.partial(per_device, dict(mesh.shape)),
        mesh=mesh,
        in_specs=(rows,) * 4 + (P(),) * 13,
        out_specs=(rows,) * 2 + (P(),) * 13,
        check_vma=False,
    )
```

time: 278 us -> 233 us (0.84)
  local copies, waits for them, and re-layouts: 26.8 us -> 1.47 us
  Pallas kernels: 242 us -> 228 us
  other arithmetic: 6.12 us -> 0 us
    pallas_call x3, Pallas kernels: 242 us -> 228 us  [the longest x1 113 us: forward(): pl.pallas_call(functools.partial(forward_kernel, fields, slots, width, hi...]
    broadcast_in_dim x9 -> x0, local copies, waits for them, and re-layouts: 9.42 us -> none  [the longest x8 9.42 us: local_block(): row = lambda v: v[None, :]]
    slice x7 -> x0, local copies, waits for them, and re-layouts: 5.5 us -> none  [the longest x3 4.28 us: unblock(): part = blocked[at:at + rows * columns // LANES].astype(f32)]
    unnamed x6 -> x1, local copies, waits for them, and re-layouts: 5.75 us -> 1.47 us
    reshape x3 -> x0, local copies, waits for them, and re-layouts: 3.5 us -> none  [unblock(): part.reshape(columns // LANES, rows, LANES).transpose(1, 0, 2)]
where the time goes in v3:
time: 233 us; the launch traced here: 231 us
  Pallas kernels  228 us (98%)
    pallas_call x1, Pallas kernels, forward(): pl.pallas_call(functools.partial(forward_kernel, fields, slots, width, hi...  113 us
    pallas_call x1, Pallas kernels, backward(): pl.pallas_call(functools.partial(backward_kernel, exchange_orders(sizes),...  92.8 us
    pallas_call x1, Pallas kernels, unpack_all(): pl.pallas_call(functools.partial(unpack_kernel, fields, slots, width, hid...  22.7 us

profile of v3, /device:TPU:0, one launch (start us, length us, event | category | flops | bytes accessed | tf_op | source)
XLA Modules:
  0.0 230.8 jit_solution(12034555470566267549)
XLA Ops:
  0.6 1.5 copy.32.visible
  2.1 113.0 %forward_rows.1 = (s32[128]{0:T(128)}, bf16[128,64,384]{2,1,0:T(8,128)(2,1)}, bf16[128,64,1152]{2,1,0:T(8,128)(2,1)}, bf16[128,64,384]{2,1,0:T(8,128)(2,1)}, bf1...) custom-call(s32[128]{0:T(128)} %counts.5, ...), custom_call_target="tpu_custom_call" | custom-call | tf_op jit(solution)/shard_map/forward_rows/pallas_call | solution.py:671
  115.1 92.8 %backward_rows.1 = (bf16[128,64,384]{2,1,0:T(8,128)(2,1)}, bf16[128,64,1152]{2,1,0:T(8,128)(2,1)}, bf16[10752,128]{1,0:T(8,128)(2,1)}, bf16[3584,128]{1,0:T(8,128)(2,1)}) custom-call(s32[128]{0:T(128)} %counts.5, s32[128]{0:T(128)} %get-tuple-element.26.starts, bf16[128,64,1152]{2,1,0:T(8,128)(2,1)} %get-tuple-element.27.qkv, ...), custom_call_target="tpu_custom_call" | custom-call | tf_op jit(solution)/shard_map/backward_rows/pallas_call | solution.py:717
  207.9 22.7 %unpack_rows.1 = (bf16[128,64,384]{2,1,0:T(8,128)(2,1)}, bf16[128,128,384]{2,1,0:T(8,128)(2,1)}, f32[384,1152]{1,0:T(8,128)}, f32[384]{0:T(512)}, f32[384]{0:T(5...) custom-call(s32[128]{0:T(128)} %counts.5, ...), custom_call_target="tpu_custom_call" | custom-call | tf_op jit(solution)/shard_map/unpack_rows/pallas_call | solution.py:751

commit v4 on v3

--- a/solution.py
+++ b/solution.py
@@ -13,7 +13,11 @@
 ROWS = 512
 TILE = 16
 UNROLL = 8
+AHEAD = 16
 GROUP = 8
+BATCH = 16
+PART = 256
+SPLIT = 2
 CHUNK = 256
 VMEM_BYTES = 60 * 1024 * 1024
 f32 = jnp.float32
@@ -179,24 +183,27 @@
         self.send_sems, self.recv_sems = send_sems, recv_sems
         self.stages = len(orders[0])
         self.parts = rows_of_parts(rows, orders)
+        self.partners = {pair: partner(*pair) for pair in orders[0]}
+        self.bases = []
+        for order, (base, share) in zip(orders, self.parts):
+            bases = [base]
+            for k, pair in enumerate(order):
+                bases.append(bases[-1] + self.partners[pair][0] * (share >> (k + 1)))
+            self.bases.append(bases)
 
     def greet(self):
         barrier = pltpu.get_barrier_semaphore()
         for axis, distance in self.orders[0]:
-            _, other = partner(axis, distance)
+            _, other = self.partners[axis, distance]
             pl.semaphore_signal(barrier, inc=1, device_id=other, device_id_type=pl.DeviceIdType.MESH)
         pl.semaphore_wait(barrier, self.stages)
 
     def segment(self, part, stage):
-        base, share = self.parts[part]
-        for k in range(stage):
-            side, _ = partner(*self.orders[part][k])
-            base = base + side * (share >> (k + 1))
-        return base, share >> stage
+        return self.bases[part][stage], self.parts[part][1] >> stage
 
     def copy(self, part, stage, src, dst):
         axis, distance = self.orders[part][stage if stage < self.stages else 2 * self.stages - 1 - stage]
-        _, other = partner(axis, distance)
+        _, other = self.partners[axis, distance]
         return pltpu.make_async_remote_copy(
             src_ref=src, dst_ref=dst,
             send_sem=self.send_sems.at[part, stage], recv_sem=self.recv_sems.at[part, stage],
@@ -219,7 +226,7 @@
     def leave(self, part, stage):
         if stage < self.stages:
             base, size = self.segment(part, stage)
-            side, _ = partner(*self.orders[part][stage])
+            side, _ = self.partners[self.orders[part][stage]]
             half = size // 2
             away = pl.ds(pl.multiple_of(base + (1 - side) * half, TILE), half)
             self.sent[self.slot(part, stage), :] = self.total[away, :].astype(bf16)
@@ -275,11 +282,38 @@
     counts, patches, visible, upstream,
     w_qkv, b_query, b_value, w_out, b_out, w_up, b_up, w_down, b_down,
     gain_attn, shift_attn, gain_mlp, shift_mlp,
-    starts, x_out, qkv_out, probs_out, att_out, mix_out, enc_out, sums,
+    starts, x_out, unit_out, qkv_out, probs_out, att_out, mix_out, base_out, act_out, sums,
     x_v, g_v, qkv_v, mix_v, probs_v, act_v, dup_v, mask_v,
-    gb_up, gb_down, gb_out, gg_mlp, gs_mlp, window_sems, probs_sems,
+    gb_up, gb_down, gb_out, gg_mlp, gs_mlp, window_sems, probs_sems, land_sems,
+    act_sems, base_sems,
 ):
     up_at, down_at, out_at, vector_at = sum_rows(width, hidden)
+    patch_rows = patches.shape[0] // fields
+    steps = fields // BATCH
+    landing = qkv_v.shape[0] // (BATCH * patch_rows)
+    cut = [slice(k * width, (k + 1) * width) for k in range(3)]
+
+    def arrivals(third, step):
+        size = BATCH * patch_rows
+        src = pl.ds(pl.multiple_of(step * size, size), size)
+        dst = pl.ds(pl.multiple_of((step - third * landing) * size, size), size)
+        size = BATCH * slots
+        up = pl.ds(pl.multiple_of(step * size, size), size)
+        return (
+            pltpu.make_async_copy(patches.at[src], qkv_v.at[dst, cut[third]], land_sems.at[0, step]),
+            pltpu.make_async_copy(upstream.at[up], qkv_v.at[up, cut[2]], land_sems.at[1, step]),
+        )
+
+    def start_arrivals(third, step, carry):
+        for copy in arrivals(third, step):
+            copy.start()
+        return carry
+
+    for third in range(steps // landing):
+        lax.fori_loop(
+            third * landing, (third + 1) * landing, functools.partial(start_arrivals, third), 0
+        )
+
     def place(f, at):
         count = counts[f]
         head = lax.rem(at, TILE)
@@ -300,36 +334,35 @@
         head = lax.rem(start, TILE)
         return pl.multiple_of(start - head, TILE), head, counts[f]
 
-    def pack(patch_blk, vis_blk, up_blk, x_blk):
-        step = pl.program_id(0)
-        patch_row = lax.broadcasted_iota(jnp.int32, (patch_blk.shape[1], slots), 0)
+    def pack(third, step, carry):
+        for copy in arrivals(third, step):
+            copy.wait()
+        patch_row = lax.broadcasted_iota(jnp.int32, (patch_rows, slots), 0)
         rows = lax.broadcasted_iota(jnp.int32, (slots, slots), 0)
         cols = lax.broadcasted_iota(jnp.int32, (slots, slots), 1)
-        places = [where_is(step * GROUP + u) for u in range(GROUP)]
+        places = [where_is(step * BATCH + u) for u in range(BATCH)]
         takes, shifts = [], []
         for u, (base, head, count) in enumerate(places):
-            picks = shifted_picks(vis_blk[pl.ds(u, 1), :], head, count)
+            picks = shifted_picks(visible[pl.ds(step * BATCH + u, 1), :], head, count)
             takes.append((patch_row == picks).astype(f32).astype(bf16))
             shifts.append(((rows - cols == head) & (cols < count)).astype(f32).astype(bf16))
         takes = [take.T for take in takes]
-        x_wins = [mm(takes[u], patch_blk[u]).astype(bf16) for u in range(GROUP)]
-        g_wins = [mm(shifts[u], up_blk[u]).astype(bf16) for u in range(GROUP)]
-        for u, x_win in enumerate(x_wins):
-            x_blk[u] = x_win
+        x_wins, g_wins = [], []
+        for u in range(BATCH):
+            at = (step - third * landing) * BATCH + u
+            field = qkv_v[pl.ds(pl.multiple_of(at * patch_rows, patch_rows), patch_rows), cut[third]]
+            x_wins.append(mm(takes[u], field).astype(bf16))
+        for u in range(BATCH):
+            at = step * BATCH + u
+            field = qkv_v[pl.ds(pl.multiple_of(at * slots, slots), slots), cut[2]]
+            g_wins.append(mm(shifts[u], field).astype(bf16))
         for (base, head, _), x_win, g_win in zip(places, x_wins, g_wins):
             merge_store(x_v, base, head, x_win)
             merge_store(g_v, base, head, g_win)
-
-    pltpu.emit_pipeline(
-        pack,
-        grid=(fields // GROUP,),
-        in_specs=[
-            pl.BlockSpec((GROUP,) + patches.shape[1:], lambda i: (i, 0, 0)),
-            pl.BlockSpec((GROUP, visible.shape[1]), lambda i: (i, 0)),
-            pl.BlockSpec((GROUP,) + upstream.shape[1:], lambda i: (i, 0, 0)),
-        ],
-        out_specs=[pl.BlockSpec((GROUP, slots, width), lambda i: (i, 0, 0))],
-    )(patches, visible, upstream, x_out)
+        return carry
+
+    for third in range(steps // landing):
+        lax.fori_loop(third * landing, (third + 1) * landing, functools.partial(pack, third), 0)
     x_v[pl.ds(tail, ROWS), :] = jnp.zeros((ROWS, width), bf16)
     g_v[pl.ds(tail, ROWS), :] = jnp.zeros((ROWS, width), bf16)
 
@@ -337,23 +370,34 @@
         base, _, _ = where_is(f)
         return pltpu.make_async_copy(src.at[pl.ds(base, slots)], dst.at[f], window_sems.at[kind])
 
-    def project(i, carry):
+    def finished(i, f):
+        base, _, _ = where_is(jnp.minimum(f, fields - 1))
+        return (f < fields) & (base + slots <= (i + 1) * ROWS)
+
+    def project(i, sent):
         rows = pl.ds(pl.multiple_of(i * ROWS, ROWS), ROWS)
         unit, _ = row_norm(x_v[rows, :].astype(f32))
+        mix_v[rows, :] = unit.astype(bf16)
         normed = (unit * row(gain_attn) + row(shift_attn)).astype(bf16)
-        third = [slice(k * width, (k + 1) * width) for k in range(3)]
-        query = mm(normed, w_qkv[:, third[0]]) + row(b_query)
-        qkv_v[rows, third[0]] = (query * HEAD**-0.5).astype(bf16)
-        qkv_v[rows, third[1]] = mm(normed, w_qkv[:, third[1]]).astype(bf16)
-        qkv_v[rows, third[2]] = (mm(normed, w_qkv[:, third[2]]) + row(b_value)).astype(bf16)
-        return carry
+        query = mm(normed, w_qkv[:, cut[0]]) + row(b_query)
+        qkv_v[rows, cut[0]] = (query * HEAD**-0.5).astype(bf16)
+        qkv_v[rows, cut[1]] = mm(normed, w_qkv[:, cut[1]]).astype(bf16)
+        qkv_v[rows, cut[2]] = (mm(normed, w_qkv[:, cut[2]]) + row(b_value)).astype(bf16)
+
+        def send(f):
+            window_copy(f, mix_v, unit_out, 4).start()
+            window_copy(f, x_v, x_out, 5).start()
+            return f + 1
+
+        return lax.while_loop(functools.partial(finished, i), send, sent)
 
     lax.fori_loop(0, blocks, project, 0)
+    pltpu.make_async_copy(unit_out, unit_out, window_sems.at[4]).wait()
 
     def probs_copy(i):
         slot = lax.rem(i, 2)
         return pltpu.make_async_copy(
-            probs_v.at[slot], probs_out.at[pl.ds(i * UNROLL, UNROLL)], probs_sems.at[slot]
+            probs_v.at[slot], probs_out.at[pl.ds(i * AHEAD, AHEAD)], probs_sems.at[slot]
         )
 
     def attend(i, carry):
@@ -363,9 +407,9 @@
         def _():
             probs_copy(i - 2).wait()
 
-        for u in range(UNROLL):
-            window_copy(i * UNROLL + u, qkv_v, qkv_out, 0).start()
-        places = [where_is(i * UNROLL + u) for u in range(UNROLL)]
+        for u in range(AHEAD):
+            window_copy(i * AHEAD + u, qkv_v, qkv_out, 0).start()
+        places = [where_is(i * AHEAD + u) for u in range(AHEAD)]
         windows = [pl.ds(base, slots) for base, _, _ in places]
         scores = []
         for window in windows:
@@ -391,14 +435,29 @@
         probs_copy(i).start()
         return carry
 
-    steps = fields // UNROLL
+    steps = fields // AHEAD
     lax.fori_loop(0, steps, attend, 0)
     probs_copy(steps - 2).wait()
     probs_copy(steps - 1).wait()
     mix_v[pl.ds(tail, ROWS), :] = jnp.zeros((ROWS, width), bf16)
 
+    def act_copy(i):
+        rows = pl.ds(pl.multiple_of(i * ROWS, ROWS), ROWS)
+        slot = lax.rem(i, 2)
+        return pltpu.make_async_copy(act_v.at[slot], act_out.at[rows], act_sems.at[slot])
+
+    def base_copy(i):
+        rows = pl.ds(pl.multiple_of(i * ROWS, ROWS), ROWS)
+        return pltpu.make_async_copy(x_v.at[rows], base_out.at[rows], base_sems.at[i])
+
     def feed(i, sent):
         rows = pl.ds(pl.multiple_of(i * ROWS, ROWS), ROWS)
+        slot = lax.rem(i, 2)
+
+        @pl.when(i >= 2)
+        def _():
+            act_copy(i - 2).wait()
+
         mixed = mix_v[rows, :]
         grad_b = g_v[rows, :]
         grad = grad_b.astype(f32)
@@ -413,15 +472,16 @@
             d_act = mm_nt(grad_b, w_down[cols, :])
             cdf = 0.5 + 0.5 * lax.erf(up * 0.7071067811865476)
             pdf = 0.3989422804014327 * jnp.exp(-0.5 * up * up)
-            act_v[:, cols] = (up * cdf).astype(bf16)
+            act_v[slot, :, cols] = (up * cdf).astype(bf16)
             d_up = d_act * (cdf + up * pdf)
             dup_v[:, cols] = d_up.astype(bf16)
             gb_up[:, cols] += fold(d_up)
-        down = mm(act_v[...], w_down[...])
+        act_copy(i).start()
         d_normed = mm_nt(dup_v[...], w_up[...])
         add_blocks(sums, up_at, mm(normed_t, dup_v[...]))
-        add_blocks(sums, down_at, mm(grad_t, act_v[...]))
-        x_v[rows, :] = (residual + down + row(b_down)).astype(bf16)
+        add_blocks(sums, down_at, mm(grad_t, act_v[slot]))
+        x_v[rows, :] = (residual + row(b_down)).astype(bf16)
+        base_copy(i).start()
         gb_down[...] += fold(grad)
         gg_mlp[...] += fold(d_normed * unit)
         gs_mlp[...] += fold(d_normed)
@@ -432,50 +492,49 @@
         g_v[rows, :] = d_att
         mix_v[rows, :] = mm_nt(d_att, w_out[...]).astype(bf16)
 
-        def finished(f):
-            base, _, _ = where_is(jnp.minimum(f, fields - 1))
-            return (f < fields) & (base + slots <= (i + 1) * ROWS)
-
         def send(f):
             window_copy(f, g_v, att_out, 1).start()
             window_copy(f, mix_v, mix_out, 2).start()
-            window_copy(f, x_v, enc_out, 3).start()
             return f + 1
 
-        return lax.while_loop(finished, send, sent)
-
+        return lax.while_loop(functools.partial(finished, i), send, sent)
+
+    pltpu.make_async_copy(x_out, x_out, window_sems.at[5]).wait()
     lax.fori_loop(0, blocks, feed, 0)
     at = vector_at
     for partial in (gb_up, gb_down, gb_out, gg_mlp, gs_mlp):
         at = add_vector(sums, at, partial[...])
 
-    for kind, ref in enumerate((qkv_out, att_out, mix_out, enc_out)):
+    lax.fori_loop(jnp.maximum(blocks - 2, 0), blocks, lambda i, c: act_copy(i).wait(), None)
+    lax.fori_loop(0, blocks, lambda i, c: base_copy(i).wait(), None)
+    for kind, ref in enumerate((qkv_out, att_out, mix_out)):
         pltpu.make_async_copy(ref, ref, window_sems.at[kind]).wait()
 
 
 FIRST_IN_ATTEND = (1, 3, 6, 9, 11, 13, 15)
-FIRST_IN_PROJECT = (1, 4, 8, 12)
-SECOND_IN_PROJECT = (0, 2, 5, 9, 13)
+FIRST_IN_PROJECT = (2, 6, 10, 14)
+SECOND_IN_PROJECT = (0, 2, 4, 6, 8, 10, 12, 14)
 
 
 def backward_kernel(
     orders, fields, slots, width,
-    counts, starts, qkv, probs, mix, att, x_in, sums_a, w_qkv, gain_attn, shift_attn,
-    d_in, packed, out_a, out_b,
-    mask_v, gb_qkv, total_a, total_b, load_sem, store_sems,
+    counts, starts, qkv, probs, mix, unit, att, x_in, base, act, sums_a,
+    w_qkv, gain_attn, shift_attn, w_down,
+    d_in, enc, out_a, out_b,
+    packed_v, mask_v, gb_qkv, total_a, total_b, load_sem, store_sems,
     sent_a, got_a, summed_a, send_a, recv_a, sent_b, got_b, summed_b, send_b, recv_b,
 ):
     first = Reducer(orders, total_a.shape[0], total_a, sent_a, got_a, summed_a, send_a, recv_a)
     second = Reducer(orders, total_b.shape[0], total_b, sent_b, got_b, summed_b, send_b, recv_b)
     load = pltpu.make_async_copy(sums_a, total_a, load_sem)
     load.start()
+    steps = fields // UNROLL
+    rows = UNROLL * slots
+
     first.greet()
     fill_mask(mask_v)
     total_b[...] = jnp.zeros_like(total_b)
     gb_qkv[...] = jnp.zeros_like(gb_qkv)
-    load.wait()
-    steps = fields // UNROLL
-    rows = UNROLL * slots
 
     def at_step(step, reducer, ahead, begin):
         for k, when in enumerate(ahead):
@@ -484,8 +543,19 @@
             def _(k=k):
                 reducer.advance(begin + k)
 
-    def attend(qkv_b, probs_b, mix_b, x_b, packed_b):
+    def field_rows(step, u):
+        return pl.ds(pl.multiple_of((step * UNROLL + u) * slots, slots), slots)
+
+    def here(step):
+        return pl.ds(pl.multiple_of(step * rows, rows), rows)
+
+    def attend(qkv_b, probs_b, mix_b, unit_b):
         step = pl.program_id(0)
+
+        @pl.when(step == FIRST_IN_ATTEND[0])
+        def _():
+            load.wait()
+
         at_step(step, first, FIRST_IN_ATTEND, 0)
         grads = []
         for u in range(UNROLL):
@@ -496,7 +566,7 @@
             grads.append(block_heads(mix_b[u] * live.astype(f32).astype(bf16), mask_v))
         d_probs = [heads_dot(qkv_b[u, :, 2 * width :], grads[u]) for u in range(UNROLL)]
         for u in range(UNROLL):
-            packed_b[u, :, 2 * width :] = heads_out(probs_b[u], grads[u]).astype(bf16)
+            packed_v[field_rows(step, u), 2 * width :] = heads_out(probs_b[u], grads[u]).astype(bf16)
         d_scores = []
         for u in range(UNROLL):
             weights = probs_b[u].astype(f32)
@@ -505,14 +575,13 @@
             d_scores.append((weighted - weights * inner).astype(bf16))
         for u in range(UNROLL):
             query = block_heads(qkv_b[u, :, :width], mask_v)
-            packed_b[u, :, width : 2 * width] = heads_out(d_scores[u], query).astype(bf16)
+            packed_v[field_rows(step, u), width : 2 * width] = heads_out(d_scores[u], query).astype(bf16)
         turned = [pairs_t(d_score) for d_score in d_scores]
         for u in range(UNROLL):
             d_query = heads_out_t(turned[u], qkv_b[u, :, width : 2 * width])
-            packed_b[u, :, :width] = (d_query * HEAD**-0.5).astype(bf16)
-        unit, _ = row_norm(x_b[...].reshape(rows, width).astype(f32))
-        grad = packed_b[...].reshape(rows, 3 * width)
-        add_blocks(total_b, 0, mm_tn(unit.astype(bf16), grad))
+            packed_v[field_rows(step, u), :width] = (d_query * HEAD**-0.5).astype(bf16)
+        grad = packed_v[here(step), :]
+        add_blocks(total_b, 0, mm_tn(unit_b[...].reshape(rows, width), grad))
         gb_qkv[...] += fold(grad.astype(f32))
 
     def block(*shape):
@@ -521,9 +590,8 @@
     pltpu.emit_pipeline(
         attend,
         grid=(steps,),
-        in_specs=[block(slots, 3 * width), block(slots, width), block(slots, width), block(slots, width)],
-        out_specs=[block(slots, 3 * width)],
-    )(qkv, probs, mix, x_in, packed)
+        in_specs=[block(slots, 3 * width)] + [block(slots, width)] * 3,
+    )(qkv, probs, mix, unit)
 
     at = 3 * width * width // LANES
     add_vector(total_b, at, gb_qkv[...])
@@ -533,34 +601,48 @@
     gain_sum = jnp.zeros((width, LANES), f32)
     shift_sum = jnp.zeros((width, LANES), f32)
     for k in range(3 * width // LANES):
-        here = pl.ds(k * width, width)
+        at_rows = pl.ds(k * width, width)
         cols = slice(k * LANES, (k + 1) * LANES)
         weight = w_qkv[:, cols].astype(f32)
-        part = total_b[here, :]
+        part = total_b[at_rows, :]
         column = jnp.broadcast_to(grad_sum[:, cols], (width, LANES))
         gain_sum += weight * part
         shift_sum += weight * column
-        total_b[here, :] = gain * part + shift * column
+        total_b[at_rows, :] = gain * part + shift * column
     at += 3 * width // LANES
     at = add_vector(total_b, at, gain_sum.T)
     add_vector(total_b, at, shift_sum.T)
 
-    def project(packed_b, x_b, att_b, d_in_b):
+    less = PART // SPLIT
+
+    def project(x_b, att_b, act_b, base_b, d_in_b, enc_b):
         step = pl.program_id(0)
         at_step(step, second, SECOND_IN_PROJECT, 0)
         at_step(step, first, FIRST_IN_PROJECT, len(FIRST_IN_ATTEND))
-        unit, rstd = row_norm(x_b[...].reshape(rows, width).astype(f32))
-        d_normed = mm_nt(packed_b[...].reshape(rows, 3 * width), w_qkv[...])
-        d_x = norm_back(d_normed * row(gain_attn), unit, rstd)
-        d_x = att_b[...].reshape(rows, width).astype(f32) + d_x
-        d_in_b[...] = d_x.astype(bf16).reshape(UNROLL, slots, width)
-
+        grads, downs = {}, {}
+        for k in range(rows // PART + 1):
+            if k < rows // PART:
+                at = pl.multiple_of(step * rows + k * PART, PART)
+                grads[k] = mm_nt(packed_v[pl.ds(at, PART), :], w_qkv[...])
+                downs[k] = mm(act_b[k * less : (k + 1) * less, :], w_down[...])
+            if k:
+                part = pl.ds((k - 1) * PART, PART)
+                unit, rstd = row_norm(x_b[part, :].astype(f32))
+                d_x = norm_back(grads.pop(k - 1) * row(gain_attn), unit, rstd)
+                d_in_b[part, :] = (att_b[part, :].astype(f32) + d_x).astype(bf16)
+                part = pl.ds((k - 1) * less, less)
+                enc_b[part, :] = (base_b[part, :].astype(f32) + downs.pop(k - 1)).astype(bf16)
+
+    narrow = pl.BlockSpec((rows, width), lambda i: (i, 0))
+    short = pl.BlockSpec((rows // SPLIT, width), lambda i: (i, 0))
     pltpu.emit_pipeline(
         project,
         grid=(steps,),
-        in_specs=[block(slots, 3 * width), block(slots, width), block(slots, width)],
-        out_specs=[block(slots, width)],
-    )(packed, x_in, att, d_in)
+        in_specs=[
+            narrow, narrow, pl.BlockSpec((rows // SPLIT, act.shape[1]), lambda i: (i, 0)), short,
+        ],
+        out_specs=[narrow, short],
+    )(x_in, att, act, base, d_in, enc)
 
     for k in range(len(FIRST_IN_ATTEND) + len(FIRST_IN_PROJECT), first.steps):
         first.advance(k)
@@ -595,20 +677,113 @@
 
 def unpack_kernel(
     fields, slots, width, hidden,
-    counts, starts, visible, d_in, enc, sums_a, sums_b,
+    counts, starts, visible, d_in, enc, base, act, w_down_in, sums_a, sums_b,
     encoded, input_grad, w_qkv, b_query, b_value, w_out, b_out, w_up, b_up, w_down, b_down,
     gain_attn, shift_attn, gain_mlp, shift_mlp,
-    qkv_v, up_v, down_v, sems,
+    d_in_v, enc_v, out_v, grad_v, act_v, qkv_v, up_v, down_v, sems, weight_sems,
 ):
     up_at, down_at, out_at, at = sum_rows(width, hidden)
+    steps = fields // GROUP
+
+    def group(step):
+        return pl.ds(step * GROUP, GROUP)
+
+    def enc_load(src, step):
+        rows = pl.ds(pl.multiple_of(step * GROUP * slots, GROUP * slots), GROUP * slots)
+        return pltpu.make_async_copy(src.at[rows], enc_v.at[rows], sems.at[1, step])
+
+    early = enc.shape[0] // (GROUP * slots)
+
+    def act_load(step):
+        size = GROUP * slots
+        src = pl.ds(pl.multiple_of(step * size, size), size)
+        dst = pl.ds(pl.multiple_of((step - early) * size, size), size)
+        return pltpu.make_async_copy(act.at[src], act_v.at[dst], sems.at[2, step])
+
+    def used(step):
+        return step * GROUP * slots < starts[fields - 1] + slots
+
+    def loads(step):
+        rows = pl.ds(pl.multiple_of(step * GROUP * slots, GROUP * slots), GROUP * slots)
+        return (
+            pltpu.make_async_copy(d_in.at[rows], d_in_v.at[rows], sems.at[0, step]),
+        )
+
+    def stores(step):
+        return (
+            pltpu.make_async_copy(out_v.at[group(step)], encoded.at[group(step)], sems.at[1, step]),
+            pltpu.make_async_copy(grad_v.at[group(step)], input_grad.at[group(step)], sems.at[0, step]),
+        )
+
+    def start_loads(step, carry):
+        for copy in loads(step):
+            copy.start()
+
+        @pl.when(step < early)
+        def _():
+            enc_load(enc, step).start()
+
+        @pl.when((step >= early) & used(step))
+        def _():
+            enc_load(base, step).start()
+            act_load(step).start()
+
+        return carry
+
+    def wait_stores(step, carry):
+        for copy in stores(step):
+            copy.wait()
+        return carry
+
+    def unpack(step, carry):
+        for copy in loads(step):
+            copy.wait()
+
+        @pl.when(step < early)
+        def _():
+            enc_load(enc, step).wait()
+
+        @pl.when((step >= early) & used(step))
+        def _():
+            enc_load(base, step).wait()
+            act_load(step).wait()
+            size = GROUP * slots
+            here = pl.ds(pl.multiple_of(step * size, size), size)
+            late = pl.ds(pl.multiple_of((step - early) * size, size), size)
+            last = enc_v[here, :].astype(f32) + mm(act_v[late, :], w_down_in[...])
+            enc_v[here, :] = last.astype(bf16)
+
+        patch_row = lax.broadcasted_iota(jnp.int32, (input_grad.shape[1], slots), 0)
+        rows = lax.broadcasted_iota(jnp.int32, (slots, slots), 0)
+        cols = lax.broadcasted_iota(jnp.int32, (slots, slots), 1)
+        puts, shifts = [], []
+        for u in range(GROUP):
+            f = step * GROUP + u
+            head, count = lax.rem(starts[f], TILE), counts[f]
+            picks = shifted_picks(visible[pl.ds(f, 1), :], head, count)
+            puts.append((patch_row == picks).astype(f32).astype(bf16))
+            shifts.append(((cols - rows == head) & (rows < count)).astype(f32).astype(bf16))
+        for u in range(GROUP):
+            f = step * GROUP + u
+            window = pl.ds(pl.multiple_of(f * slots, slots), slots)
+            grad_v[f] = mm(puts[u], d_in_v[window, :]).astype(bf16)
+            at = pl.multiple_of(starts[f] - lax.rem(starts[f], TILE), TILE)
+            out_v[f] = mm(shifts[u], enc_v[pl.ds(at, slots), :]).astype(bf16)
+        for copy in stores(step):
+            copy.start()
+        return carry
+
+    lax.fori_loop(0, steps, start_loads, 0)
+    lax.fori_loop(0, steps, unpack, 0)
+    copies = []
     unblock(sums_a, up_at, up_v)
-    copies = [pltpu.make_async_copy(up_v, w_up, sems.at[0])]
+    copies.append(pltpu.make_async_copy(up_v, w_up, weight_sems.at[0]))
     copies[0].start()
     unblock_t(sums_a, down_at, down_v)
-    copies.append(pltpu.make_async_copy(down_v, w_down, sems.at[1]))
+    copies.append(pltpu.make_async_copy(down_v, w_down, weight_sems.at[1]))
     copies[1].start()
     unblock(sums_b, 0, qkv_v)
-    copies.append(pltpu.make_async_copy(qkv_v, w_qkv, sems.at[2]))
+    copies.append(pltpu.make_async_copy(qkv_v, w_qkv, weight_sems.at[2]))
     copies[2].start()
     unblock(sums_a, out_at, w_out)
     for ref in (b_up, b_down, b_out, gain_mlp, shift_mlp):
@@ -618,36 +793,7 @@
     for ref, rows in ((b_query, 2), (b_value, 1), (gain_attn, 1), (shift_attn, 1)):
         unblock_vector(sums_b, at, ref)
         at += rows * width // LANES
-
-    def unpack(vis_blk, d_in_b, enc_b, enc_blk, grad_blk):
-        step = pl.program_id(0)
-        patch_row = lax.broadcasted_iota(jnp.int32, (grad_blk.shape[1], slots), 0)
-        rows = lax.broadcasted_iota(jnp.int32, (slots, slots), 0)
-        cols = lax.broadcasted_iota(jnp.int32, (slots, slots), 1)
-        puts, shifts = [], []
-        for u in range(GROUP):
-            f = step * GROUP + u
-            head, count = lax.rem(starts[f], TILE), counts[f]
-            picks = shifted_picks(vis_blk[pl.ds(u, 1), :], head, count)
-            puts.append((patch_row == picks).astype(f32).astype(bf16))
-            shifts.append(((cols - rows == head) & (rows < count)).astype(f32).astype(bf16))
-        for u in range(GROUP):
-            grad_blk[u] = mm(puts[u], d_in_b[u]).astype(bf16)
-            enc_blk[u] = mm(shifts[u], enc_b[u]).astype(bf16)
-
-    def block(*shape):
-        return pl.BlockSpec((GROUP,) + shape, lambda i: (i, 0, 0))
-
-    pltpu.emit_pipeline(
-        unpack,
-        grid=(fields // GROUP,),
-        in_specs=[
-            pl.BlockSpec((GROUP, visible.shape[1]), lambda i: (i, 0)),
-            block(slots, width),
-            block(slots, width),
-        ],
-        out_specs=[block(*encoded.shape[1:]), block(*input_grad.shape[1:])],
-    )(visible, d_in, enc, encoded, input_grad)
+    lax.fori_loop(0, steps, wait_stores, 0)
     for copy in copies:
         copy.wait()
 
@@ -673,22 +819,24 @@
         out_shape=[
             shape((fields,), jnp.int32),
             windows,
+            windows,
             shape((fields, slots, 3 * width), bf16),
             windows,
             windows,
             windows,
-            windows,
+            shape((cap, width), bf16),
+            shape((cap, hidden), bf16),
             shape((rows_a, LANES), f32),
         ],
-        in_specs=[smem, hbm, hbm, hbm] + [vmem] * 13,
-        out_specs=[smem] + [hbm] * 6 + [vmem],
+        in_specs=[smem, hbm, vmem, hbm] + [vmem] * 13,
+        out_specs=[smem] + [hbm] * 8 + [vmem],
         scratch_shapes=[
             pltpu.VMEM((tall, width), bf16),
             pltpu.VMEM((tall, width), bf16),
             pltpu.VMEM((cap, 3 * width), bf16),
             pltpu.VMEM((tall, width), bf16),
-            pltpu.VMEM((2, UNROLL, slots, width), bf16),
-            pltpu.VMEM((ROWS, hidden), bf16),
+            pltpu.VMEM((2, AHEAD, slots, width), bf16),
+            pltpu.VMEM((2, ROWS, hidden), bf16),
             pltpu.VMEM((ROWS, hidden), bf16),
             pltpu.VMEM((4 * HEAD, 4 * HEAD), bf16),
             pltpu.VMEM((8, hidden), f32),
@@ -696,18 +844,24 @@
             pltpu.VMEM((8, width), f32),
             pltpu.VMEM((8, width), f32),
             pltpu.VMEM((8, width), f32),
-            pltpu.SemaphoreType.DMA((4,)),
+            pltpu.SemaphoreType.DMA((6,)),
             pltpu.SemaphoreType.DMA((2,)),
+            pltpu.SemaphoreType.DMA((2, fields // BATCH)),
+            pltpu.SemaphoreType.DMA((2,)),
+            pltpu.SemaphoreType.DMA((cap // ROWS,)),
         ],
         compiler_params=pltpu.CompilerParams(vmem_limit_bytes=VMEM_BYTES),
         name="forward_rows",
     )(
-        counts, patches, visible, upstream, w_qkv, b_query, b_value, w_out, b_out,
-        w_up, b_up, w_down, b_down, gain_attn, shift_attn, gain_mlp, shift_mlp,
+        counts, patches.reshape(-1, width), visible, upstream.reshape(-1, width),
+        w_qkv, b_query, b_value, w_out, b_out, w_up, b_up, w_down, b_down, gain_attn, shift_attn, gain_mlp, shift_mlp,
     )
 
 
-def backward(sizes, counts, starts, qkv, probs, mix, att, x_rows, sums_a, w_qkv, gain, shift):
+def backward(
+    sizes, counts, starts, qkv, probs, mix, unit, att, x_rows, base, act, sums_a,
+    w_qkv, gain, shift, w_down,
+):
     fields, slots, width = mix.shape
     rows_b = padded_rows((3 * width * width + 5 * width) // LANES, sizes)
     shape = jax.ShapeDtypeStruct
@@ -717,14 +871,15 @@
     return pl.pallas_call(
         functools.partial(backward_kernel, exchange_orders(sizes), fields, slots, width),
         out_shape=[
-            shape(mix.shape, bf16),
-            shape(qkv.shape, bf16),
+            shape((fields * slots, width), bf16),
+            shape((act.shape[0] // SPLIT, width), bf16),
             shape(sums_a.shape, bf16),
             shape((rows_b, LANES), bf16),
         ],
-        in_specs=[smem, smem] + [hbm] * 6 + [vmem] * 3,
+        in_specs=[smem, smem] + [hbm] * 9 + [vmem] * 4,
         out_specs=[hbm] * 4,
         scratch_shapes=[
+            pltpu.VMEM((fields * slots, 3 * width), bf16),
             pltpu.VMEM((4 * HEAD, 4 * HEAD), bf16),
             pltpu.VMEM((8, 3 * width), f32),
             pltpu.VMEM(sums_a.shape, f32),
@@ -738,11 +893,16 @@
             collective_id=0, has_side_effects=True, vmem_limit_bytes=VMEM_BYTES
         ),
         name="backward_rows",
-    )(counts, starts, qkv, probs, mix, att, x_rows, sums_a, w_qkv, gain, shift)
-
-
-def unpack_all(counts, starts, visible, d_in, enc, sums_a, sums_b, patch_rows, hidden):
-    fields, slots, width = d_in.shape
+    )(
+        counts, starts, qkv, probs, mix, unit, att.reshape(-1, width), x_rows.reshape(-1, width),
+        base, act, sums_a, w_qkv, gain, shift, w_down,
+    )
+
+
+def unpack_all(
+    counts, starts, visible, d_in, enc, base, act, w_down, sums_a, sums_b, patch_rows, hidden
+):
+    (fields, slots), width = visible.shape, d_in.shape[1]
     shape = jax.ShapeDtypeStruct
     hbm = pl.BlockSpec(memory_space=pl.ANY)
     vmem = pl.BlockSpec(memory_space=pltpu.VMEM)
@@ -759,29 +919,36 @@
             shape((hidden, width), f32), vector,
             vector, vector, vector, vector,
         ],
-        in_specs=[smem, smem] + [hbm] * 3 + [vmem] * 2,
+        in_specs=[smem, smem, vmem] + [hbm] * 4 + [vmem] * 3,
         out_specs=[hbm] * 3 + [vmem] * 4 + [hbm, vmem, hbm] + [vmem] * 5,
         scratch_shapes=[
+            pltpu.VMEM(d_in.shape, bf16),
+            pltpu.VMEM(base.shape, bf16),
+            pltpu.VMEM((fields, slots, width), bf16),
+            pltpu.VMEM((fields, patch_rows, width), bf16),
+            pltpu.VMEM((base.shape[0] - enc.shape[0], hidden), bf16),
             pltpu.VMEM((width, 3 * width), f32),
             pltpu.VMEM((width, hidden), f32),
             pltpu.VMEM((hidden, width), f32),
+            pltpu.SemaphoreType.DMA((3, fields // GROUP)),
             pltpu.SemaphoreType.DMA((3,)),
         ],
         compiler_params=pltpu.CompilerParams(vmem_limit_bytes=VMEM_BYTES),
         name="unpack_rows",
-    )(counts, starts, visible, d_in, enc, sums_a, sums_b)
+    )(counts, starts, visible, d_in, enc, base, act, w_down, sums_a, sums_b)
 
 
 def per_device(sizes, *args):
     patches, visible, counts = args[:3]
     w_qkv, w_up, gain_attn, shift_attn = args[4], args[9], args[13], args[14]
-    starts, x_rows, qkv, probs, att, mix, enc, sums_a = forward(sizes, args)
-    d_in, _, total_a, total_b = backward(
-        sizes, counts, starts, qkv, probs, mix, att, x_rows, sums_a, w_qkv, gain_attn, shift_attn
+    starts, x_rows, unit, qkv, probs, att, mix, base, act, sums_a = forward(sizes, args)
+    d_in, enc, total_a, total_b = backward(
+        sizes, counts, starts, qkv, probs, mix, unit, att, x_rows, base, act, sums_a,
+        w_qkv, gain_attn, shift_attn, args[11],
     )
     return tuple(
         unpack_all(
-            counts, starts, visible, d_in, enc, total_a, total_b, patches.shape[1], w_up.shape[1]
+            counts, starts, visible, d_in, enc, base, act, args[11], total_a, total_b, patches.shape[1], w_up.shape[1]
         )
     )
 

time: 233 us -> 206 us (0.88)
  Pallas kernels: 228 us -> 204 us
    pallas_call x1, Pallas kernels: 92.8 us -> 81.1 us  [backward(): pl.pallas_call(functools.partial(backward_kernel, exchange_orders(sizes),...]
    pallas_call x1, Pallas kernels: 113 us -> 102 us  [forward(): pl.pallas_call(functools.partial(forward_kernel, fields, slots, width, hi...]
    pallas_call x1, Pallas kernels: 22.7 us -> 20.2 us  [unpack_all(): pl.pallas_call(functools.partial(unpack_kernel, fields, slots, width, hid...]
where the time goes in v4:
time: 206 us
  Pallas kernels  204 us (99%)
    pallas_call x1, Pallas kernels, forward(): pl.pallas_call(functools.partial(forward_kernel, fields, slots, width, hi...  102 us
    pallas_call x1, Pallas kernels, backward(): pl.pallas_call(functools.partial(backward_kernel, exchange_orders(sizes),...  81.1 us
    pallas_call x1, Pallas kernels, unpack_all(): pl.pallas_call(functools.partial(unpack_kernel, fields, slots, width, hid...  20.2 us

profile of v4, /device:TPU:0, one launch (start us, length us, event | category | flops | bytes accessed | tf_op | source)
XLA Modules:
  0.0 206.0 jit_solution(10934755190051648620)
XLA Ops:
  0.6 1.5 copy.32.visible
  2.1 102.5 %forward_rows.1 = (s32[128]{0:T(128)}, bf16[128,64,384]{2,1,0:T(8,128)(2,1)}, bf16[128,64,384]{2,1,0:T(8,128)(2,1)}, bf16[128,64,1152]{2,1,0:T(8,128)(2,1)}, bf1...) custom-call(s32[128]{0:T(128)} %counts.5, ...), custom_call_target="tpu_custom_call" | custom-call | tf_op jit(solution)/shard_map/forward_rows/pallas_call | solution.py:817
  104.6 81.1 %backward_rows.1 = (bf16[8192,384]{1,0:T(8,128)(2,1)}, bf16[4096,384]{1,0:T(8,128)(2,1)}, bf16[10752,128]{1,0:T(8,128)(2,1)}, bf16[3584,128]{1,0:T(8,128)(2,1)}) custom-call(s32[128]{0:T(128)} %counts.5, s32[128]{0:T(128)} %get-tuple-element.29.starts, bf16[128,64,1152]{2,1,0:T(8,128)(2,1)} %get-tuple-element.30.qkv, ...), custom_call_target="tpu_custom_call" | custom-call | tf_op jit(solution)/shard_map/backward_rows/pallas_call | solution.py:871
  185.7 20.2 %unpack_rows.1 = (bf16[128,64,384]{2,1,0:T(8,128)(2,1)}, bf16[128,128,384]{2,1,0:T(8,128)(2,1)}, f32[384,1152]{1,0:T(8,128)}, f32[384]{0:T(512)}, f32[384]{0:T(5...) custom-call(s32[128]{0:T(128)} %counts.5, ...), custom_call_target="tpu_custom_call" | custom-call | tf_op jit(solution)/shard_map/unpack_rows/pallas_call | solution.py:911

commit v5 on v4

--- a/solution.py
+++ b/solution.py
@@ -12,7 +12,7 @@
 FILL = -1e30
 ROWS = 512
 TILE = 16
-UNROLL = 8
+UNROLL = 16
 AHEAD = 16
 GROUP = 8
 BATCH = 16
@@ -157,17 +157,25 @@
     wide, narrow = mesh_bits(sizes)
     first, last = narrow[:1], wide[-1:]
     middle = wide[:1] + narrow[1:] + wide[1:-1]
-    return [first + middle[k:] + middle[:k] + last for k in range(min(3, len(middle)))]
-
-
-def partner(axis, distance):
-    mine = lax.axis_index(axis)
-    side = lax.rem(mine // distance, 2)
-    return side, {axis: mine + distance * (1 - 2 * side)}
+    orders = [first + middle[k:] + middle[:k] + last for k in range(min(3, len(middle)))]
+    return [[(pair,) for pair in order] for order in orders]
+
+
+def direct_orders(sizes):
+    wide, narrow = mesh_bits(sizes)
+    plane, line = tuple(wide[:1] + narrow[1:]), tuple(wide[1:])
+    return [[tuple(narrow[:1]), plane, line], [tuple(narrow[:1]), line, plane]]
+
+
+def members(group):
+    return [
+        tuple(pair for k, pair in enumerate(group) if mask >> k & 1)
+        for mask in range(1, 1 << len(group))
+    ]
 
 
 def rows_of_parts(rows, orders):
-    unit = TILE << len(orders[0])
+    unit = TILE << sum(len(group) for group in orders[0])
     units, parts, at = rows // unit, [], 0
     for k in range(len(orders)):
         share = (units + len(orders) - 1 - k) // len(orders) * unit
@@ -183,61 +191,81 @@
         self.send_sems, self.recv_sems = send_sems, recv_sems
         self.stages = len(orders[0])
         self.parts = rows_of_parts(rows, orders)
-        self.partners = {pair: partner(*pair) for pair in orders[0]}
-        self.bases = []
-        for order, (base, share) in zip(orders, self.parts):
-            bases = [base]
-            for k, pair in enumerate(order):
-                bases.append(bases[-1] + self.partners[pair][0] * (share >> (k + 1)))
+        self.sides = {}
+        for group in orders[0]:
+            for axis, distance in group:
+                self.sides[axis, distance] = lax.rem(lax.axis_index(axis) // distance, 2)
+        self.bases, self.sizes = [], []
+        for order, (base, size) in zip(orders, self.parts):
+            bases, sizes = [base], [size]
+            for group in order:
+                sizes.append(sizes[-1] >> len(group))
+                bases.append(bases[-1] + self.place(group) * sizes[-1])
             self.bases.append(bases)
-
-    def greet(self):
+            self.sizes.append(sizes)
+
+    def place(self, group, flipped=()):
+        place = 0
+        for k, pair in enumerate(group):
+            side = self.sides[pair]
+            place = place + (1 << k) * (1 - side if pair in flipped else side)
+        return place
+
+    def device(self, flipped):
+        other = {}
+        for axis, distance in flipped:
+            mine = other.get(axis, lax.axis_index(axis))
+            other[axis] = mine + distance * (1 - 2 * self.sides[axis, distance])
+        return other
+
+    def partners(self):
+        return {flipped for order in self.orders for group in order for flipped in members(group)}
+
+    def greet(self, partners):
         barrier = pltpu.get_barrier_semaphore()
-        for axis, distance in self.orders[0]:
-            _, other = self.partners[axis, distance]
-            pl.semaphore_signal(barrier, inc=1, device_id=other, device_id_type=pl.DeviceIdType.MESH)
-        pl.semaphore_wait(barrier, self.stages)
-
-    def segment(self, part, stage):
-        return self.bases[part][stage], self.parts[part][1] >> stage
-
-    def copy(self, part, stage, src, dst):
-        axis, distance = self.orders[part][stage if stage < self.stages else 2 * self.stages - 1 - stage]
-        _, other = self.partners[axis, distance]
-        return pltpu.make_async_remote_copy(
-            src_ref=src, dst_ref=dst,
-            send_sem=self.send_sems.at[part, stage], recv_sem=self.recv_sems.at[part, stage],
-            device_id=other, device_id_type=pl.DeviceIdType.MESH,
-        )
-
-    def slot(self, part, stage):
+        for flipped in sorted(partners):
+            pl.semaphore_signal(
+                barrier, inc=1, device_id=self.device(flipped), device_id_type=pl.DeviceIdType.MESH
+            )
+        pl.semaphore_wait(barrier, len(partners))
+
+    def flights(self, part, stage):
+        summing = stage < self.stages
+        level = stage if summing else 2 * self.stages - 1 - stage
+        group = self.orders[part][level]
+        size = self.sizes[part][level + 1]
         base, share = self.parts[part]
-        return pl.ds(base + share - (share >> stage), share >> (stage + 1))
-
-    def flight(self, part, stage):
+        for k, flipped in enumerate(members(group)):
+            if summing:
+                slot = pl.ds(base + share - self.sizes[part][level] + k * size, size)
+                src, dst = self.sent.at[slot], self.got.at[slot]
+            else:
+                slot = pl.ds(pl.multiple_of(self.bases[part][level + 1], TILE), size)
+                src = dst = self.summed.at[slot]
+            copy = pltpu.make_async_remote_copy(
+                src_ref=src, dst_ref=dst,
+                send_sem=self.send_sems.at[part, stage, k], recv_sem=self.recv_sems.at[part, stage, k],
+                device_id=self.device(flipped), device_id_type=pl.DeviceIdType.MESH,
+            )
+            yield copy, flipped, slot
+
+    def leave(self, part, stage):
+        for copy, flipped, slot in self.flights(part, stage):
+            if stage < self.stages:
+                size = self.sizes[part][stage + 1]
+                at = self.bases[part][stage] + self.place(self.orders[part][stage], flipped) * size
+                self.sent[slot, :] = self.total[pl.ds(pl.multiple_of(at, TILE), size), :].astype(bf16)
+            copy.start()
+
+    def arrive(self, part, stage):
+        flights = list(self.flights(part, stage))
+        for copy, _, _ in flights:
+            copy.wait()
         if stage < self.stages:
-            slot = self.slot(part, stage)
-            return self.copy(part, stage, self.sent.at[slot], self.got.at[slot])
-        level = 2 * self.stages - stage
-        base, size = self.segment(part, level)
-        here = pl.ds(pl.multiple_of(base, TILE), size)
-        return self.copy(part, stage, self.summed.at[here], self.summed.at[here])
-
-    def leave(self, part, stage):
-        if stage < self.stages:
-            base, size = self.segment(part, stage)
-            side, _ = self.partners[self.orders[part][stage]]
-            half = size // 2
-            away = pl.ds(pl.multiple_of(base + (1 - side) * half, TILE), half)
-            self.sent[self.slot(part, stage), :] = self.total[away, :].astype(bf16)
-        self.flight(part, stage).start()
-
-    def arrive(self, part, stage):
-        self.flight(part, stage).wait()
-        if stage < self.stages:
-            base, size = self.segment(part, stage + 1)
-            here = pl.ds(pl.multiple_of(base, TILE), size)
-            value = self.total[here, :] + self.got[self.slot(part, stage), :].astype(f32)
+            here = pl.ds(pl.multiple_of(self.bases[part][stage + 1], TILE), self.sizes[part][stage + 1])
+            value = self.total[here, :]
+            for _, _, slot in flights:
+                value = value + self.got[slot, :].astype(f32)
             if stage + 1 < self.stages:
                 self.total[here, :] = value
             else:
@@ -260,9 +288,9 @@
     return (rows + unit - 1) // unit * unit
 
 
-def reducer_scratch(rows, sizes):
-    orders = exchange_orders(sizes)
-    flights = (len(orders), 2 * len(orders[0]))
+def reducer_scratch(rows, orders):
+    most = max(len(members(group)) for group in orders[0])
+    flights = (len(orders), 2 * len(orders[0]), most)
     return [
         pltpu.VMEM((rows, LANES), bf16),
         pltpu.VMEM((rows, LANES), bf16),
@@ -283,7 +311,7 @@
     w_qkv, b_query, b_value, w_out, b_out, w_up, b_up, w_down, b_down,
     gain_attn, shift_attn, gain_mlp, shift_mlp,
     starts, x_out, unit_out, qkv_out, probs_out, att_out, mix_out, base_out, act_out, sums,
-    x_v, g_v, qkv_v, mix_v, probs_v, act_v, dup_v, mask_v,
+    x_v, g_v, qkv_v, mix_v, probs_v, act_v, dup_v, mask_v, picks_v,
     gb_up, gb_down, gb_out, gg_mlp, gs_mlp, window_sems, probs_sems, land_sems,
     act_sems, base_sems,
 ):
@@ -328,6 +356,7 @@
     for ref in (sums, gb_up, gb_down, gb_out, gg_mlp, gs_mlp):
         ref[...] = jnp.zeros_like(ref)
     fill_mask(mask_v)
+    picks_v[...] = visible[...].T
 
     def where_is(f):
         start = starts[f]
@@ -343,7 +372,7 @@
         places = [where_is(step * BATCH + u) for u in range(BATCH)]
         takes, shifts = [], []
         for u, (base, head, count) in enumerate(places):
-            picks = shifted_picks(visible[pl.ds(step * BATCH + u, 1), :], head, count)
+            picks = shifted_picks(picks_v[pl.ds(step * BATCH + u, 1), :], head, count)
             takes.append((patch_row == picks).astype(f32).astype(bf16))
             shifts.append(((rows - cols == head) & (cols < count)).astype(f32).astype(bf16))
         takes = [take.T for take in takes]
@@ -511,27 +540,27 @@
         pltpu.make_async_copy(ref, ref, window_sems.at[kind]).wait()
 
 
-FIRST_IN_ATTEND = (1, 3, 6, 9, 11, 13, 15)
-FIRST_IN_PROJECT = (2, 6, 10, 14)
-SECOND_IN_PROJECT = (0, 2, 4, 6, 8, 10, 12, 14)
+FIRST_IN_ATTEND = (1, 2, 4, 5, 6, 7)
+FIRST_IN_PROJECT = (1, 2, 4, 6)
+SECOND_IN_PROJECT = (0, 1, 3, 5, 7)
 
 
 def backward_kernel(
-    orders, fields, slots, width,
+    orders_a, orders_b, fields, slots, width,
     counts, starts, qkv, probs, mix, unit, att, x_in, base, act, sums_a,
     w_qkv, gain_attn, shift_attn, w_down,
     d_in, enc, out_a, out_b,
     packed_v, mask_v, gb_qkv, total_a, total_b, load_sem, store_sems,
     sent_a, got_a, summed_a, send_a, recv_a, sent_b, got_b, summed_b, send_b, recv_b,
 ):
-    first = Reducer(orders, total_a.shape[0], total_a, sent_a, got_a, summed_a, send_a, recv_a)
-    second = Reducer(orders, total_b.shape[0], total_b, sent_b, got_b, summed_b, send_b, recv_b)
+    first = Reducer(orders_a, total_a.shape[0], total_a, sent_a, got_a, summed_a, send_a, recv_a)
+    second = Reducer(orders_b, total_b.shape[0], total_b, sent_b, got_b, summed_b, send_b, recv_b)
     load = pltpu.make_async_copy(sums_a, total_a, load_sem)
     load.start()
     steps = fields // UNROLL
     rows = UNROLL * slots
 
-    first.greet()
+    first.greet(first.partners() | second.partners())
     fill_mask(mask_v)
     total_b[...] = jnp.zeros_like(total_b)
     gb_qkv[...] = jnp.zeros_like(gb_qkv)
@@ -680,7 +709,7 @@
     counts, starts, visible, d_in, enc, base, act, w_down_in, sums_a, sums_b,
     encoded, input_grad, w_qkv, b_query, b_value, w_out, b_out, w_up, b_up, w_down, b_down,
     gain_attn, shift_attn, gain_mlp, shift_mlp,
-    d_in_v, enc_v, out_v, grad_v, act_v, qkv_v, up_v, down_v, sems, weight_sems,
+    picks_v, d_in_v, enc_v, out_v, grad_v, act_v, qkv_v, up_v, down_v, sems, weight_sems,
 ):
     up_at, down_at, out_at, at = sum_rows(width, hidden)
     steps = fields // GROUP
@@ -760,7 +789,7 @@
         for u in range(GROUP):
             f = step * GROUP + u
             head, count = lax.rem(starts[f], TILE), counts[f]
-            picks = shifted_picks(visible[pl.ds(f, 1), :], head, count)
+            picks = shifted_picks(picks_v[pl.ds(f, 1), :], head, count)
             puts.append((patch_row == picks).astype(f32).astype(bf16))
             shifts.append(((cols - rows == head) & (rows < count)).astype(f32).astype(bf16))
         for u in range(GROUP):
@@ -774,7 +803,7 @@
         return carry
 
     lax.fori_loop(0, steps, start_loads, 0)
-    lax.fori_loop(0, steps, unpack, 0)
+    picks_v[...] = visible[...].T
     copies = []
     unblock(sums_a, up_at, up_v)
     copies.append(pltpu.make_async_copy(up_v, w_up, weight_sems.at[0]))
@@ -793,6 +822,7 @@
     for ref, rows in ((b_query, 2), (b_value, 1), (gain_attn, 1), (shift_attn, 1)):
         unblock_vector(sums_b, at, ref)
         at += rows * width // LANES
+    lax.fori_loop(0, steps, unpack, 0)
     lax.fori_loop(0, steps, wait_stores, 0)
     for copy in copies:
         copy.wait()
@@ -839,6 +869,7 @@
             pltpu.VMEM((2, ROWS, hidden), bf16),
             pltpu.VMEM((ROWS, hidden), bf16),
             pltpu.VMEM((4 * HEAD, 4 * HEAD), bf16),
+            pltpu.VMEM((fields, slots), jnp.int32),
             pltpu.VMEM((8, hidden), f32),
             pltpu.VMEM((8, width), f32),
             pltpu.VMEM((8, width), f32),
@@ -853,7 +884,7 @@
         compiler_params=pltpu.CompilerParams(vmem_limit_bytes=VMEM_BYTES),
         name="forward_rows",
     )(
-        counts, patches.reshape(-1, width), visible, upstream.reshape(-1, width),
+        counts, patches.reshape(-1, width), visible.T, upstream.reshape(-1, width),
         w_qkv, b_query, b_value, w_out, b_out, w_up, b_up, w_down, b_down, gain_attn, shift_attn, gain_mlp, shift_mlp,
     )
 
@@ -863,13 +894,14 @@
     w_qkv, gain, shift, w_down,
 ):
     fields, slots, width = mix.shape
+    orders_a, orders_b = exchange_orders(sizes), direct_orders(sizes)
     rows_b = padded_rows((3 * width * width + 5 * width) // LANES, sizes)
     shape = jax.ShapeDtypeStruct
     hbm = pl.BlockSpec(memory_space=pl.ANY)
     vmem = pl.BlockSpec(memory_space=pltpu.VMEM)
     smem = pl.BlockSpec(memory_space=pltpu.SMEM)
     return pl.pallas_call(
-        functools.partial(backward_kernel, exchange_orders(sizes), fields, slots, width),
+        functools.partial(backward_kernel, orders_a, orders_b, fields, slots, width),
         out_shape=[
             shape((fields * slots, width), bf16),
             shape((act.shape[0] // SPLIT, width), bf16),
@@ -887,8 +919,8 @@
             pltpu.SemaphoreType.DMA,
             pltpu.SemaphoreType.DMA((2,)),
         ]
-        + reducer_scratch(sums_a.shape[0], sizes)
-        + reducer_scratch(rows_b, sizes),
+        + reducer_scratch(sums_a.shape[0], orders_a)
+        + reducer_scratch(rows_b, orders_b),
         compiler_params=pltpu.CompilerParams(
             collective_id=0, has_side_effects=True, vmem_limit_bytes=VMEM_BYTES
         ),
@@ -902,7 +934,7 @@
 def unpack_all(
     counts, starts, visible, d_in, enc, base, act, w_down, sums_a, sums_b, patch_rows, hidden
 ):
-    (fields, slots), width = visible.shape, d_in.shape[1]
+    (slots, fields), width = visible.shape, d_in.shape[1]
     shape = jax.ShapeDtypeStruct
     hbm = pl.BlockSpec(memory_space=pl.ANY)
     vmem = pl.BlockSpec(memory_space=pltpu.VMEM)
@@ -922,6 +954,7 @@
         in_specs=[smem, smem, vmem] + [hbm] * 4 + [vmem] * 3,
         out_specs=[hbm] * 3 + [vmem] * 4 + [hbm, vmem, hbm] + [vmem] * 5,
         scratch_shapes=[
+            pltpu.VMEM((fields, slots), jnp.int32),
             pltpu.VMEM(d_in.shape, bf16),
             pltpu.VMEM(base.shape, bf16),
             pltpu.VMEM((fields, slots, width), bf16),
@@ -948,7 +981,7 @@
     )
     return tuple(
         unpack_all(
-            counts, starts, visible, d_in, enc, base, act, args[11], total_a, total_b, patches.shape[1], w_up.shape[1]
+            counts, starts, visible.T, d_in, enc, base, act, args[11], total_a, total_b, patches.shape[1], w_up.shape[1]
         )
     )
 

time: 206 us -> 199 us (0.966)
  Pallas kernels: 204 us -> 198 us
    pallas_call x1, Pallas kernels: 102 us -> 96.3 us  [forward(): pl.pallas_call(functools.partial(forward_kernel, fields, slots, width, hi...]
where the time goes in v5:
time: 199 us; the launch traced here: 198 us
  Pallas kernels  198 us (99%)
    pallas_call x1, Pallas kernels, forward(): pl.pallas_call(functools.partial(forward_kernel, fields, slots, width, hi...  96.3 us
    pallas_call x1, Pallas kernels, backward(): pl.pallas_call(functools.partial(backward_kernel, orders_a, orders_b, fie...  82.1 us
    pallas_call x1, Pallas kernels, unpack_all(): pl.pallas_call(functools.partial(unpack_kernel, fields, slots, width, hid...  19.1 us

profile of v5, /device:TPU:0, one launch (start us, length us, event | category | flops | bytes accessed | tf_op | source)
XLA Modules:
  0.0 198.4 jit_solution(10301814081977982801)
XLA Ops:
  0.6 96.3 %forward_rows.1 = (s32[128]{0:T(128)}, bf16[128,64,384]{2,1,0:T(8,128)(2,1)}, bf16[128,64,384]{2,1,0:T(8,128)(2,1)}, bf16[128,64,1152]{2,1,0:T(8,128)(2,1)}, bf1...) custom-call(s32[128]{0:T(128)} %counts.5, ...), custom_call_target="tpu_custom_call" | custom-call | tf_op jit(solution)/shard_map/forward_rows/pallas_call | solution.py:847
  97.0 82.1 %backward_rows.1 = (bf16[8192,384]{1,0:T(8,128)(2,1)}, bf16[4096,384]{1,0:T(8,128)(2,1)}, bf16[10752,128]{1,0:T(8,128)(2,1)}, bf16[3584,128]{1,0:T(8,128)(2,1)}) custom-call(s32[128]{0:T(128)} %counts.5, s32[128]{0:T(128)} %get-tuple-element.29.starts, bf16[128,64,1152]{2,1,0:T(8,128)(2,1)} %get-tuple-element.30.qkv, ...), custom_call_target="tpu_custom_call" | custom-call | tf_op jit(solution)/shard_map/backward_rows/pallas_call | solution.py:903
  179.1 19.1 %unpack_rows.1 = (bf16[128,64,384]{2,1,0:T(8,128)(2,1)}, bf16[128,128,384]{2,1,0:T(8,128)(2,1)}, f32[384,1152]{1,0:T(8,128)}, f32[384]{0:T(512)}, f32[384]{0:T(5...) custom-call(s32[128]{0:T(128)} %counts.5, ...), custom_call_target="tpu_custom_call" | custom-call | tf_op jit(solution)/shard_map/unpack_rows/pallas_call | solution.py:943

commit v6 on v5

--- a/solution.py
+++ b/solution.py
@@ -16,6 +16,7 @@
 AHEAD = 16
 GROUP = 8
 BATCH = 16
+PIECES = 4
 PART = 256
 SPLIT = 2
 CHUNK = 256
@@ -111,6 +112,15 @@
 
 def pairs_t(values):
     return [values[:, at : at + 2 * HEAD].T for at in range(0, values.shape[1], 2 * HEAD)]
+
+
+def start_all(pairs, sems):
+    copies = [
+        pltpu.make_async_copy(src, dst, sems.at[k]) for k, (src, dst) in enumerate(pairs)
+    ]
+    for copy in copies:
+        copy.start()
+    return copies
 
 
 def add_blocks(sums, at, values):
@@ -308,12 +318,12 @@
 def forward_kernel(
     fields, slots, width, hidden,
     counts, patches, visible, upstream,
-    w_qkv, b_query, b_value, w_out, b_out, w_up, b_up, w_down, b_down,
+    w_qkv_hbm, b_query, b_value, w_out_hbm, b_out, w_up_hbm, b_up, w_down_hbm, b_down,
     gain_attn, shift_attn, gain_mlp, shift_mlp,
     starts, x_out, unit_out, qkv_out, probs_out, att_out, mix_out, base_out, act_out, sums,
     x_v, g_v, qkv_v, mix_v, probs_v, act_v, dup_v, mask_v, picks_v,
     gb_up, gb_down, gb_out, gg_mlp, gs_mlp, window_sems, probs_sems, land_sems,
-    act_sems, base_sems,
+    act_sems, base_sems, w_qkv, w_out, w_up, w_down, weight_sems,
 ):
     up_at, down_at, out_at, vector_at = sum_rows(width, hidden)
     patch_rows = patches.shape[0] // fields
@@ -341,6 +351,10 @@
         lax.fori_loop(
             third * landing, (third + 1) * landing, functools.partial(start_arrivals, third), 0
         )
+
+    weights = start_all(
+        ((w_qkv_hbm, w_qkv), (w_out_hbm, w_out), (w_up_hbm, w_up), (w_down_hbm, w_down)), weight_sems
+    )
 
     def place(f, at):
         count = counts[f]
@@ -403,14 +417,24 @@
         base, _, _ = where_is(jnp.minimum(f, fields - 1))
         return (f < fields) & (base + slots <= (i + 1) * ROWS)
 
-    def project(i, sent):
-        rows = pl.ds(pl.multiple_of(i * ROWS, ROWS), ROWS)
+    def norm(i, piece):
+        size = ROWS // PIECES
+        rows = pl.ds(pl.multiple_of(i * ROWS + piece * size, size), size)
         unit, _ = row_norm(x_v[rows, :].astype(f32))
         mix_v[rows, :] = unit.astype(bf16)
         normed = (unit * row(gain_attn) + row(shift_attn)).astype(bf16)
+        act_v[lax.rem(i, 2), piece * size : (piece + 1) * size, 0:width] = normed
+
+    def project(i, sent):
+        rows = pl.ds(pl.multiple_of(i * ROWS, ROWS), ROWS)
+        normed = act_v[lax.rem(i, 2), :, 0:width]
         query = mm(normed, w_qkv[:, cut[0]]) + row(b_query)
         qkv_v[rows, cut[0]] = (query * HEAD**-0.5).astype(bf16)
+        norm(i + 1, 0)
+        norm(i + 1, 1)
         qkv_v[rows, cut[1]] = mm(normed, w_qkv[:, cut[1]]).astype(bf16)
+        norm(i + 1, 2)
+        norm(i + 1, 3)
         qkv_v[rows, cut[2]] = (mm(normed, w_qkv[:, cut[2]]) + row(b_value)).astype(bf16)
 
         def send(f):
@@ -420,6 +444,10 @@
 
         return lax.while_loop(functools.partial(finished, i), send, sent)
 
+    for copy in weights:
+        copy.wait()
+    for piece in range(PIECES):
+        norm(0, piece)
     lax.fori_loop(0, blocks, project, 0)
     pltpu.make_async_copy(unit_out, unit_out, window_sems.at[4]).wait()
 
@@ -548,15 +576,16 @@
 def backward_kernel(
     orders_a, orders_b, fields, slots, width,
     counts, starts, qkv, probs, mix, unit, att, x_in, base, act, sums_a,
-    w_qkv, gain_attn, shift_attn, w_down,
+    w_qkv_hbm, gain_attn, shift_attn, w_down_hbm,
     d_in, enc, out_a, out_b,
-    packed_v, mask_v, gb_qkv, total_a, total_b, load_sem, store_sems,
+    packed_v, mask_v, gb_qkv, total_a, total_b, w_qkv, w_down, load_sem, store_sems, weight_sems,
     sent_a, got_a, summed_a, send_a, recv_a, sent_b, got_b, summed_b, send_b, recv_b,
 ):
     first = Reducer(orders_a, total_a.shape[0], total_a, sent_a, got_a, summed_a, send_a, recv_a)
     second = Reducer(orders_b, total_b.shape[0], total_b, sent_b, got_b, summed_b, send_b, recv_b)
     load = pltpu.make_async_copy(sums_a, total_a, load_sem)
     load.start()
+    weight_loads = start_all(((w_qkv_hbm, w_qkv), (w_down_hbm, w_down)), weight_sems)
     steps = fields // UNROLL
     rows = UNROLL * slots
 
@@ -622,6 +651,8 @@
         in_specs=[block(slots, 3 * width)] + [block(slots, width)] * 3,
     )(qkv, probs, mix, unit)
 
+    for copy in weight_loads:
+        copy.wait()
     at = 3 * width * width // LANES
     add_vector(total_b, at, gb_qkv[...])
     grad_sum = jnp.sum(gb_qkv[...], axis=0, keepdims=True)
@@ -706,10 +737,11 @@
 
 def unpack_kernel(
     fields, slots, width, hidden,
-    counts, starts, visible, d_in, enc, base, act, w_down_in, sums_a, sums_b,
+    counts, starts, visible, d_in, enc, base, act, w_down_hbm, sums_a_hbm, sums_b_hbm,
     encoded, input_grad, w_qkv, b_query, b_value, w_out, b_out, w_up, b_up, w_down, b_down,
     gain_attn, shift_attn, gain_mlp, shift_mlp,
-    picks_v, d_in_v, enc_v, out_v, grad_v, act_v, qkv_v, up_v, down_v, sems, weight_sems,
+    picks_v, d_in_v, enc_v, out_v, grad_v, act_v, qkv_v, up_v, down_v,
+    sums_a, sums_b, w_down_in, sems, weight_sems,
 ):
     up_at, down_at, out_at, at = sum_rows(width, hidden)
     steps = fields // GROUP
@@ -802,8 +834,18 @@
             copy.start()
         return carry
 
+    ahead = [
+        pltpu.make_async_copy(src, dst, weight_sems.at[3 + k])
+        for k, (src, dst) in enumerate(
+            ((sums_a_hbm, sums_a), (sums_b_hbm, sums_b), (w_down_hbm, w_down_in))
+        )
+    ]
+    for copy in ahead:
+        copy.start()
     lax.fori_loop(0, steps, start_loads, 0)
     picks_v[...] = visible[...].T
+    for copy in ahead:
+        copy.wait()
     copies = []
     unblock(sums_a, up_at, up_v)
     copies.append(pltpu.make_async_copy(up_v, w_up, weight_sems.at[0]))
@@ -858,7 +900,7 @@
             shape((cap, hidden), bf16),
             shape((rows_a, LANES), f32),
         ],
-        in_specs=[smem, hbm, vmem, hbm] + [vmem] * 13,
+        in_specs=[smem, hbm, vmem, hbm, hbm, vmem, vmem, hbm, vmem, hbm, vmem, hbm] + [vmem] * 5,
         out_specs=[smem] + [hbm] * 8 + [vmem],
         scratch_shapes=[
             pltpu.VMEM((tall, width), bf16),
@@ -880,6 +922,11 @@
             pltpu.SemaphoreType.DMA((2, fields // BATCH)),
             pltpu.SemaphoreType.DMA((2,)),
             pltpu.SemaphoreType.DMA((cap // ROWS,)),
+            pltpu.VMEM(w_qkv.shape, bf16),
+            pltpu.VMEM(w_out.shape, bf16),
+            pltpu.VMEM(w_up.shape, bf16),
+            pltpu.VMEM(w_down.shape, bf16),
+            pltpu.SemaphoreType.DMA((4,)),
         ],
         compiler_params=pltpu.CompilerParams(vmem_limit_bytes=VMEM_BYTES),
         name="forward_rows",
@@ -908,7 +955,7 @@
             shape(sums_a.shape, bf16),
             shape((rows_b, LANES), bf16),
         ],
-        in_specs=[smem, smem] + [hbm] * 9 + [vmem] * 4,
+        in_specs=[smem, smem] + [hbm] * 10 + [vmem] * 2 + [hbm],
         out_specs=[hbm] * 4,
         scratch_shapes=[
             pltpu.VMEM((fields * slots, 3 * width), bf16),
@@ -916,7 +963,10 @@
             pltpu.VMEM((8, 3 * width), f32),
             pltpu.VMEM(sums_a.shape, f32),
             pltpu.VMEM((rows_b, LANES), f32),
+            pltpu.VMEM(w_qkv.shape, bf16),
+            pltpu.VMEM(w_down.shape, bf16),
             pltpu.SemaphoreType.DMA,
+            pltpu.SemaphoreType.DMA((2,)),
             pltpu.SemaphoreType.DMA((2,)),
         ]
         + reducer_scratch(sums_a.shape[0], orders_a)
@@ -951,7 +1001,7 @@
             shape((hidden, width), f32), vector,
             vector, vector, vector, vector,
         ],
-        in_specs=[smem, smem, vmem] + [hbm] * 4 + [vmem] * 3,
+        in_specs=[smem, smem, vmem] + [hbm] * 7,
         out_specs=[hbm] * 3 + [vmem] * 4 + [hbm, vmem, hbm] + [vmem] * 5,
         scratch_shapes=[
             pltpu.VMEM((fields, slots), jnp.int32),
@@ -963,8 +1013,11 @@
             pltpu.VMEM((width, 3 * width), f32),
             pltpu.VMEM((width, hidden), f32),
             pltpu.VMEM((hidden, width), f32),
+            pltpu.VMEM(sums_a.shape, bf16),
+            pltpu.VMEM(sums_b.shape, bf16),
+            pltpu.VMEM(w_down.shape, bf16),
             pltpu.SemaphoreType.DMA((3, fields // GROUP)),
-            pltpu.SemaphoreType.DMA((3,)),
+            pltpu.SemaphoreType.DMA((6,)),
         ],
         compiler_params=pltpu.CompilerParams(vmem_limit_bytes=VMEM_BYTES),
         name="unpack_rows",

time: 199 us -> 194 us (0.975)
  Pallas kernels: 198 us -> 191 us
    pallas_call x1, Pallas kernels: 96.3 us -> 93.7 us  [forward(): pl.pallas_call(functools.partial(forward_kernel, fields, slots, width, hi...]
    pallas_call x1, Pallas kernels: 19.1 us -> 17.1 us  [unpack_all(): pl.pallas_call(functools.partial(unpack_kernel, fields, slots, width, hid...]
where the time goes in v6:
time: 194 us; the launch traced here: 192 us
  Pallas kernels  191 us (98%)
    pallas_call x1, Pallas kernels, forward(): pl.pallas_call(functools.partial(forward_kernel, fields, slots, width, hi...  93.7 us
    pallas_call x1, Pallas kernels, backward(): pl.pallas_call(functools.partial(backward_kernel, orders_a, orders_b, fie...  80.6 us
    pallas_call x1, Pallas kernels, unpack_all(): pl.pallas_call(functools.partial(unpack_kernel, fields, slots, width, hid...  17.1 us

profile of v6, /device:TPU:0, one launch (start us, length us, event | category | flops | bytes accessed | tf_op | source)
XLA Modules:
  0.0 192.3 jit_solution(2973082896761055980)
XLA Ops:
  0.6 93.7 %forward_rows.1 = (s32[128]{0:T(128)}, bf16[128,64,384]{2,1,0:T(8,128)(2,1)}, bf16[128,64,384]{2,1,0:T(8,128)(2,1)}, bf16[128,64,1152]{2,1,0:T(8,128)(2,1)}, bf1...) custom-call(s32[128]{0:T(128)} %counts.5, ...), custom_call_target="tpu_custom_call" | custom-call | tf_op jit(solution)/shard_map/forward_rows/pallas_call | solution.py:889
  94.4 80.6 %backward_rows.1 = (bf16[8192,384]{1,0:T(8,128)(2,1)}, bf16[4096,384]{1,0:T(8,128)(2,1)}, bf16[10752,128]{1,0:T(8,128)(2,1)}, bf16[3584,128]{1,0:T(8,128)(2,1)}) custom-call(s32[128]{0:T(128)} %counts.5, s32[128]{0:T(128)} %get-tuple-element.29.starts, bf16[128,64,1152]{2,1,0:T(8,128)(2,1)} %get-tuple-element.30.qkv, ...), custom_call_target="tpu_custom_call" | custom-call | tf_op jit(solution)/shard_map/backward_rows/pallas_call | solution.py:950
  175.0 17.1 %unpack_rows.1 = (bf16[128,64,384]{2,1,0:T(8,128)(2,1)}, bf16[128,128,384]{2,1,0:T(8,128)(2,1)}, f32[384,1152]{1,0:T(8,128)}, f32[384]{0:T(512)}, f32[384]{0:T(5...) custom-call(s32[128]{0:T(128)} %counts.5, ...), custom_call_target="tpu_custom_call" | custom-call | tf_op jit(solution)/shard_map/unpack_rows/pallas_call | solution.py:993

commit v7 on v6

--- a/solution.py
+++ b/solution.py
@@ -320,10 +320,10 @@
     counts, patches, visible, upstream,
     w_qkv_hbm, b_query, b_value, w_out_hbm, b_out, w_up_hbm, b_up, w_down_hbm, b_down,
     gain_attn, shift_attn, gain_mlp, shift_mlp,
-    starts, x_out, unit_out, qkv_out, probs_out, att_out, mix_out, base_out, act_out, sums,
+    starts, x_out, unit_out, qkv_out, probs_out, att_out, mix_out, base_out, act_out, sums_out,
     x_v, g_v, qkv_v, mix_v, probs_v, act_v, dup_v, mask_v, picks_v,
     gb_up, gb_down, gb_out, gg_mlp, gs_mlp, window_sems, probs_sems, land_sems,
-    act_sems, base_sems, w_qkv, w_out, w_up, w_down, weight_sems,
+    act_sems, base_sems, w_qkv, w_out, w_up, w_down, weight_sems, sums, sums_sem,
 ):
     up_at, down_at, out_at, vector_at = sum_rows(width, hidden)
     patch_rows = patches.shape[0] // fields
@@ -561,9 +561,12 @@
     at = vector_at
     for partial in (gb_up, gb_down, gb_out, gg_mlp, gs_mlp):
         at = add_vector(sums, at, partial[...])
+    sums_copy = pltpu.make_async_copy(sums, sums_out, sums_sem)
+    sums_copy.start()
 
     lax.fori_loop(jnp.maximum(blocks - 2, 0), blocks, lambda i, c: act_copy(i).wait(), None)
     lax.fori_loop(0, blocks, lambda i, c: base_copy(i).wait(), None)
+    sums_copy.wait()
     for kind, ref in enumerate((qkv_out, att_out, mix_out)):
         pltpu.make_async_copy(ref, ref, window_sems.at[kind]).wait()
 
@@ -729,10 +732,10 @@
         dst[k * LANES : (k + 1) * LANES, :] = part.T
 
 
-def unblock_vector(src, at, dst):
+def unblock_vector(rows, at, dst):
     (columns,) = dst.shape
     for k in range(columns // LANES):
-        dst[k * LANES : (k + 1) * LANES] = src[pl.ds(at + k, 1), :].astype(f32).reshape(LANES)
+        dst[k * LANES : (k + 1) * LANES] = rows[at + k : at + k + 1, :].reshape(LANES)
 
 
 def unpack_kernel(
@@ -857,12 +860,15 @@
     copies.append(pltpu.make_async_copy(qkv_v, w_qkv, weight_sems.at[2]))
     copies[2].start()
     unblock(sums_a, out_at, w_out)
+    vectors = sums_a[pl.ds(at, 2 * TILE), :].astype(f32)
+    at = 0
     for ref in (b_up, b_down, b_out, gain_mlp, shift_mlp):
-        unblock_vector(sums_a, at, ref)
+        unblock_vector(vectors, at, ref)
         at += ref.shape[0] // LANES
-    at = 3 * width * width // LANES
+    vectors = sums_b[pl.ds(3 * width * width // LANES, TILE), :].astype(f32)
+    at = 0
     for ref, rows in ((b_query, 2), (b_value, 1), (gain_attn, 1), (shift_attn, 1)):
-        unblock_vector(sums_b, at, ref)
+        unblock_vector(vectors, at, ref)
         at += rows * width // LANES
     lax.fori_loop(0, steps, unpack, 0)
     lax.fori_loop(0, steps, wait_stores, 0)
@@ -901,7 +907,7 @@
             shape((rows_a, LANES), f32),
         ],
         in_specs=[smem, hbm, vmem, hbm, hbm, vmem, vmem, hbm, vmem, hbm, vmem, hbm] + [vmem] * 5,
-        out_specs=[smem] + [hbm] * 8 + [vmem],
+        out_specs=[smem] + [hbm] * 9,
         scratch_shapes=[
             pltpu.VMEM((tall, width), bf16),
             pltpu.VMEM((tall, width), bf16),
@@ -927,6 +933,8 @@
             pltpu.VMEM(w_up.shape, bf16),
             pltpu.VMEM(w_down.shape, bf16),
             pltpu.SemaphoreType.DMA((4,)),
+            pltpu.VMEM((rows_a, LANES), f32),
+            pltpu.SemaphoreType.DMA,
         ],
         compiler_params=pltpu.CompilerParams(vmem_limit_bytes=VMEM_BYTES),
         name="forward_rows",

time: 194 us -> 195 us (level)
  no operation moved by 1% of the time
where the time goes in v7:
time: 195 us; the launch traced here: 193 us
  Pallas kernels  192 us (98%)
    pallas_call x1, Pallas kernels, forward(): pl.pallas_call(functools.partial(forward_kernel, fields, slots, width, hi...  93.6 us
    pallas_call x1, Pallas kernels, backward(): pl.pallas_call(functools.partial(backward_kernel, orders_a, orders_b, fie...  81.3 us
    pallas_call x1, Pallas kernels, unpack_all(): pl.pallas_call(functools.partial(unpack_kernel, fields, slots, width, hid...  17.1 us

profile of v7, /device:TPU:0, one launch (start us, length us, event | category | flops | bytes accessed | tf_op | source)
XLA Modules:
  0.0 192.9 jit_solution(3313412150043339446)
XLA Ops:
  0.6 93.6 %forward_rows.1 = (s32[128]{0:T(128)}, bf16[128,64,384]{2,1,0:T(8,128)(2,1)}, bf16[128,64,384]{2,1,0:T(8,128)(2,1)}, bf16[128,64,1152]{2,1,0:T(8,128)(2,1)}, bf1...) custom-call(s32[128]{0:T(128)} %counts.5, ...), custom_call_target="tpu_custom_call" | custom-call | tf_op jit(solution)/shard_map/forward_rows/pallas_call | solution.py:895
  94.3 81.3 %backward_rows.1 = (bf16[8192,384]{1,0:T(8,128)(2,1)}, bf16[4096,384]{1,0:T(8,128)(2,1)}, bf16[10752,128]{1,0:T(8,128)(2,1)}, bf16[3584,128]{1,0:T(8,128)(2,1)}) custom-call(s32[128]{0:T(128)} %counts.5, s32[128]{0:T(128)} %get-tuple-element.29.starts, bf16[128,64,1152]{2,1,0:T(8,128)(2,1)} %get-tuple-element.30.qkv, ...), custom_call_target="tpu_custom_call" | custom-call | tf_op jit(solution)/shard_map/backward_rows/pallas_call | solution.py:958
  175.6 17.1 %unpack_rows.1 = (bf16[128,64,384]{2,1,0:T(8,128)(2,1)}, bf16[128,128,384]{2,1,0:T(8,128)(2,1)}, f32[384,1152]{1,0:T(8,128)}, f32[384]{0:T(512)}, f32[384]{0:T(5...) custom-call(s32[128]{0:T(128)} %counts.5, ...), custom_call_target="tpu_custom_call" | custom-call | tf_op jit(solution)/shard_map/unpack_rows/pallas_call | solution.py:1001
